TPU v7x, 32 devices: a whole 2x2x4 slice. The times are simulated.
32 devices in a mesh: gx: 8 (over z, x), gy: 4 (over y, core).
Axes of the slice: x: 2, y: 2, z: 4, core: 2. Of those that a mesh axis runs over, the one named last changes fastest.
Arguments:
- adjoint_forcing: float32 [4, 6, 256, 1024], P(None, None, 'gx', 'gy'), may hold values from -6 to 6
- field_mixing: float32 [4, 4], replicated, may hold values from -3 to 3
- time_mixing: float32 [6, 6], replicated, may hold values from -2.5 to 2.5
- kernel_east: float32 [21], replicated, may hold values from 0.1 to 1
- kernel_north: float32 [21], replicated, may hold values from 0.1 to 1
- spatial_modes: bfloat16 [256, 1024, 256], P('gx', 'gy'), may hold values from -0.015625 to 0.015625
- coefficients: float32 [256, 24], P('gy'), may hold values from -6 to 6
Outputs:
- gradient: float32 [256, 24], P('gy')
All inputs are finite; a program needn't handle non-finite values.
Results may differ from a plain program's by a relative error of at most 0.0029.
Values sent between devices are 32-bit elements; how exact they have to be, the bound alone decides.
No kernel may reach another device: no remote copies, remote signals or barrier semaphores. Data moves between devices by JAX's collectives and lax.ppermute only.
A program may use at most 64 MiB of HBM per device.

v0:
```python
import jax
import jax.numpy as jnp
from jax import lax
from jax.sharding import PartitionSpec as P


def padded(block, sides, width):
    for axis, dim in sides:
        count = lax.axis_size(axis)
        forward = [(i, i + 1) for i in range(count - 1)]
        backward = [(target, source) for source, target in forward]
        low = lax.ppermute(
            lax.slice_in_dim(block, block.shape[dim] - width, None, axis=dim), axis, forward
        )
        high = lax.ppermute(lax.slice_in_dim(block, 0, width, axis=dim), axis, backward)
        block = jnp.concatenate([low, block, high], axis=dim)
    return block


def smooth_valid(extended, taps, axis, count):
    total = taps[0] * lax.slice_in_dim(extended, 0, count, axis=axis)
    for j in range(1, taps.shape[0]):
        total = total + taps[j] * lax.slice_in_dim(extended, j, j + count, axis=axis)
    return total


def local(
    adjoint_forcing,
    field_mixing,
    time_mixing,
    kernel_east,
    kernel_north,
    spatial_modes,
    coefficients,
):
    fields, levels, width_x, width_y = adjoint_forcing.shape
    reach = (kernel_east.shape[0] - 1) // 2
    mixed = jnp.einsum(
        "gf,st,gsxy->ftxy",
        field_mixing,
        time_mixing,
        adjoint_forcing,
        precision=lax.Precision.HIGHEST,
    )
    wide_x = padded(mixed, (("gx", 2),), reach)
    along_x = smooth_valid(wide_x, kernel_east, 2, width_x)
    wide_y = padded(along_x, (("gy", 3),), reach)
    smoothed = smooth_valid(wide_y, kernel_north, 3, width_y)
    smoothed = smoothed.astype(jnp.bfloat16)
    flat_state = smoothed.reshape(fields * levels, width_x * width_y)
    flat_modes = spatial_modes.reshape(width_x * width_y, spatial_modes.shape[2])
    projection = lax.dot_general(
        flat_modes, flat_state, (((0,), (1,)), ((), ())), preferred_element_type=jnp.float32
    )
    owned = coefficients.shape[0]
    total = lax.psum(projection, ("gx", "gy"))
    mine = lax.dynamic_slice_in_dim(total, lax.axis_index("gy") * owned, owned, 0)
    return coefficients + mine


def solution(mesh):
    in_specs = (P(None, None, "gx", "gy"), P(), P(), P(), P(), P("gx", "gy", None), P("gy", None))
    out_specs = P("gy", None)
    return jax.shard_map(local, mesh=mesh, in_specs=in_specs, out_specs=out_specs, check_vma=False)
```

profile of v0, /device:TPU:1, one launch (start us, length us, event | category | flops | bytes accessed | tf_op | source)
XLA Modules:
  0.0 117.0 jit_solution(11781619505577167260)
XLA Ops:
  0.0 0.0 copy-start
  0.0 3.1 %fusion.118 = f32[6,32,256,4]{2,3,1,0:T(4,128)S(1)} fusion(f32[4,6,32,256]{3,2,1,0:T(8,128)} %param.7, f32[4,4]{1,0:T(4,128)} %param.8), kind=kOutput, calls=%fused_computation.196 | convolution fusion | flops 9437184 | bytes 1572928 | tf_op jit(solution)/shard_map/gf,st,gsxy->ftxy/dot_general | solution.py:38
  3.1 0.0 copy-done
  3.1 0.0 copy-start.2
  3.1 0.0 copy-start.3
  3.1 1.5 %convolution_bitcast_fusion = f32[4,6,32,256]{3,1,0,2:T(8,128)S(1)} fusion(f32[6,32,256,4]{2,3,1,0:T(4,128)S(1)} %fusion.118, f32[6,6]{1,0:T(8,128)S(1)} %copy-done), kind=kOutput, calls=%fused_computation.72 | convolution fusion | flops 14155776 | bytes 1573008 | tf_op jit(solution)/shard_map/gf,st,gsxy->ftxy/dot_general | solution.py:38
  4.6 0.1 fusion.123
  4.6 4.0 %collective-permute-start = (f32[4,6,10,256]{3,1,0,2:T(8,128)S(1)}, f32[4,6,10,256]{3,1,0,2:T(8,128)S(1)}, u32[]{:S(2)}, u32[]{:S(2)}) collective-permute-start(f32[4,6,10,256]{3,1,0,2:T(8,128)S(1)} %get-tuple-element.7), channel_id=1, source_target_pairs={{0,4},{4,8},{8,12},{12,16},{16,20},{20,24},{24,28},{1,5},{5,9},{9,... | collective-permute-start | bytes 737288 | tf_op jit(solution)/shard_map/ppermute | solution.py:12
  8.6 1.3 %collective-permute-start.1 = (f32[4,6,10,256]{3,1,0,2:T(8,128)S(1)}, f32[4,6,10,256]{3,1,0,2:T(8,128)S(1)}, u32[]{:S(2)}, u32[]{:S(2)}) collective-permute-start(f32[4,6,10,256]{3,1,0,2:T(8,128)S(1)} %get-tuple-element.8), channel_id=1, source_target_pairs={{4,0},{8,4},{12,8},{16,12},{20,16},{24,20},{28,24},{5,1},{9,5},{13... | collective-permute-start | bytes 737288 | tf_op jit(solution)/shard_map/ppermute | solution.py:15
  9.9 0.0 copy-done.2
  9.9 0.7 fusion.127
  10.6 0.7 fusion.126
  11.3 0.0 copy-done.3
  11.3 0.7 fusion.124
  12.0 9.9 %collective-permute-done = f32[4,6,10,256]{3,1,0,2:T(8,128)S(1)} collective-permute-done((f32[4,6,10,256]{3,1,0,2:T(8,128)S(1)}, f32[4,6,10,256]{3,1,0,2:T(8,128)S(1)}, u32[]{:S(2)}, u32[]{:S(2)}) %collective-permute-start) | collective-permute-done | bytes 245792 | tf_op jit(solution)/shard_map/ppermute | solution.py:12
  22.0 0.0 collective-permute-done.1
  22.0 15.8 %fusion.3 = f32[4,6,32,256]{3,1,0,2:T(8,128)S(1)} fusion(f32[4,6,32,256]{3,1,0,2:T(8,128)S(1)} %convolution_bitcast_fusion, f32[4,6,10,256]{3,1,0,2:T(8,128)S(1)} %collective-permute-done.1, f32[4,6,10,256]{3,1,0,2:T(8,128)S(1)} %collective-permute-done, f32[]{:T(128)} %bitcast.25, f32[]{:T(128)} %bitcast.24, f32[]{:T(128)} %bitcast.23, f32[]{:T(128)} %bitcast.22, ...), kind=kLoop, calls=%fused_computation.77 | loop fusion | flops 11993088 | bytes 2064468 | tf_op jit(solution)/shard_map/add | solution.py:23
  37.8 0.2 fusion.122
  38.0 4.6 %collective-permute-start.2 = (f32[4,6,32,10]{3,1,0,2:T(8,128)S(1)}, f32[4,6,32,10]{3,1,0,2:T(8,128)S(1)}, u32[]{:S(2)}, u32[]{:S(2)}) collective-permute-start(f32[4,6,32,10]{3,1,0,2:T(8,128)S(1)} %get-tuple-element.5), channel_id=1, source_target_pairs={{0,1},{1,2},{2,3},{4,5},{5,6},{6,7},{8,9},{9,10},{10,11},{12,13},{... | collective-permute-start | bytes 92168 | tf_op jit(solution)/shard_map/ppermute | solution.py:12
  42.6 1.9 %collective-permute-start.3 = (f32[4,6,32,10]{3,1,0,2:T(8,128)S(1)}, f32[4,6,32,10]{3,1,0,2:T(8,128)S(1)}, u32[]{:S(2)}, u32[]{:S(2)}) collective-permute-start(f32[4,6,32,10]{3,1,0,2:T(8,128)S(1)} %get-tuple-element.6), channel_id=1, source_target_pairs={{1,0},{2,1},{3,2},{5,4},{6,5},{7,6},{9,8},{10,9},{11,10},{13,12},{... | collective-permute-start | bytes 92168 | tf_op jit(solution)/shard_map/ppermute | solution.py:15
  44.5 0.7 fusion.125
  45.2 3.5 %collective-permute-done.2 = f32[4,6,32,10]{3,1,0,2:T(8,128)S(1)} collective-permute-done((f32[4,6,32,10]{3,1,0,2:T(8,128)S(1)}, f32[4,6,32,10]{3,1,0,2:T(8,128)S(1)}, u32[]{:S(2)}, u32[]{:S(2)}) %collective-permute-start.2) | collective-permute-done | bytes 30752 | tf_op jit(solution)/shard_map/ppermute | solution.py:12
  48.7 4.4 %collective-permute-done.3 = f32[4,6,32,10]{3,1,0,2:T(8,128)S(1)} collective-permute-done((f32[4,6,32,10]{3,1,0,2:T(8,128)S(1)}, f32[4,6,32,10]{3,1,0,2:T(8,128)S(1)}, u32[]{:S(2)}, u32[]{:S(2)}) %collective-permute-start.3) | collective-permute-done | bytes 30752 | tf_op jit(solution)/shard_map/ppermute | solution.py:15
  53.1 0.0 copy-start.1
  53.1 22.8 %fusion.60 = bf16[4,6,32,256]{3,1,0,2:T(8,128)(2,1)S(1)} fusion(f32[4,6,32,256]{3,1,0,2:T(8,128)S(1)} %fusion.3, f32[4,6,32,10]{3,1,0,2:T(8,128)S(1)} %collective-permute-done.3, f32[4,6,32,10]{3,1,0,2:T(8,128)S(1)} %collective-permute-done.2, f32[]{:T(128)} %bitcast.45, f32[]{:T(128)} %bitcast.44, f32[]{:T(128)} %bitcast.43, f32[]{:T(128)} %bitcast.42, ...), kind=kLoop, calls=%fused_computation.134 | loop fusion | flops 12189696 | bytes 1241172 | tf_op jit(solution)/shard_map/convert_element_type | solution.py:49
  75.9 0.2 copy.10
  76.1 0.2 copy.16
  76.4 0.0 copy-done.1
  76.4 0.0 copy-start.4
  76.4 0.7 convolution_bitcast_fusion.1
  77.0 39.2 %psum.7 = f32[256,24]{0,1:T(8,128)S(1)} all-reduce(f32[256,24]{0,1:T(8,128)S(1)} %convolution_bitcast_fusion.1), channel_id=1, replica_groups=mesh['gx'=8,'gy'=4] {'gx','gy'}, use_global_device_ids=true, to_apply=%region_0.0 | all-reduce | flops 6144 | bytes 49152 | tf_op jit(solution)/shard_map/psum | solution.py:56
  116.3 0.0 copy-done.4
  116.3 0.7 dynamic-slice_add_fusion
Async XLA Ops:
  0.0 3.1 %copy-start = (f32[6,6]{1,0:T(8,128)S(1)}, f32[6,6]{1,0:T(8,128)}, u32[]{:S(2)}) copy-start(f32[6,6]{1,0:T(8,128)} %param.9) | copy-start | bytes 436
  3.1 6.8 %copy-start.2 = (f32[21]{0:T(128)S(1)}, f32[21]{0:T(128)}, u32[]{:S(2)}) copy-start(f32[21]{0:T(128)} %param.10) | copy-start | bytes 256
  3.1 8.2 %copy-start.3 = (f32[21]{0:T(128)S(1)}, f32[21]{0:T(128)}, u32[]{:S(2)}) copy-start(f32[21]{0:T(128)} %param.11) | copy-start | bytes 256
  4.6 17.3 %collective-permute-start = (f32[4,6,10,256]{3,1,0,2:T(8,128)S(1)}, f32[4,6,10,256]{3,1,0,2:T(8,128)S(1)}, u32[]{:S(2)}, u32[]{:S(2)}) collective-permute-start(f32[4,6,10,256]{3,1,0,2:T(8,128)S(1)} %get-tuple-element.7), channel_id=1, source_target_pairs={{0,4},{4,8},{8,12},{12,16},{16,20},{20,24},{24,28},{1,5},{5,9},{9,... | collective-permute-start | bytes 737288 | tf_op jit(solution)/shard_map/ppermute | solution.py:12
  8.6 13.4 %collective-permute-start.1 = (f32[4,6,10,256]{3,1,0,2:T(8,128)S(1)}, f32[4,6,10,256]{3,1,0,2:T(8,128)S(1)}, u32[]{:S(2)}, u32[]{:S(2)}) collective-permute-start(f32[4,6,10,256]{3,1,0,2:T(8,128)S(1)} %get-tuple-element.8), channel_id=1, source_target_pairs={{4,0},{8,4},{12,8},{16,12},{20,16},{24,20},{28,24},{5,1},{9,5},{13... | collective-permute-start | bytes 737288 | tf_op jit(solution)/shard_map/ppermute | solution.py:15
  38.0 10.7 %collective-permute-start.2 = (f32[4,6,32,10]{3,1,0,2:T(8,128)S(1)}, f32[4,6,32,10]{3,1,0,2:T(8,128)S(1)}, u32[]{:S(2)}, u32[]{:S(2)}) collective-permute-start(f32[4,6,32,10]{3,1,0,2:T(8,128)S(1)} %get-tuple-element.5), channel_id=1, source_target_pairs={{0,1},{1,2},{2,3},{4,5},{5,6},{6,7},{8,9},{9,10},{10,11},{12,13},{... | collective-permute-start | bytes 92168 | tf_op jit(solution)/shard_map/ppermute | solution.py:12
  42.6 10.5 %collective-permute-start.3 = (f32[4,6,32,10]{3,1,0,2:T(8,128)S(1)}, f32[4,6,32,10]{3,1,0,2:T(8,128)S(1)}, u32[]{:S(2)}, u32[]{:S(2)}) collective-permute-start(f32[4,6,32,10]{3,1,0,2:T(8,128)S(1)} %get-tuple-element.6), channel_id=1, source_target_pairs={{1,0},{2,1},{3,2},{5,4},{6,5},{7,6},{9,8},{10,9},{11,10},{13,12},{... | collective-permute-start | bytes 92168 | tf_op jit(solution)/shard_map/ppermute | solution.py:15
  53.1 23.3 %copy-start.1 = (bf16[32,256,256]{2,1,0:T(8,128)(2,1)S(1)}, bf16[32,256,256]{2,1,0:T(8,128)(2,1)}, u32[]{:S(2)}) copy-start(bf16[32,256,256]{2,1,0:T(8,128)(2,1)} %param.12) | copy-start | bytes 12582916
  76.4 39.9 %copy-start.4 = (f32[64,24]{0,1:T(8,128)S(1)}, f32[64,24]{0,1:T(8,128)}, u32[]{:S(2)}) copy-start(f32[64,24]{0,1:T(8,128)} %param.13) | copy-start | bytes 18436
where the time goes:
time: 119 us; the launch traced here: 117 us
  other arithmetic  39.3 us (33%)
  blocking collectives  39.2 us (33%)
  waiting for transfers between devices  17.8 us (15%)
  starting transfers between devices  11.8 us (10%)
  matrix products  5.17 us (4%)
  local copies, waits for them, and re-layouts  3.52 us (3%)
    psum x1, blocking collectives, local(): total = lax.psum(projection, ('gx', 'gy'))  39.2 us
    convert_element_type x1, other arithmetic, local(): smoothed = smoothed.astype(jnp.bfloat16)  22.8 us
    add x1, other arithmetic, smooth_valid(): total + taps[j] * lax.slice_in_dim(extended, j, j + count, axis=axis)  15.8 us
    ppermute x2, waiting for transfers between devices, padded(): lax.ppermute(lax.slice_in_dim(block, block.shape[dim] - width, None, axis...  13.4 us
    ppermute x2, starting transfers between devices, padded(): lax.ppermute(lax.slice_in_dim(block, block.shape[dim] - width, None, axis...  8.54 us
    dot_general x2, matrix products, local(): jnp.einsum('gf,st,gsxy->ftxy', field_mixing, time_mixing, adjoint_forcing...  4.51 us
    ppermute x2, waiting for transfers between devices, padded(): lax.ppermute(lax.slice_in_dim(block, 0, width, axis=dim), axis, backward)  4.4 us
    ppermute x2, starting transfers between devices, padded(): lax.ppermute(lax.slice_in_dim(block, 0, width, axis=dim), axis, backward)  3.21 us
  transfers between devices with their start and end apart: 4, of which 3 were waited for; matrix products, arithmetic and copies ran while one was open for 2% of the time, Pallas kernels for 0%

commit v1 on v0

v1 whole, which is shorter than its diff:
```python
import functools

import jax
import jax.numpy as jnp
from jax import lax
from jax.experimental import pallas as pl
from jax.experimental.pallas import tpu as pltpu
from jax.sharding import PartitionSpec as P

F32, BF16 = jnp.float32, jnp.bfloat16
NT = (((1,), (1,)), ((), ()))
TN = (((0,), (0,)), ((), ()))
NN = (((1,), (0,)), ((), ()))
STRIP = 16


def dot(a, b, dims=NN):
    return lax.dot_general(a, b, dims, preferred_element_type=F32)


def halves(v):
    high = v.astype(BF16)
    return high, (v - high.astype(F32)).astype(BF16)


def dot2(a, b, dims=NN):
    (ah, al), (bh, bl) = a, b
    return dot(ah, bh, dims) + dot(ah, bl, dims) + dot(al, bh, dims)


def iota(shape, dim):
    return lax.broadcasted_iota(jnp.int32, shape, dim)


def turn_kernel(reach, a_ref, t_ref, s1_ref, s2_ref):
    t_ref[...] = jnp.swapaxes(a_ref[...], 0, 1)
    odd = lax.axis_index("gx") % 2
    last = t_ref.shape[0] - 1
    for n in range(reach):
        s1_ref[n] = t_ref[odd * n + (1 - odd) * (last - n)]
        s2_ref[n] = t_ref[(1 - odd) * n + odd * (last - n)]


def strip_kernel(reach, t_ref, core_ref, chip_ref):
    width_x, channels, width_y = t_ref.shape
    odd = lax.axis_index("gy") % 2
    row, col = iota((2 * STRIP, width_y), 0), iota((2 * STRIP, width_y), 1)
    to_core = row < STRIP
    at = jnp.where(to_core, row, row - STRIP)
    low = jnp.where(to_core, odd, 1 - odd) == 1
    wanted = at + jnp.where(low, 0, width_y - reach)
    pick = jnp.where((col == wanted) & (at < reach), 1.0, 0.0).astype(BF16)
    data = t_ref[...].reshape(width_x * channels, width_y)
    high, rest = halves(data)
    low_part = (data - high.astype(F32) - rest.astype(F32)).astype(BF16)
    strips = dot(pick, high, NT) + dot(pick, rest, NT) + dot(pick, low_part, NT)
    core_ref[...] = strips[:STRIP]
    chip_ref[...] = strips[STRIP:]


def band_kernel(reach, north_ref, field_ref, time_ref, t_ref, y_ref, bh_ref, bl_ref, eh_ref, el_ref, mix_ref):
    width_x, channels, width_y = t_ref.shape
    odd = lax.axis_index("gy") % 2
    shift = iota((width_y, width_y), 0) - iota((width_y, width_y), 1) + reach
    row = iota((2 * STRIP, width_y), 0)
    from_core = row < STRIP
    at = jnp.where(from_core, row, row - STRIP)
    left = jnp.where(from_core, odd, 1 - odd) == 1
    source = jnp.where(left, at - reach, width_y + at)
    edge_shift = jnp.where(at < reach, source - iota((2 * STRIP, width_y), 1) + reach, -1)
    band = jnp.zeros((width_y, width_y), F32)
    edge = jnp.zeros((2 * STRIP, width_y), F32)
    for j in range(2 * reach + 1):
        band = jnp.where(shift == j, north_ref[j], band)
        edge = jnp.where(edge_shift == j, north_ref[j], edge)
    band, edge = halves(band), halves(edge)
    bh_ref[...], bl_ref[...] = band
    eh_ref[...], el_ref[...] = edge
    y_ref[...] = dot2(halves(t_ref[...].reshape(width_x * channels, width_y)), band).reshape(t_ref.shape)
    fields, levels = field_ref.shape[0], time_ref.shape[0]
    out, into = iota((channels, channels), 0), iota((channels, channels), 1)
    by_field = jnp.zeros((channels, channels), F32)
    by_time = jnp.zeros((channels, channels), F32)
    for g in range(fields):
        for f in range(fields):
            here = (into // levels == g) & (out // levels == f)
            by_field = jnp.where(here, field_ref[g, f], by_field)
    for s in range(levels):
        for t in range(levels):
            by_time = jnp.where((into % levels == s) & (out % levels == t), time_ref[s, t], by_time)
    mix_ref[...] = by_field * by_time


def corner_kernel(reach, channels, core_ref, chip_ref, strips_ref, c1_ref, c2_ref):
    odd = lax.axis_index("gx") % 2
    strips = jnp.concatenate([core_ref[...], chip_ref[...]], axis=0)
    strips_ref[...] = strips
    top = strips[:, : reach * channels]
    bottom = strips[:, strips.shape[1] - reach * channels :]
    c1_ref[...] = jnp.where(odd == 1, top, bottom)
    c2_ref[...] = jnp.where(odd == 1, bottom, top)


def split_rows(v):
    high = v.astype(BF16).astype(F32)
    return jnp.concatenate([high, v - high], axis=0).astype(BF16)


def tile_kernel(reach, east_ref, y_ref, strips_ref, eh_ref, el_ref, modes_ref, p_ref, total, smooth):
    width_x, channels, width_y = y_ref.shape
    more = dot2(halves(strips_ref[...]), (eh_ref[...], el_ref[...]), TN)
    total[...] = y_ref[...] + more.reshape(y_ref.shape)
    acc = jnp.zeros((2 * channels, modes_ref.shape[2]), F32)
    for x in range(width_x):
        value = None
        for j in range(2 * reach + 1):
            if 0 <= x + j - reach < width_x:
                term = east_ref[j] * total[x + j - reach]
                value = term if value is None else value + term
        smooth[x] = split_rows(value)
    for x in range(width_x):
        acc = acc + dot(smooth[x], modes_ref[x])
    p_ref[...] = acc[:channels] + acc[channels:]


def halo_kernel(reach, owned, east_ref, p_ref, r1_ref, r2_ref, c1_ref, c2_ref, bh_ref, bl_ref, eh_ref, el_ref, modes_ref, out_ref, by_y, by_corner, smooth):
    channels, width_y = r1_ref.shape[1:]
    width_x, _, modes = modes_ref.shape
    odd = lax.axis_index("gx") % 2
    band, edge = (bh_ref[...], bl_ref[...]), (eh_ref[...], el_ref[...])
    acc = jnp.zeros((2 * channels, modes), F32)
    for r_ref, c_ref, left in ((r1_ref, c1_ref, odd), (r2_ref, c2_ref, 1 - odd)):
        rows = r_ref[...].reshape(reach * channels, width_y)
        by_y[...] = dot2(halves(rows), band).reshape(r_ref.shape)
        by_corner[...] = dot2(halves(c_ref[...]), edge, TN).reshape(r_ref.shape)
        taps = [jnp.where(left == 1, east_ref[d], east_ref[2 * reach - d]) for d in range(reach)]
        came = [by_y[n] + by_corner[left * (reach - 1 - n) + (1 - left) * n] for n in range(reach)]
        for m in range(reach):
            value = taps[m] * came[0]
            for n in range(1, m + 1):
                value = value + taps[m - n] * came[n]
            smooth[m] = split_rows(value)
        for m in range(reach):
            acc = acc + dot(smooth[m], modes_ref[left * (reach - 1 - m) + (1 - left) * (width_x - reach + m)])
    total = p_ref[...] + acc[:channels] + acc[channels:]
    folds = 128 // owned
    rows = channels // folds
    for g in range(modes // owned):
        piece = jnp.concatenate(
            [total[k * rows : (k + 1) * rows, g * owned : (g + 1) * owned] for k in range(folds)], axis=1
        )
        for k in range(out_ref.shape[0]):
            out_ref[k, g] = piece


def sum_kernel(parts_ref, mix_ref, coefficients_ref, out_ref):
    channels, owned = out_ref.shape
    folds = 128 // owned
    rows = channels // folds
    total = jnp.sum(parts_ref[...], axis=0)
    value = coefficients_ref[...]
    for k in range(folds):
        mixed = lax.dot_general(
            mix_ref[:, k * rows : (k + 1) * rows], total, NN, precision=lax.Precision.HIGHEST, preferred_element_type=F32
        )
        value = value + mixed[:, k * owned : (k + 1) * owned]
    out_ref[...] = value


def call(body, ins, outs, scratch=(), flops=0):
    args, specs = [], []
    for item in ins:
        scalar = isinstance(item, tuple)
        if scalar:
            args.append(item[0])
            specs.append(pl.BlockSpec(memory_space=pltpu.SMEM))
        else:
            args.append(pltpu.with_memory_space_constraint(item, pltpu.VMEM))
            specs.append(pl.BlockSpec(memory_space=pltpu.VMEM))
    return pl.pallas_call(
        body,
        out_shape=[pltpu.VMEM(shape, dtype) for shape, dtype in outs],
        in_specs=specs,
        out_specs=[pl.BlockSpec(memory_space=pltpu.VMEM)] * len(outs),
        scratch_shapes=list(scratch),
        compiler_params=pltpu.CompilerParams(vmem_limit_bytes=24 << 20),
        cost_estimate=pl.CostEstimate(flops=flops, bytes_accessed=1 << 20, transcendentals=0),
    )(*args)


def pairs(count, first):
    found = []
    for low in range(first, count - 1, 2):
        found += [(low, low + 1), (low + 1, low)]
    return found


def local(adjoint_forcing, field_mixing, time_mixing, kernel_east, kernel_north, spatial_modes, coefficients):
    fields, levels, width_x, width_y = adjoint_forcing.shape
    channels, modes, owned = fields * levels, spatial_modes.shape[2], coefficients.shape[0]
    reach = (kernel_east.shape[0] - 1) // 2
    count_x, count_y = lax.axis_size("gx"), lax.axis_size("gy")
    raw = adjoint_forcing.reshape(channels, width_x, width_y)
    slab = (reach, channels, width_y)
    t, s1, s2 = call(
        functools.partial(turn_kernel, reach), [raw], [((width_x, channels, width_y), F32), (slab, F32), (slab, F32)]
    )
    r1 = lax.ppermute(s1, "gx", pairs(count_x, 0))
    strip = ((STRIP, width_x * channels), F32)
    core, chip = call(functools.partial(strip_kernel, reach), [t], [strip, strip])
    core = lax.ppermute(core, "gy", pairs(count_y, 0))
    chip = lax.ppermute(chip, "gy", pairs(count_y, 1))
    r2 = lax.ppermute(s2, "gx", pairs(count_x, 1))
    y, bh, bl, eh, el, mix = call(
        functools.partial(band_kernel, reach),
        [(kernel_north, True), (field_mixing, True), (time_mixing, True), t],
        [
            (t.shape, F32),
            ((width_y, width_y), BF16),
            ((width_y, width_y), BF16),
            ((2 * STRIP, width_y), BF16),
            ((2 * STRIP, width_y), BF16),
            ((channels, channels), F32),
        ],
    )
    corner = ((2 * STRIP, reach * channels), F32)
    strips, c1, c2 = call(
        functools.partial(corner_kernel, reach, channels),
        [core, chip],
        [((2 * STRIP, width_x * channels), F32), corner, corner],
    )
    c1 = lax.ppermute(c1, "gx", pairs(count_x, 0))
    c2 = lax.ppermute(c2, "gx", pairs(count_x, 1))
    (share,) = call(
        functools.partial(tile_kernel, reach),
        [(kernel_east, True), y, strips, eh, el, spatial_modes],
        [((channels, modes), F32)],
        [pltpu.VMEM(t.shape, F32), pltpu.VMEM((width_x, 2 * channels, width_y), BF16)],
    )
    folds = 128 // owned
    (out,) = call(
        functools.partial(halo_kernel, reach, owned),
        [(kernel_east, True), share, r1, r2, c1, c2, bh, bl, eh, el, spatial_modes],
        [((count_x, count_y, channels // folds, 128), F32)],
        [pltpu.VMEM(slab, F32), pltpu.VMEM(slab, F32), pltpu.VMEM((reach, 2 * channels, width_y), BF16)],
    )
    out = out.reshape((count_x * count_y,) + out.shape[2:])
    parts = lax.all_to_all(out, ("gx", "gy"), 0, 0, tiled=True)
    (gradient,) = call(sum_kernel, [parts, mix, coefficients.T], [((channels, owned), F32)])
    return gradient.T


def solution(mesh):
    in_specs = (P(None, None, "gx", "gy"), P(), P(), P(), P(), P("gx", "gy", None), P("gy", None))
    out_specs = P("gy", None)
    return jax.shard_map(local, mesh=mesh, in_specs=in_specs, out_specs=out_specs, check_vma=False)
```

time: 119 us -> 45.3 us (0.38); the launches traced: 117 us -> 44.5 us
  other arithmetic: 39.3 us -> 0 us
  blocking collectives: 39.2 us -> 16.4 us
  waiting for transfers between devices: 17.8 us -> 2.35 us
  Pallas kernels: 0 us -> 7.16 us
  matrix products: 5.17 us -> 0 us
  local copies, waits for them, and re-layouts: 3.52 us -> 6.61 us
    psum x1 -> x0, blocking collectives: 39.2 us -> none  [local(): total = lax.psum(projection, ('gx', 'gy'))]
    convert_element_type x1 -> x0, other arithmetic: 22.8 us -> none  [local(): smoothed = smoothed.astype(jnp.bfloat16)]
    add x2 -> x0, other arithmetic: 16.5 us -> none  [the longest x1 15.8 us: smooth_valid(): total + taps[j] * lax.slice_in_dim(extended, j, j + count, axis=axis)]
    all_to_all x0 -> x1, blocking collectives: none -> 16.4 us  [local(): parts = lax.all_to_all(out, ('gx', 'gy'), 0, 0, tiled=True)]
    ppermute x4 -> x6, waiting for transfers between devices: 17.8 us -> 2.35 us  [the longest x1 2.33 us: local(): chip = lax.ppermute(chip, 'gy', pairs(count_y, 1))]
    pallas_call x0 -> x7, Pallas kernels: none -> 7.16 us  [call(): pl.pallas_call(body, out_shape=[pltpu.VMEM(shape, dtype) for shape, dtype...]
    unnamed x11 -> x17, local copies, waits for them, and re-layouts: 0.25 us -> 6.61 us
    dot_general x3 -> x0, matrix products: 5.17 us -> none  [the longest x2 4.51 us: local(): jnp.einsum('gf,st,gsxy->ftxy', field_mixing, time_mixing, adjoint_forcing...]
  transfers between devices with their start and end apart: 4 -> 6, of which waited for: 3 -> 1; matrix products, arithmetic and copies ran while one was open for 2% -> 0% of each run, Pallas kernels for 0% -> 10%
where the time goes in v1:
time: 45.3 us; the launch traced here: 44.5 us
  blocking collectives  16.4 us (36%)
  starting transfers between devices  11.8 us (26%)
  Pallas kernels  7.16 us (16%)
  local copies, waits for them, and re-layouts  6.61 us (15%)
  waiting for transfers between devices  2.35 us (5%)
    all_to_all x1, blocking collectives, local(): parts = lax.all_to_all(out, ('gx', 'gy'), 0, 0, tiled=True)  16.4 us
    pallas_call x7, Pallas kernels, call(): pl.pallas_call(body, out_shape=[pltpu.VMEM(shape, dtype) for shape, dtype...  7.16 us
    unnamed x17, local copies, waits for them, and re-layouts  6.61 us
    ppermute x1, starting transfers between devices, local(): c1 = lax.ppermute(c1, 'gx', pairs(count_x, 0))  4.33 us
    ppermute x1, starting transfers between devices, local(): chip = lax.ppermute(chip, 'gy', pairs(count_y, 1))  3.05 us
    ppermute x1, waiting for transfers between devices, local(): chip = lax.ppermute(chip, 'gy', pairs(count_y, 1))  2.33 us
    ppermute x1, starting transfers between devices, local(): r1 = lax.ppermute(s1, 'gx', pairs(count_x, 0))  2.1 us
    ppermute x1, starting transfers between devices, local(): core = lax.ppermute(core, 'gy', pairs(count_y, 0))  0.97 us
  transfers between devices with their start and end apart: 6, of which 1 were waited for; matrix products, arithmetic and copies ran while one was open for 0% of the time, Pallas kernels for 10%

profile of v1, /device:TPU:1, one launch (start us, length us, event | category | flops | bytes accessed | tf_op | source)
XLA Modules:
  0.0 44.5 jit_solution(16725965985180503695)
XLA Ops:
  0.0 0.0 copy-start.2
  0.0 1.1 %copy-done.2 = f32[4,6,32,256]{3,2,1,0:T(8,128)S(1)} copy-done((f32[4,6,32,256]{3,2,1,0:T(8,128)S(1)}, f32[4,6,32,256]{3,2,1,0:T(8,128)}, u32[]{:S(2)}) %copy-start.2) | copy-done | bytes 786456
  1.1 0.2 shard_map.73
  1.3 2.1 %collective-permute-start.2 = (f32[10,24,256]{2,1,0:T(8,128)S(1)}, f32[10,24,256]{2,1,0:T(8,128)S(1)}, u32[]{:S(2)}, u32[]{:S(2)}) collective-permute-start(f32[10,24,256]{2,1,0:T(8,128)S(1)} %get-tuple-element.26), channel_id=1, source_target_pairs={{0,4},{4,0},{8,12},{12,8},{16,20},{20,16},{24,28},{28,24},{1,5},{5... | collective-permute-start | bytes 737288 | tf_op jit(solution)/shard_map/ppermute | solution.py:208
  3.4 0.7 %collective-permute-start.3 = (f32[10,24,256]{2,1,0:T(8,128)S(1)}, f32[10,24,256]{2,1,0:T(8,128)S(1)}, u32[]{:S(2)}, u32[]{:S(2)}) collective-permute-start(f32[10,24,256]{2,1,0:T(8,128)S(1)} %get-tuple-element.27), channel_id=1, source_target_pairs={{4,8},{8,4},{12,16},{16,12},{20,24},{24,20},{5,9},{9,5},{13,17},{1... | collective-permute-start | bytes 737288 | tf_op jit(solution)/shard_map/ppermute | solution.py:213
  4.1 0.5 %shard_map.75 = (f32[16,768]{1,0:T(8,128)S(1)}, f32[16,768]{1,0:T(8,128)S(1)}) custom-call(f32[32,24,256]{2,1,0:T(8,128)S(1)} %get-tuple-element.19.t_ref), custom_call_target="tpu_custom_call" | custom-call | bytes 1048576 | tf_op jit(solution)/shard_map/pallas_call | solution.py:180
  4.6 1.0 %collective-permute-start = (f32[16,768]{1,0:T(8,128)S(1)}, f32[16,768]{1,0:T(8,128)S(1)}, u32[]{:S(2)}, u32[]{:S(2)}) collective-permute-start(f32[16,768]{1,0:T(8,128)S(1)} %get-tuple-element.21), channel_id=1, source_target_pairs={{0,1},{1,0},{2,3},{3,2},{4,5},{5,4},{6,7},{7,6},{8,9},{9,8},{10,11... | collective-permute-start | bytes 147464 | tf_op jit(solution)/shard_map/ppermute | solution.py:211
  5.6 3.0 %collective-permute-start.1 = (f32[16,768]{1,0:T(8,128)S(1)}, f32[16,768]{1,0:T(8,128)S(1)}, u32[]{:S(2)}, u32[]{:S(2)}) collective-permute-start(f32[16,768]{1,0:T(8,128)S(1)} %get-tuple-element.22), channel_id=1, source_target_pairs={{1,2},{2,1},{5,6},{6,5},{9,10},{10,9},{13,14},{14,13},{17,18},{18,... | collective-permute-start | bytes 147464 | tf_op jit(solution)/shard_map/ppermute | solution.py:212
  8.6 0.0 collective-permute-done.core_ref
  8.6 2.3 %collective-permute-done.1.chip_ref = f32[16,768]{1,0:T(8,128)S(1)} collective-permute-done((f32[16,768]{1,0:T(8,128)S(1)}, f32[16,768]{1,0:T(8,128)S(1)}, u32[]{:S(2)}, u32[]{:S(2)}) %collective-permute-start.1) | collective-permute-done | bytes 49184 | tf_op jit(solution)/shard_map/ppermute | solution.py:212
  11.0 0.1 shard_map.76
  11.1 4.3 %collective-permute-start.4 = (f32[32,240]{1,0:T(8,128)S(1)}, f32[32,240]{1,0:T(8,128)S(1)}, u32[]{:S(2)}, u32[]{:S(2)}) collective-permute-start(f32[32,240]{1,0:T(8,128)S(1)} %get-tuple-element.28), channel_id=1, source_target_pairs={{0,4},{4,0},{8,12},{12,8},{16,20},{20,16},{24,28},{28,24},{1,5},{5... | collective-permute-start | bytes 92168 | tf_op jit(solution)/shard_map/ppermute | solution.py:232
  15.4 0.7 %collective-permute-start.5 = (f32[32,240]{1,0:T(8,128)S(1)}, f32[32,240]{1,0:T(8,128)S(1)}, u32[]{:S(2)}, u32[]{:S(2)}) collective-permute-start(f32[32,240]{1,0:T(8,128)S(1)} %get-tuple-element.29), channel_id=1, source_target_pairs={{4,8},{8,4},{12,16},{16,12},{20,24},{24,20},{5,9},{9,5},{13,17},{1... | collective-permute-start | bytes 92168 | tf_op jit(solution)/shard_map/ppermute | solution.py:233
  16.1 0.0 copy-start.4
  16.1 0.7 %copy-done.4 = f32[6,6]{1,0:T(8,128)S(1)} copy-done((f32[6,6]{1,0:T(8,128)S(1)}, f32[6,6]{1,0:T(8,128)}, u32[]{:S(2)}) %copy-start.4) | copy-done | bytes 168
  16.8 0.0 copy-start.5
  16.8 0.7 %copy-done.5 = f32[4,4]{1,0:T(4,128)S(1)} copy-done((f32[4,4]{1,0:T(4,128)S(1)}, f32[4,4]{1,0:T(4,128)}, u32[]{:S(2)}) %copy-start.5) | copy-done | bytes 88
  17.5 0.0 copy-start.7
  17.5 0.7 %copy-done.7 = f32[21]{0:T(128)S(1)} copy-done((f32[21]{0:T(128)S(1)}, f32[21]{0:T(128)}, u32[]{:S(2)}) %copy-start.7) | copy-done | bytes 108
  18.1 1.4 %shard_map.74 = (f32[32,24,256]{2,1,0:T(8,128)S(1)}, bf16[256,256]{1,0:T(8,128)(2,1)S(1)}, bf16[256,256]{1,0:T(8,128)(2,1)S(1)}, bf16[32,256]{1,0:T(8,128)(2,1)S...) custom-call(f32[21]{0:T(128)S(1)} %copy-done.7, f32[4,4]{1,0:T(4,128)S(1)} %copy-done.5, f32[6,6]{1,0:T(8,128)S(1)} %copy-done.4, ...), custom_call_target="tpu_custom_call" | custom-call | bytes 1048576 | tf_op jit(solution)/shard_map/pallas_call | solution.py:180
  19.5 0.0 copy-start
  19.6 2.2 %copy-done = bf16[32,256,256]{2,1,0:T(8,128)(2,1)S(1)} copy-done((bf16[32,256,256]{2,1,0:T(8,128)(2,1)S(1)}, bf16[32,256,256]{2,1,0:T(8,128)(2,1)}, u32[]{:S(2)}) %copy-start) | copy-done | bytes 4194328
  21.7 0.0 copy-start.6
  21.7 0.7 %copy-done.6 = f32[21]{0:T(128)S(1)} copy-done((f32[21]{0:T(128)S(1)}, f32[21]{0:T(128)}, u32[]{:S(2)}) %copy-start.6) | copy-done | bytes 108
  22.4 0.0 copy-start.1
  22.4 2.6 %shard_map.77.p_ref = f32[24,256]{1,0:T(8,128)S(1)} custom-call(f32[21]{0:T(128)S(1)} %copy-done.6, f32[32,24,256]{2,1,0:T(8,128)S(1)} %get-tuple-element.20.y_ref, f32[32,768]{1,0:T(8,128)S(1)} %get-tuple-element.23.strips_ref, bf16[32,256]{1,0:T(8,128)(2,1)S(1)} %get-tuple-element.24.eh_ref, bf16[32,256]{1,0:T(8,128)(2,1)S(1)} %get-tuple-element.25.el_ref, ...), custom_call_target="tpu_custom_call" | custom-call | bytes 1048576 | tf_op jit(solution)/shard_map/pallas_call | solution.py:180
  25.0 0.0 copy-start.3
  25.0 0.0 collective-permute-done.4.c1_ref
  25.0 0.0 collective-permute-done.5.c2_ref
  25.0 0.0 collective-permute-done.2.r1_ref
  25.0 0.0 collective-permute-done.3.r2_ref
  25.1 0.0 copy-done.1
  25.1 2.0 %shard_map.78 = f32[8,4,12,128]{3,2,1,0:T(8,128)S(1)} custom-call(f32[21]{0:T(128)S(1)} %copy-done.6, f32[24,256]{1,0:T(8,128)S(1)} %shard_map.77.p_ref, f32[10,24,256]{2,1,0:T(8,128)S(1)} %collective-permute-done.2.r1_ref, f32[10,24,256]{2,1,0:T(8,128)S(1)} %collective-permute-done.3.r2_ref, f32[32,240]{1,0:T(8,128)S(1)} %collective-permute-done.4.c1_ref, ...), custom_call_target="tpu_custom_call" | custom-call | bytes 1048576 | tf_op jit(solution)/shard_map/pallas_call | solution.py:180
  27.1 16.4 %all_to_all.5.parts_ref = f32[32,12,128]{2,1,0:T(8,128)S(1)} all-to-all(f32[32,12,128]{2,1,0:T(8,128)S(1)} %bitcast.5), channel_id=1, replica_groups=mesh['gx'=8,'gy'=4] {'gx','gy'}, dimensions={0} | all-to-all | bytes 393216 | tf_op jit(solution)/shard_map/all_to_all | solution.py:248
  43.5 0.0 copy-done.3
  43.5 0.3 shard_map.79
  43.8 0.6 %copy.8 = f32[64,24]{0,1:T(8,128)} copy(f32[64,24]{0,1:T(8,128)S(1)} %bitcast.4) | data formatting | bytes 12288
Async XLA Ops:
  0.0 1.1 %copy-start.2 = (f32[4,6,32,256]{3,2,1,0:T(8,128)S(1)}, f32[4,6,32,256]{3,2,1,0:T(8,128)}, u32[]{:S(2)}) copy-start(f32[4,6,32,256]{3,2,1,0:T(8,128)} %param.7) | copy-start | bytes 2359300
  1.3 23.7 %collective-permute-start.2 = (f32[10,24,256]{2,1,0:T(8,128)S(1)}, f32[10,24,256]{2,1,0:T(8,128)S(1)}, u32[]{:S(2)}, u32[]{:S(2)}) collective-permute-start(f32[10,24,256]{2,1,0:T(8,128)S(1)} %get-tuple-element.26), channel_id=1, source_target_pairs={{0,4},{4,0},{8,12},{12,8},{16,20},{20,16},{24,28},{28,24},{1,5},{5... | collective-permute-start | bytes 737288 | tf_op jit(solution)/shard_map/ppermute | solution.py:208
  3.4 21.6 %collective-permute-start.3 = (f32[10,24,256]{2,1,0:T(8,128)S(1)}, f32[10,24,256]{2,1,0:T(8,128)S(1)}, u32[]{:S(2)}, u32[]{:S(2)}) collective-permute-start(f32[10,24,256]{2,1,0:T(8,128)S(1)} %get-tuple-element.27), channel_id=1, source_target_pairs={{4,8},{8,4},{12,16},{16,12},{20,24},{24,20},{5,9},{9,5},{13,17},{1... | collective-permute-start | bytes 737288 | tf_op jit(solution)/shard_map/ppermute | solution.py:213
  4.6 4.0 %collective-permute-start = (f32[16,768]{1,0:T(8,128)S(1)}, f32[16,768]{1,0:T(8,128)S(1)}, u32[]{:S(2)}, u32[]{:S(2)}) collective-permute-start(f32[16,768]{1,0:T(8,128)S(1)} %get-tuple-element.21), channel_id=1, source_target_pairs={{0,1},{1,0},{2,3},{3,2},{4,5},{5,4},{6,7},{7,6},{8,9},{9,8},{10,11... | collective-permute-start | bytes 147464 | tf_op jit(solution)/shard_map/ppermute | solution.py:211
  5.6 5.4 %collective-permute-start.1 = (f32[16,768]{1,0:T(8,128)S(1)}, f32[16,768]{1,0:T(8,128)S(1)}, u32[]{:S(2)}, u32[]{:S(2)}) collective-permute-start(f32[16,768]{1,0:T(8,128)S(1)} %get-tuple-element.22), channel_id=1, source_target_pairs={{1,2},{2,1},{5,6},{6,5},{9,10},{10,9},{13,14},{14,13},{17,18},{18,... | collective-permute-start | bytes 147464 | tf_op jit(solution)/shard_map/ppermute | solution.py:212
  11.1 13.9 %collective-permute-start.4 = (f32[32,240]{1,0:T(8,128)S(1)}, f32[32,240]{1,0:T(8,128)S(1)}, u32[]{:S(2)}, u32[]{:S(2)}) collective-permute-start(f32[32,240]{1,0:T(8,128)S(1)} %get-tuple-element.28), channel_id=1, source_target_pairs={{0,4},{4,0},{8,12},{12,8},{16,20},{20,16},{24,28},{28,24},{1,5},{5... | collective-permute-start | bytes 92168 | tf_op jit(solution)/shard_map/ppermute | solution.py:232
  15.4 9.6 %collective-permute-start.5 = (f32[32,240]{1,0:T(8,128)S(1)}, f32[32,240]{1,0:T(8,128)S(1)}, u32[]{:S(2)}, u32[]{:S(2)}) collective-permute-start(f32[32,240]{1,0:T(8,128)S(1)} %get-tuple-element.29), channel_id=1, source_target_pairs={{4,8},{8,4},{12,16},{16,12},{20,24},{24,20},{5,9},{9,5},{13,17},{1... | collective-permute-start | bytes 92168 | tf_op jit(solution)/shard_map/ppermute | solution.py:233
  16.1 0.7 %copy-start.4 = (f32[6,6]{1,0:T(8,128)S(1)}, f32[6,6]{1,0:T(8,128)}, u32[]{:S(2)}) copy-start(f32[6,6]{1,0:T(8,128)} %time_ref.1) | copy-start | bytes 436
  16.8 0.7 %copy-start.5 = (f32[4,4]{1,0:T(4,128)S(1)}, f32[4,4]{1,0:T(4,128)}, u32[]{:S(2)}) copy-start(f32[4,4]{1,0:T(4,128)} %field_ref.1) | copy-start | bytes 196
  17.5 0.7 %copy-start.7 = (f32[21]{0:T(128)S(1)}, f32[21]{0:T(128)}, u32[]{:S(2)}) copy-start(f32[21]{0:T(128)} %north_ref.1) | copy-start | bytes 256
  19.5 2.2 %copy-start = (bf16[32,256,256]{2,1,0:T(8,128)(2,1)S(1)}, bf16[32,256,256]{2,1,0:T(8,128)(2,1)}, u32[]{:S(2)}) copy-start(bf16[32,256,256]{2,1,0:T(8,128)(2,1)} %modes_ref.3) | copy-start | bytes 12582916
  21.7 0.7 %copy-start.6 = (f32[21]{0:T(128)S(1)}, f32[21]{0:T(128)}, u32[]{:S(2)}) copy-start(f32[21]{0:T(128)} %east_ref.3) | copy-start | bytes 256
  22.4 2.7 %copy-start.1 = (bf16[32,256,256]{2,1,0:T(8,128)(2,1)S(1)}, bf16[32,256,256]{2,1,0:T(8,128)(2,1)}, u32[]{:S(2)}) copy-start(bf16[32,256,256]{2,1,0:T(8,128)(2,1)} %modes_ref.3) | copy-start | bytes 12582916
  25.0 18.5 %copy-start.3 = (f32[64,24]{0,1:T(8,128)S(1)}, f32[64,24]{0,1:T(8,128)}, u32[]{:S(2)}) copy-start(f32[64,24]{0,1:T(8,128)} %param.13) | copy-start | bytes 18436

commit v2 on v1

v2 whole, which is shorter than its diff:
```python
import functools

import jax
import jax.numpy as jnp
from jax import lax
from jax.experimental import pallas as pl
from jax.experimental.pallas import tpu as pltpu
from jax.sharding import PartitionSpec as P

F32, BF16 = jnp.float32, jnp.bfloat16
NN = (((1,), (0,)), ((), ()))
NT = (((1,), (1,)), ((), ()))
TN = (((0,), (0,)), ((), ()))
STRIP = 12
EDGE = 32


def dot(a, b, dims=NN):
    return lax.dot_general(a, b, dims, preferred_element_type=F32)


def halves(v):
    high = v.astype(BF16)
    return high, (v - high.astype(F32)).astype(BF16)


def dot2(a, b, dims=NN):
    (ah, al), (bh, bl) = a, b
    return dot(ah, bh, dims) + dot(ah, bl, dims) + dot(al, bh, dims)


def iota(shape, dim):
    return lax.broadcasted_iota(jnp.int32, shape, dim)


def stacked(v):
    high = v.astype(BF16).astype(F32)
    parts = [high, v - high, high]
    if (3 * v.shape[0]) % 16:
        parts.append(jnp.zeros((-3 * v.shape[0] % 96, v.shape[1]), F32))
    return jnp.concatenate(parts, axis=0).astype(BF16)


def wide(m):
    high = m.astype(BF16).astype(F32)
    parts = [high, high, m - high]
    if (3 * m.shape[1]) % 16:
        parts.append(jnp.zeros((m.shape[0], -3 * m.shape[1] % 96), F32))
    return jnp.concatenate(parts, axis=1).astype(BF16)


def turn_kernel(reach, a_ref, t_ref, s1_ref):
    t_ref[...] = jnp.swapaxes(a_ref[...], 0, 1)
    odd = lax.axis_index("gx") % 2
    s1_ref[...] = t_ref[pl.ds((1 - odd) * (t_ref.shape[0] - reach), reach)]


def strip_kernel(reach, t_ref, core_ref, chip_ref):
    width_x, channels, width_y = t_ref.shape
    odd = lax.axis_index("gy") % 2
    row, col = iota((EDGE, width_y), 0), iota((EDGE, width_y), 1)
    to_core = row < STRIP
    at = jnp.where(to_core, row, row - STRIP)
    low = jnp.where(to_core, odd, 1 - odd) == 1
    wanted = at + jnp.where(low, 0, width_y - reach)
    pick = jnp.where((col == wanted) & (at < reach), 1.0, 0.0).astype(BF16)
    data = t_ref[...].reshape(width_x * channels, width_y)
    high, rest = halves(data)
    low_part = (data - high.astype(F32) - rest.astype(F32)).astype(BF16)
    strips = dot(pick, high, NT) + dot(pick, rest, NT) + dot(pick, low_part, NT)
    core_ref[...] = strips[:STRIP]
    chip_ref[...] = strips[STRIP : 2 * STRIP]


def band_kernel(
    reach, east_hbm, north_hbm, field_hbm, time_hbm, a_ref, y_ref, bh_ref, bl_ref, eh_ref, el_ref, x_ref, mix_ref, taps_ref,
    east_ref, north_ref, field_ref, time_ref, sem,
):
    copies = [
        pltpu.make_async_copy(source, target, sem.at[i])
        for i, (source, target) in enumerate(
            ((east_hbm, east_ref), (north_hbm, north_ref), (field_hbm, field_ref), (time_hbm, time_ref))
        )
    ]
    for copy in copies:
        copy.start()
    channels, width_x, width_y = a_ref.shape
    span = 2 * reach + 1
    odd = lax.axis_index("gy") % 2
    shift = iota((width_y, width_y), 0) - iota((width_y, width_y), 1) + reach
    row = iota((EDGE, width_y), 0)
    from_core = row < STRIP
    at = jnp.where(from_core, row, row - STRIP)
    left = jnp.where(from_core, odd, 1 - odd) == 1
    source = jnp.where(left, at - reach, width_y + at)
    edge_shift = jnp.where(at < reach, source - iota((EDGE, width_y), 1) + reach, -1)
    x_shift = iota((width_x, width_x), 1) - iota((width_x, width_x), 0) + reach
    data = halves(a_ref[...].reshape(channels * width_x, width_y))
    for copy in copies:
        copy.wait()
    first = iota((8, width_y), 1)
    base = jnp.zeros((8, width_y), F32)
    edge = jnp.zeros((EDGE, width_y), F32)
    along = jnp.zeros((width_x, width_x), F32)
    for j in range(span):
        tap = north_ref[j]
        base = jnp.where(first == (reach - j) % width_y, tap, base)
        edge = jnp.where(edge_shift == j, tap, edge)
        along = jnp.where(x_shift == j, east_ref[j], along)
        taps_ref[j] = jnp.full(taps_ref.shape[1:], east_ref[j], F32)
    rolled = pltpu.roll(jnp.broadcast_to(base[:1], (width_y, width_y)), 0, 1, stride=1, stride_axis=0)
    band = halves(jnp.where((shift >= 0) & (shift < span), rolled, 0.0))
    edge = halves(edge)
    bh_ref[...], bl_ref[...] = band
    eh_ref[...], el_ref[...] = edge
    x_ref[...] = wide(along)
    fields, levels = field_ref.shape[0], time_ref.shape[0]
    rows = mix_ref.shape[0]
    out, into = iota((rows, channels), 0), iota((rows, channels), 1)
    by_field = jnp.zeros((rows, channels), F32)
    by_time = jnp.zeros((rows, channels), F32)
    for g in range(fields):
        for f in range(fields):
            by_field = jnp.where((into // levels == g) & (out // levels == f), field_ref[g, f], by_field)
    for s in range(levels):
        for t in range(levels):
            by_time = jnp.where((into % levels == s) & (out % levels == t), time_ref[s, t], by_time)
    mix_ref[...] = wide(by_field * by_time)
    y_ref[...] = dot2(data, band).reshape(a_ref.shape)


def joined(core, chip):
    return jnp.concatenate([core, chip, jnp.zeros((EDGE - 2 * STRIP, core.shape[1]), F32)], axis=0)


def corner_kernel(reach, t_ref, core_ref, chip_ref, s2_ref):
    width_x, channels, width_y = t_ref.shape
    odd = lax.axis_index("gx") % 2
    s2_ref[:reach] = t_ref[pl.ds(odd * (width_x - reach), reach)]
    strips = joined(core_ref[...], chip_ref[...])[: 2 * STRIP]
    top = strips[:, : reach * channels]
    bottom = strips[:, (width_x - reach) * channels :]
    rows = jnp.where(odd == 1, bottom, top)
    s2_ref[reach] = jnp.concatenate([rows, jnp.zeros((2 * STRIP, width_y - reach * channels), F32)], axis=1)


def tile_kernel(reach, modes_hbm, y_ref, core_ref, chip_ref, eh_ref, el_ref, x_ref, mix_ref, s_ref, p_ref, modes_ref, sem):
    channels, width_x, width_y = y_ref.shape
    blocks = sem.shape[0]
    size = width_x // blocks
    copies = [
        pltpu.make_async_copy(modes_hbm.at[pl.ds(b * size, size)], modes_ref.at[pl.ds(b * size, size)], sem.at[b])
        for b in range(blocks)
    ]
    for copy in copies:
        copy.start()
    more = dot2(halves(joined(core_ref[...], chip_ref[...])), (eh_ref[...], el_ref[...]), TN)
    y = y_ref[...] + jnp.swapaxes(more.reshape(width_x, channels, width_y), 0, 1)
    along = x_ref[...]
    smooth = jnp.stack([dot(along, stacked(y[c])) for c in range(channels)])
    s_ref[...] = jnp.swapaxes(smooth, 0, 1)
    mix = mix_ref[...]
    acc = jnp.zeros((mix.shape[0], modes_ref.shape[2]), F32)
    inner = [dot(mix, stacked(s_ref[x])).astype(BF16) for x in range(reach, width_x - reach)]
    for copy in copies:
        copy.wait()
    for x in range(reach, width_x - reach):
        acc = acc + dot(inner[x - reach], modes_ref[x])
    p_ref[...] = acc


def side(reach, left, rows, corners, s_ref, taps_ref, bh_ref, bl_ref, eh_ref, el_ref, mix_ref, modes_ref, by_y):
    width_x, channels, width_y = s_ref.shape
    by = dot2(halves(rows.reshape(reach * channels, width_y)), (bh_ref[...], bl_ref[...]))
    by = by + dot2(halves(corners), (eh_ref[...], el_ref[...]), TN)
    by_y[...] = by.reshape(reach, channels, width_y)
    split = (channels // 8, 8, width_y)
    came = [by_y[left * (reach - 1 - n) + (1 - left) * n].reshape(split) for n in range(reach)]
    taps = [taps_ref[left * d + (1 - left) * (2 * reach - d)][None] for d in range(reach)]
    mix = mix_ref[...]
    acc = jnp.zeros((mix.shape[0], modes_ref.shape[2]), F32)
    for m in range(reach):
        x = left * (reach - 1 - m) + (1 - left) * (width_x - reach + m)
        value = s_ref[x].reshape(split)
        for n in range(m + 1):
            value = value + taps[m - n] * came[n]
        mixed = dot(mix, stacked(value.reshape(channels, width_y))).astype(BF16)
        acc = acc + dot(mixed, modes_ref[x])
    return acc


def first_kernel(reach, p_ref, r_ref, core_ref, chip_ref, s_ref, *rest):
    *refs, out_ref, by_y = rest
    odd = lax.axis_index("gx") % 2
    corners = joined(core_ref[...], chip_ref[...])
    out_ref[...] = p_ref[...] + side(reach, odd, r_ref[...], corners, s_ref, *refs, by_y)


def second_kernel(reach, owned, p_ref, r_ref, s_ref, *rest):
    *refs, out_ref, by_y = rest
    odd = lax.axis_index("gx") % 2
    _, channels, width_y = s_ref.shape
    corners = jnp.concatenate([r_ref[reach], jnp.zeros((EDGE - 2 * STRIP, width_y), F32)], axis=0)[:, : reach * channels]
    total = p_ref[...] + side(reach, 1 - odd, r_ref[:reach], corners, s_ref, *refs, by_y)
    folds = 128 // owned
    rows = channels // folds
    for g in range(total.shape[1] // owned):
        piece = jnp.concatenate(
            [total[k * rows : (k + 1) * rows, g * owned : (g + 1) * owned] for k in range(folds)], axis=1
        )
        for k in range(out_ref.shape[0]):
            out_ref[k, g] = piece


def sum_kernel(parts_ref, coefficients_ref, out_ref):
    channels, owned = out_ref.shape
    folds = 128 // owned
    total = jnp.sum(parts_ref[...], axis=0)
    pieces = [total[:, k * owned : (k + 1) * owned] for k in range(folds)]
    out_ref[...] = coefficients_ref[...] + jnp.concatenate(pieces, axis=0)


def vmem(array):
    return pltpu.with_memory_space_constraint(array, pltpu.VMEM)


def call(body, ins, outs, scratch=(), flops=0, outside=0, keep=True):
    args = [item if i < outside else vmem(item) for i, item in enumerate(ins)]
    specs = [pl.BlockSpec(memory_space=pl.ANY if i < outside else pltpu.VMEM) for i in range(len(ins))]
    make = pltpu.VMEM if keep else jax.ShapeDtypeStruct
    return pl.pallas_call(
        body,
        out_shape=[make(shape, dtype) for shape, dtype in outs],
        in_specs=specs,
        out_specs=[pl.BlockSpec(memory_space=pltpu.VMEM)] * len(outs),
        scratch_shapes=list(scratch),
        compiler_params=pltpu.CompilerParams(vmem_limit_bytes=24 << 20),
        cost_estimate=pl.CostEstimate(flops=flops, bytes_accessed=1 << 20, transcendentals=0),
    )(*args)


def pairs(count, first):
    found = []
    for low in range(first, count - 1, 2):
        found += [(low, low + 1), (low + 1, low)]
    return found


def local(adjoint_forcing, field_mixing, time_mixing, kernel_east, kernel_north, spatial_modes, coefficients):
    fields, levels, width_x, width_y = adjoint_forcing.shape
    channels, modes, owned = fields * levels, spatial_modes.shape[2], coefficients.shape[0]
    reach = (kernel_east.shape[0] - 1) // 2
    count_x, count_y = lax.axis_size("gx"), lax.axis_size("gy")
    raw = vmem(adjoint_forcing.reshape(channels, width_x, width_y))
    slab = (reach, channels, width_y)
    full = ((width_x, channels, width_y), F32)
    t, s1 = call(functools.partial(turn_kernel, reach), [raw], [full, (slab, F32)])
    r1 = lax.ppermute(s1, "gx", pairs(count_x, 0))
    strip = ((STRIP, width_x * channels), F32)
    core, chip = call(functools.partial(strip_kernel, reach), [t], [strip, strip])
    core = lax.ppermute(core, "gy", pairs(count_y, 0))
    chip = lax.ppermute(chip, "gy", pairs(count_y, 1))
    edge = ((EDGE, width_y), BF16)
    band = ((width_y, width_y), BF16)
    wide_rows = -(-channels // 16) * 16
    y, bh, bl, eh, el, along, mix, taps = call(
        functools.partial(band_kernel, reach),
        [kernel_east, kernel_north, field_mixing, time_mixing, raw],
        [
            ((channels, width_x, width_y), F32),
            band,
            band,
            edge,
            edge,
            ((width_x, 3 * width_x + -3 * width_x % 96), BF16),
            ((wide_rows, 3 * channels + -3 * channels % 96), BF16),
            ((2 * reach + 1, 8, width_y), F32),
        ],
        [
            pltpu.SMEM(kernel_east.shape, F32),
            pltpu.SMEM(kernel_north.shape, F32),
            pltpu.SMEM(field_mixing.shape, F32),
            pltpu.SMEM(time_mixing.shape, F32),
            pltpu.SemaphoreType.DMA((4,)),
        ],
        outside=4,
    )
    (s2,) = call(functools.partial(corner_kernel, reach), [t, core, chip], [((reach + 1, channels, width_y), F32)])
    r2 = lax.ppermute(s2, "gx", pairs(count_x, 1))
    strip = ((STRIP, reach * channels), F32)
    core1, chip1 = call(functools.partial(strip_kernel, reach), [r1], [strip, strip])
    core1 = lax.ppermute(core1, "gy", pairs(count_y, 0))
    chip1 = lax.ppermute(chip1, "gy", pairs(count_y, 1))
    share = ((wide_rows, modes), F32)
    smooth, inner, held = call(
        functools.partial(tile_kernel, reach),
        [spatial_modes, y, core, chip, eh, el, along, mix],
        [full, share, (spatial_modes.shape, BF16)],
        [pltpu.SemaphoreType.DMA((4,))],
        outside=1,
    )
    both = [smooth, taps, bh, bl, eh, el, mix, held]
    (partial,) = call(
        functools.partial(first_kernel, reach), [inner, r1, core1, chip1, *both], [share], [pltpu.VMEM(slab, F32)]
    )
    folds = 128 // owned
    (out,) = call(
        functools.partial(second_kernel, reach, owned),
        [partial, r2, *both],
        [((count_x, count_y, channels // folds, 128), F32)],
        [pltpu.VMEM(slab, F32)],
    )
    out = out.reshape((count_x * count_y,) + out.shape[2:])
    parts = lax.all_to_all(out, ("gx", "gy"), 0, 0, tiled=True)
    (gradient,) = call(sum_kernel, [parts, coefficients.T], [((channels, owned), F32)], keep=False)
    return gradient.T


def solution(mesh):
    in_specs = (P(None, None, "gx", "gy"), P(), P(), P(), P(), P("gx", "gy", None), P("gy", None))
    out_specs = P("gy", None)
    return jax.shard_map(local, mesh=mesh, in_specs=in_specs, out_specs=out_specs, check_vma=False)
```

time: 45.3 us -> 53.9 us (1.19)
  waiting for transfers between devices: 2.35 us -> 9.16 us
  Pallas kernels: 7.16 us -> 8.96 us
  blocking collectives: 16.4 us -> 15.3 us
    ppermute x1, waiting for transfers between devices: 0.01 us -> 7.4 us  [local(): r1 = lax.ppermute(s1, 'gx', pairs(count_x, 0))]
    ppermute x2, starting transfers between devices: 4.98 us -> 2.69 us  [the longest x1 2.62 us: local(): chip1 = lax.ppermute(chip1, 'gy', pairs(count_y, 1))]
    ppermute x1, starting transfers between devices: 2.1 us -> 4.36 us  [local(): r1 = lax.ppermute(s1, 'gx', pairs(count_x, 0))]
    pallas_call x7 -> x9, Pallas kernels: 7.16 us -> 8.96 us  [call(): pl.pallas_call(body, out_shape=[make(shape, dtype) for shape, dtype in ou...]
    ppermute x1, starting transfers between devices: 3.05 us -> 4.49 us  [local(): chip = lax.ppermute(chip, 'gy', pairs(count_y, 1))]
    all_to_all x1, blocking collectives: 16.4 us -> 15.3 us  [local(): parts = lax.all_to_all(out, ('gx', 'gy'), 0, 0, tiled=True)]
    ppermute x1, starting transfers between devices: 0.97 us -> 0.07 us  [local(): core = lax.ppermute(core, 'gy', pairs(count_y, 0))]
    ppermute x1, waiting for transfers between devices: 2.33 us -> 1.75 us  [local(): chip = lax.ppermute(chip, 'gy', pairs(count_y, 1))]
  transfers between devices with their start and end apart: 6 -> 6, of which waited for: 1 -> 2; matrix products, arithmetic and copies ran while one was open for 0% -> 0% of each run, Pallas kernels for 10% -> 10%
where the time goes in v2:
time: 53.9 us; the launch traced here: 53 us
  blocking collectives  15.3 us (28%)
  starting transfers between devices  12.3 us (23%)
  waiting for transfers between devices  9.16 us (17%)
  Pallas kernels  8.96 us (17%)
  local copies, waits for them, and re-layouts  7.14 us (13%)
    all_to_all x1, blocking collectives, local(): parts = lax.all_to_all(out, ('gx', 'gy'), 0, 0, tiled=True)  15.3 us
    pallas_call x9, Pallas kernels, call(): pl.pallas_call(body, out_shape=[make(shape, dtype) for shape, dtype in ou...  8.96 us
    ppermute x1, waiting for transfers between devices, local(): r1 = lax.ppermute(s1, 'gx', pairs(count_x, 0))  7.4 us
    unnamed x16, local copies, waits for them, and re-layouts  7.14 us
    ppermute x1, starting transfers between devices, local(): chip = lax.ppermute(chip, 'gy', pairs(count_y, 1))  4.49 us
    ppermute x1, starting transfers between devices, local(): r1 = lax.ppermute(s1, 'gx', pairs(count_x, 0))  4.36 us
    ppermute x1, starting transfers between devices, local(): chip1 = lax.ppermute(chip1, 'gy', pairs(count_y, 1))  2.62 us
    ppermute x1, waiting for transfers between devices, local(): chip = lax.ppermute(chip, 'gy', pairs(count_y, 1))  1.75 us
  transfers between devices with their start and end apart: 6, of which 2 were waited for; matrix products, arithmetic and copies ran while one was open for 0% of the time, Pallas kernels for 10%

profile of v2, /device:TPU:1, one launch (start us, length us, event | category | flops | bytes accessed | tf_op | source)
XLA Modules:
  0.0 53.0 jit_solution(7439542466133947838)
XLA Ops:
  0.0 0.0 copy-start.1
  0.0 1.1 %copy-done.1 = f32[4,6,32,256]{3,2,1,0:T(8,128)S(1)} copy-done((f32[4,6,32,256]{3,2,1,0:T(8,128)S(1)}, f32[4,6,32,256]{3,2,1,0:T(8,128)}, u32[]{:S(2)}) %copy-start.1) | copy-done | bytes 786456
  1.1 0.2 shard_map.74
  1.3 0.5 shard_map.75
  1.8 0.1 collective-permute-start
  1.9 4.5 %collective-permute-start.1 = (f32[12,768]{1,0:T(8,128)S(1)}, f32[12,768]{1,0:T(8,128)S(1)}, u32[]{:S(2)}, u32[]{:S(2)}) collective-permute-start(f32[12,768]{1,0:T(8,128)S(1)} %get-tuple-element.25), channel_id=1, source_target_pairs={{1,2},{2,1},{5,6},{6,5},{9,10},{10,9},{13,14},{14,13},{17,18},{18,... | collective-permute-start | bytes 110600 | tf_op jit(solution)/shard_map/ppermute | solution.py:262
  6.4 0.0 collective-permute-done.core_ref
  6.4 1.7 %collective-permute-done.1.chip_ref = f32[12,768]{1,0:T(8,128)S(1)} collective-permute-done((f32[12,768]{1,0:T(8,128)S(1)}, f32[12,768]{1,0:T(8,128)S(1)}, u32[]{:S(2)}, u32[]{:S(2)}) %collective-permute-start.1) | collective-permute-done | bytes 36896 | tf_op jit(solution)/shard_map/ppermute | solution.py:262
  8.1 0.1 shard_map.79
  8.3 0.7 %collective-permute-start.5 = (f32[11,24,256]{2,1,0:T(8,128)S(1)}, f32[11,24,256]{2,1,0:T(8,128)S(1)}, u32[]{:S(2)}, u32[]{:S(2)}) collective-permute-start(f32[11,24,256]{2,1,0:T(8,128)S(1)} %shard_map.79), channel_id=1, source_target_pairs={{4,8},{8,4},{12,16},{16,12},{20,24},{24,20},{5,9},{9,5},{13,17},{1... | collective-permute-start | bytes 811016 | tf_op jit(solution)/shard_map/ppermute | solution.py:289
  8.9 4.4 %collective-permute-start.2 = (f32[10,24,256]{2,1,0:T(8,128)S(1)}, f32[10,24,256]{2,1,0:T(8,128)S(1)}, u32[]{:S(2)}, u32[]{:S(2)}) collective-permute-start(f32[10,24,256]{2,1,0:T(8,128)S(1)} %get-tuple-element.31), channel_id=1, source_target_pairs={{0,4},{4,0},{8,12},{12,8},{16,20},{20,16},{24,28},{28,24},{1,5},{5... | collective-permute-start | bytes 737288 | tf_op jit(solution)/shard_map/ppermute | solution.py:258
  13.3 7.4 %collective-permute-done.2.t_ref.r_ref = f32[10,24,256]{2,1,0:T(8,128)S(1)} collective-permute-done((f32[10,24,256]{2,1,0:T(8,128)S(1)}, f32[10,24,256]{2,1,0:T(8,128)S(1)}, u32[]{:S(2)}, u32[]{:S(2)}) %collective-permute-start.2) | collective-permute-done | bytes 245792 | tf_op jit(solution)/shard_map/ppermute | solution.py:258
  20.7 0.2 shard_map.77
  20.9 0.1 collective-permute-start.3
  21.0 2.6 %collective-permute-start.4 = (f32[12,240]{1,0:T(8,128)S(1)}, f32[12,240]{1,0:T(8,128)S(1)}, u32[]{:S(2)}, u32[]{:S(2)}) collective-permute-start(f32[12,240]{1,0:T(8,128)S(1)} %get-tuple-element.33), channel_id=1, source_target_pairs={{1,2},{2,1},{5,6},{6,5},{9,10},{10,9},{13,14},{14,13},{17,18},{18,... | collective-permute-start | bytes 34568 | tf_op jit(solution)/shard_map/ppermute | solution.py:293
  23.6 0.0 copy-start.2
  23.6 1.1 %copy-done.2 = f32[4,6,32,256]{3,2,1,0:T(8,128)S(1)} copy-done((f32[4,6,32,256]{3,2,1,0:T(8,128)S(1)}, f32[4,6,32,256]{3,2,1,0:T(8,128)}, u32[]{:S(2)}) %copy-start.2) | copy-done | bytes 786456
  24.7 0.0 copy-start.4
  24.7 0.7 %copy-done.4 = f32[6,6]{1,0:T(8,128)S(1)} copy-done((f32[6,6]{1,0:T(8,128)S(1)}, f32[6,6]{1,0:T(8,128)}, u32[]{:S(2)}) %copy-start.4) | copy-done | bytes 168
  25.4 0.0 copy-start.5
  25.4 0.7 %copy-done.5 = f32[4,4]{1,0:T(4,128)S(1)} copy-done((f32[4,4]{1,0:T(4,128)S(1)}, f32[4,4]{1,0:T(4,128)}, u32[]{:S(2)}) %copy-start.5) | copy-done | bytes 88
  26.1 0.0 copy-start.6
  26.1 0.7 %copy-done.6 = f32[21]{0:T(128)S(1)} copy-done((f32[21]{0:T(128)S(1)}, f32[21]{0:T(128)}, u32[]{:S(2)}) %copy-start.6) | copy-done | bytes 108
  26.8 0.0 copy-start.7
  26.8 0.7 %copy-done.7 = f32[21]{0:T(128)S(1)} copy-done((f32[21]{0:T(128)S(1)}, f32[21]{0:T(128)}, u32[]{:S(2)}) %copy-start.7) | copy-done | bytes 108
  27.4 1.3 %shard_map.73 = (f32[24,32,256]{2,1,0:T(8,128)S(1)}, bf16[256,256]{1,0:T(8,128)(2,1)S(1)}, bf16[256,256]{1,0:T(8,128)(2,1)S(1)}, bf16[32,256]{1,0:T(8,128)(2,1)S...) custom-call(f32[21]{0:T(128)S(1)} %copy-done.6, ...), custom_call_target="tpu_custom_call" | custom-call | bytes 1048576 | tf_op jit(solution)/shard_map/pallas_call | solution.py:231
  28.7 0.0 copy-start
  28.8 2.2 %copy-done = bf16[32,256,256]{2,1,0:T(8,128)(2,1)S(1)} copy-done((bf16[32,256,256]{2,1,0:T(8,128)(2,1)S(1)}, bf16[32,256,256]{2,1,0:T(8,128)(2,1)}, u32[]{:S(2)}) %copy-start) | copy-done | bytes 4194328
  30.9 2.3 %shard_map.76 = (f32[32,24,256]{2,1,0:T(8,128)S(1)}, f32[32,256]{1,0:T(8,128)S(1)}, bf16[32,256,256]{2,1,0:T(8,128)(2,1)S(1)}) custom-call(bf16[32,256,256]{2,1,0:T(8,128)(2,1)S(1)} %copy-done, f32[24,32,256]{2,1,0:T(8,128)S(1)} %get-tuple-element.22.y_ref, f32[12,768]{1,0:T(8,128)S(1)} %collective-permute-done.core_ref, ...), custom_call_target="tpu_custom_call" | custom-call | bytes 1048576 | tf_op jit(solution)/shard_map/pallas_call | solution.py:231
  33.2 0.0 collective-permute-done.3.core_ref
  33.2 0.0 collective-permute-done.4.chip_ref
  33.2 1.8 %shard_map.78.p_ref = f32[32,256]{1,0:T(8,128)S(1)} custom-call(f32[32,256]{1,0:T(8,128)S(1)} %get-tuple-element.30.p_ref, f32[10,24,256]{2,1,0:T(8,128)S(1)} %collective-permute-done.2.t_ref.r_ref, f32[12,240]{1,0:T(8,128)S(1)} %collective-permute-done.3.core_ref, f32[12,240]{1,0:T(8,128)S(1)} %collective-permute-done.4.chip_ref, ...), custom_call_target="tpu_custom_call" | custom-call | bytes 1048576 | tf_op jit(solution)/shard_map/pallas_call | solution.py:231
  35.0 0.0 copy-start.3
  35.0 0.0 collective-permute-done.5.r_ref
  35.0 1.9 %shard_map.80 = f32[8,4,12,128]{3,2,1,0:T(8,128)S(1)} custom-call(f32[32,256]{1,0:T(8,128)S(1)} %shard_map.78.p_ref, f32[11,24,256]{2,1,0:T(8,128)S(1)} %collective-permute-done.5.r_ref, f32[32,24,256]{2,1,0:T(8,128)S(1)} %get-tuple-element.34.s_ref, f32[21,8,256]{2,1,0:T(8,128)S(1)} %get-tuple-element.35.rest_0_, ...), custom_call_target="tpu_custom_call" | custom-call | bytes 1048576 | tf_op jit(solution)/shard_map/pallas_call | solution.py:231
  36.9 15.3 %all_to_all.5.parts_ref = f32[32,12,128]{2,1,0:T(8,128)S(1)} all-to-all(f32[32,12,128]{2,1,0:T(8,128)S(1)} %bitcast.6), channel_id=1, replica_groups=mesh['gx'=8,'gy'=4] {'gx','gy'}, dimensions={0} | all-to-all | bytes 393216 | tf_op jit(solution)/shard_map/all_to_all | solution.py:314
  52.3 0.0 copy-done.3
  52.3 0.7 %shard_map.81 = f32[24,64]{1,0:T(8,128)} custom-call(f32[32,12,128]{2,1,0:T(8,128)S(1)} %all_to_all.5.parts_ref, f32[24,64]{1,0:T(8,128)S(1)} %bitcast.7), custom_call_target="tpu_custom_call" | custom-call | bytes 1048576 | tf_op jit(solution)/shard_map/pallas_call | solution.py:231
Async XLA Ops:
  0.0 1.1 %copy-start.1 = (f32[4,6,32,256]{3,2,1,0:T(8,128)S(1)}, f32[4,6,32,256]{3,2,1,0:T(8,128)}, u32[]{:S(2)}) copy-start(f32[4,6,32,256]{3,2,1,0:T(8,128)} %param.7) | copy-start | bytes 2359300
  1.8 4.6 %collective-permute-start = (f32[12,768]{1,0:T(8,128)S(1)}, f32[12,768]{1,0:T(8,128)S(1)}, u32[]{:S(2)}, u32[]{:S(2)}) collective-permute-start(f32[12,768]{1,0:T(8,128)S(1)} %get-tuple-element.24), channel_id=1, source_target_pairs={{0,1},{1,0},{2,3},{3,2},{4,5},{5,4},{6,7},{7,6},{8,9},{9,8},{10,11... | collective-permute-start | bytes 110600 | tf_op jit(solution)/shard_map/ppermute | solution.py:261
  1.9 6.3 %collective-permute-start.1 = (f32[12,768]{1,0:T(8,128)S(1)}, f32[12,768]{1,0:T(8,128)S(1)}, u32[]{:S(2)}, u32[]{:S(2)}) collective-permute-start(f32[12,768]{1,0:T(8,128)S(1)} %get-tuple-element.25), channel_id=1, source_target_pairs={{1,2},{2,1},{5,6},{6,5},{9,10},{10,9},{13,14},{14,13},{17,18},{18,... | collective-permute-start | bytes 110600 | tf_op jit(solution)/shard_map/ppermute | solution.py:262
  8.3 26.8 %collective-permute-start.5 = (f32[11,24,256]{2,1,0:T(8,128)S(1)}, f32[11,24,256]{2,1,0:T(8,128)S(1)}, u32[]{:S(2)}, u32[]{:S(2)}) collective-permute-start(f32[11,24,256]{2,1,0:T(8,128)S(1)} %shard_map.79), channel_id=1, source_target_pairs={{4,8},{8,4},{12,16},{16,12},{20,24},{24,20},{5,9},{9,5},{13,17},{1... | collective-permute-start | bytes 811016 | tf_op jit(solution)/shard_map/ppermute | solution.py:289
  8.9 11.8 %collective-permute-start.2 = (f32[10,24,256]{2,1,0:T(8,128)S(1)}, f32[10,24,256]{2,1,0:T(8,128)S(1)}, u32[]{:S(2)}, u32[]{:S(2)}) collective-permute-start(f32[10,24,256]{2,1,0:T(8,128)S(1)} %get-tuple-element.31), channel_id=1, source_target_pairs={{0,4},{4,0},{8,12},{12,8},{16,20},{20,16},{24,28},{28,24},{1,5},{5... | collective-permute-start | bytes 737288 | tf_op jit(solution)/shard_map/ppermute | solution.py:258
  20.9 12.3 %collective-permute-start.3 = (f32[12,240]{1,0:T(8,128)S(1)}, f32[12,240]{1,0:T(8,128)S(1)}, u32[]{:S(2)}, u32[]{:S(2)}) collective-permute-start(f32[12,240]{1,0:T(8,128)S(1)} %get-tuple-element.32), channel_id=1, source_target_pairs={{0,1},{1,0},{2,3},{3,2},{4,5},{5,4},{6,7},{7,6},{8,9},{9,8},{10,11... | collective-permute-start | bytes 34568 | tf_op jit(solution)/shard_map/ppermute | solution.py:292
  21.0 12.2 %collective-permute-start.4 = (f32[12,240]{1,0:T(8,128)S(1)}, f32[12,240]{1,0:T(8,128)S(1)}, u32[]{:S(2)}, u32[]{:S(2)}) collective-permute-start(f32[12,240]{1,0:T(8,128)S(1)} %get-tuple-element.33), channel_id=1, source_target_pairs={{1,2},{2,1},{5,6},{6,5},{9,10},{10,9},{13,14},{14,13},{17,18},{18,... | collective-permute-start | bytes 34568 | tf_op jit(solution)/shard_map/ppermute | solution.py:293
  23.6 1.1 %copy-start.2 = (f32[4,6,32,256]{3,2,1,0:T(8,128)S(1)}, f32[4,6,32,256]{3,2,1,0:T(8,128)}, u32[]{:S(2)}) copy-start(f32[4,6,32,256]{3,2,1,0:T(8,128)} %param.7) | copy-start | bytes 2359300
  24.7 0.7 %copy-start.4 = (f32[6,6]{1,0:T(8,128)S(1)}, f32[6,6]{1,0:T(8,128)}, u32[]{:S(2)}) copy-start(f32[6,6]{1,0:T(8,128)} %time_hbm.1) | copy-start | bytes 436
  25.4 0.7 %copy-start.5 = (f32[4,4]{1,0:T(4,128)S(1)}, f32[4,4]{1,0:T(4,128)}, u32[]{:S(2)}) copy-start(f32[4,4]{1,0:T(4,128)} %field_hbm.1) | copy-start | bytes 196
  26.1 0.7 %copy-start.6 = (f32[21]{0:T(128)S(1)}, f32[21]{0:T(128)}, u32[]{:S(2)}) copy-start(f32[21]{0:T(128)} %east_hbm.1) | copy-start | bytes 256
  26.8 0.7 %copy-start.7 = (f32[21]{0:T(128)S(1)}, f32[21]{0:T(128)}, u32[]{:S(2)}) copy-start(f32[21]{0:T(128)} %north_hbm.1) | copy-start | bytes 256
  28.7 2.2 %copy-start = (bf16[32,256,256]{2,1,0:T(8,128)(2,1)S(1)}, bf16[32,256,256]{2,1,0:T(8,128)(2,1)}, u32[]{:S(2)}) copy-start(bf16[32,256,256]{2,1,0:T(8,128)(2,1)} %modes_hbm.1) | copy-start | bytes 12582916
  35.0 17.3 %copy-start.3 = (f32[64,24]{0,1:T(8,128)S(1)}, f32[64,24]{0,1:T(8,128)}, u32[]{:S(2)}) copy-start(f32[64,24]{0,1:T(8,128)} %param.13) | copy-start | bytes 18436

commit v3 on v2

--- a/solution.py
+++ b/solution.py
@@ -73,8 +73,8 @@
 
 
 def band_kernel(
-    reach, east_hbm, north_hbm, field_hbm, time_hbm, a_ref, y_ref, bh_ref, bl_ref, eh_ref, el_ref, x_ref, mix_ref, taps_ref,
-    east_ref, north_ref, field_ref, time_ref, sem,
+    reach, east_hbm, north_hbm, field_hbm, time_hbm, modes_hbm, t_ref, y_ref, bh_ref, bl_ref, eh_ref, el_ref, x_ref, mix_ref, taps_ref,
+    modes_ref, east_ref, north_ref, field_ref, time_ref, sem,
 ):
     copies = [
         pltpu.make_async_copy(source, target, sem.at[i])
@@ -84,7 +84,14 @@
     ]
     for copy in copies:
         copy.start()
-    channels, width_x, width_y = a_ref.shape
+    width_x, channels, width_y = t_ref.shape
+    half = width_x // 2
+    loads = [
+        pltpu.make_async_copy(modes_hbm.at[pl.ds(i * half, half)], modes_ref.at[pl.ds(i * half, half)], sem.at[len(copies) + i])
+        for i in range(2)
+    ]
+    for load in loads:
+        load.start()
     span = 2 * reach + 1
     odd = lax.axis_index("gy") % 2
     shift = iota((width_y, width_y), 0) - iota((width_y, width_y), 1) + reach
@@ -95,7 +102,7 @@
     source = jnp.where(left, at - reach, width_y + at)
     edge_shift = jnp.where(at < reach, source - iota((EDGE, width_y), 1) + reach, -1)
     x_shift = iota((width_x, width_x), 1) - iota((width_x, width_x), 0) + reach
-    data = halves(a_ref[...].reshape(channels * width_x, width_y))
+    data = halves(t_ref[...].reshape(width_x * channels, width_y))
     for copy in copies:
         copy.wait()
     first = iota((8, width_y), 1)
@@ -126,7 +133,9 @@
         for t in range(levels):
             by_time = jnp.where((into % levels == s) & (out % levels == t), time_ref[s, t], by_time)
     mix_ref[...] = wide(by_field * by_time)
-    y_ref[...] = dot2(data, band).reshape(a_ref.shape)
+    y_ref[...] = jnp.swapaxes(dot2(data, band).reshape(t_ref.shape), 0, 1)
+    for load in loads:
+        load.wait()
 
 
 def joined(core, chip):
@@ -144,32 +153,22 @@
     s2_ref[reach] = jnp.concatenate([rows, jnp.zeros((2 * STRIP, width_y - reach * channels), F32)], axis=1)
 
 
-def tile_kernel(reach, modes_hbm, y_ref, core_ref, chip_ref, eh_ref, el_ref, x_ref, mix_ref, s_ref, p_ref, modes_ref, sem):
+def tile_kernel(reach, y_ref, core_ref, chip_ref, eh_ref, el_ref, x_ref, mix_ref, modes_ref, s_ref, p_ref):
     channels, width_x, width_y = y_ref.shape
-    blocks = sem.shape[0]
-    size = width_x // blocks
-    copies = [
-        pltpu.make_async_copy(modes_hbm.at[pl.ds(b * size, size)], modes_ref.at[pl.ds(b * size, size)], sem.at[b])
-        for b in range(blocks)
-    ]
-    for copy in copies:
-        copy.start()
     more = dot2(halves(joined(core_ref[...], chip_ref[...])), (eh_ref[...], el_ref[...]), TN)
     y = y_ref[...] + jnp.swapaxes(more.reshape(width_x, channels, width_y), 0, 1)
     along = x_ref[...]
     smooth = jnp.stack([dot(along, stacked(y[c])) for c in range(channels)])
     s_ref[...] = jnp.swapaxes(smooth, 0, 1)
     mix = mix_ref[...]
-    acc = jnp.zeros((mix.shape[0], modes_ref.shape[2]), F32)
     inner = [dot(mix, stacked(s_ref[x])).astype(BF16) for x in range(reach, width_x - reach)]
-    for copy in copies:
-        copy.wait()
-    for x in range(reach, width_x - reach):
-        acc = acc + dot(inner[x - reach], modes_ref[x])
+    acc = dot(inner[0], modes_ref[reach])
+    for x in range(1, width_x - 2 * reach):
+        acc = acc + dot(inner[x], modes_ref[reach + x])
     p_ref[...] = acc
 
 
-def side(reach, left, rows, corners, s_ref, taps_ref, bh_ref, bl_ref, eh_ref, el_ref, mix_ref, modes_ref, by_y):
+def side(reach, left, rows, corners, s_ref, taps_ref, bh_ref, bl_ref, eh_ref, el_ref, mix_ref, modes_ref, by_y, mixed):
     width_x, channels, width_y = s_ref.shape
     by = dot2(halves(rows.reshape(reach * channels, width_y)), (bh_ref[...], bl_ref[...]))
     by = by + dot2(halves(corners), (eh_ref[...], el_ref[...]), TN)
@@ -178,46 +177,52 @@
     came = [by_y[left * (reach - 1 - n) + (1 - left) * n].reshape(split) for n in range(reach)]
     taps = [taps_ref[left * d + (1 - left) * (2 * reach - d)][None] for d in range(reach)]
     mix = mix_ref[...]
-    acc = jnp.zeros((mix.shape[0], modes_ref.shape[2]), F32)
     for m in range(reach):
         x = left * (reach - 1 - m) + (1 - left) * (width_x - reach + m)
         value = s_ref[x].reshape(split)
         for n in range(m + 1):
             value = value + taps[m - n] * came[n]
-        mixed = dot(mix, stacked(value.reshape(channels, width_y))).astype(BF16)
-        acc = acc + dot(mixed, modes_ref[x])
+        mixed[m] = dot(mix, stacked(value.reshape(channels, width_y))).astype(BF16)
+    acc = None
+    for m in range(reach):
+        term = dot(mixed[m], modes_ref[left * (reach - 1 - m) + (1 - left) * (width_x - reach + m)])
+        acc = term if acc is None else acc + term
     return acc
 
 
 def first_kernel(reach, p_ref, r_ref, core_ref, chip_ref, s_ref, *rest):
-    *refs, out_ref, by_y = rest
+    *refs, out_ref, by_y, mixed = rest
     odd = lax.axis_index("gx") % 2
     corners = joined(core_ref[...], chip_ref[...])
-    out_ref[...] = p_ref[...] + side(reach, odd, r_ref[...], corners, s_ref, *refs, by_y)
+    out_ref[...] = p_ref[...] + side(reach, odd, r_ref[...], corners, s_ref, *refs, by_y, mixed)
 
 
 def second_kernel(reach, owned, p_ref, r_ref, s_ref, *rest):
-    *refs, out_ref, by_y = rest
+    *refs, out_ref, by_y, mixed = rest
     odd = lax.axis_index("gx") % 2
     _, channels, width_y = s_ref.shape
     corners = jnp.concatenate([r_ref[reach], jnp.zeros((EDGE - 2 * STRIP, width_y), F32)], axis=0)[:, : reach * channels]
-    total = p_ref[...] + side(reach, 1 - odd, r_ref[:reach], corners, s_ref, *refs, by_y)
+    total = p_ref[...] + side(reach, 1 - odd, r_ref[:reach], corners, s_ref, *refs, by_y, mixed)
     folds = 128 // owned
     rows = channels // folds
+    high = out_ref.shape[3]
     for g in range(total.shape[1] // owned):
         piece = jnp.concatenate(
             [total[k * rows : (k + 1) * rows, g * owned : (g + 1) * owned] for k in range(folds)], axis=1
         )
         for k in range(out_ref.shape[0]):
-            out_ref[k, g] = piece
+            for j in range(out_ref.shape[2]):
+                out_ref[k, g, j] = piece[j * high : (j + 1) * high]
 
 
 def sum_kernel(parts_ref, coefficients_ref, out_ref):
     channels, owned = out_ref.shape
-    folds = 128 // owned
+    _, count, high, lanes = parts_ref.shape
     total = jnp.sum(parts_ref[...], axis=0)
-    pieces = [total[:, k * owned : (k + 1) * owned] for k in range(folds)]
-    out_ref[...] = coefficients_ref[...] + jnp.concatenate(pieces, axis=0)
+    for k in range(lanes // owned):
+        for j in range(count):
+            rows = pl.ds((k * count + j) * high, high)
+            out_ref[rows] = coefficients_ref[rows] + total[j, :, k * owned : (k + 1) * owned]
 
 
 def vmem(array):
@@ -225,8 +230,8 @@
 
 
 def call(body, ins, outs, scratch=(), flops=0, outside=0, keep=True):
-    args = [item if i < outside else vmem(item) for i, item in enumerate(ins)]
-    specs = [pl.BlockSpec(memory_space=pl.ANY if i < outside else pltpu.VMEM) for i in range(len(ins))]
+    args = [pltpu.with_memory_space_constraint(item, pltpu.HBM) if i < outside else vmem(item) for i, item in enumerate(ins)]
+    specs = [pl.BlockSpec(memory_space=pltpu.HBM if i < outside else pltpu.VMEM) for i in range(len(ins))]
     make = pltpu.VMEM if keep else jax.ShapeDtypeStruct
     return pl.pallas_call(
         body,
@@ -235,7 +240,7 @@
         out_specs=[pl.BlockSpec(memory_space=pltpu.VMEM)] * len(outs),
         scratch_shapes=list(scratch),
         compiler_params=pltpu.CompilerParams(vmem_limit_bytes=24 << 20),
-        cost_estimate=pl.CostEstimate(flops=flops, bytes_accessed=1 << 20, transcendentals=0),
+        cost_estimate=pl.CostEstimate(flops=int(1e9), bytes_accessed=1 << 20, transcendentals=0),
     )(*args)
 
 
@@ -251,7 +256,7 @@
     channels, modes, owned = fields * levels, spatial_modes.shape[2], coefficients.shape[0]
     reach = (kernel_east.shape[0] - 1) // 2
     count_x, count_y = lax.axis_size("gx"), lax.axis_size("gy")
-    raw = vmem(adjoint_forcing.reshape(channels, width_x, width_y))
+    raw = adjoint_forcing.reshape(channels, width_x, width_y)
     slab = (reach, channels, width_y)
     full = ((width_x, channels, width_y), F32)
     t, s1 = call(functools.partial(turn_kernel, reach), [raw], [full, (slab, F32)])
@@ -263,9 +268,9 @@
     edge = ((EDGE, width_y), BF16)
     band = ((width_y, width_y), BF16)
     wide_rows = -(-channels // 16) * 16
-    y, bh, bl, eh, el, along, mix, taps = call(
+    y, bh, bl, eh, el, along, mix, taps, held = call(
         functools.partial(band_kernel, reach),
-        [kernel_east, kernel_north, field_mixing, time_mixing, raw],
+        [kernel_east, kernel_north, field_mixing, time_mixing, spatial_modes, t],
         [
             ((channels, width_x, width_y), F32),
             band,
@@ -275,15 +280,16 @@
             ((width_x, 3 * width_x + -3 * width_x % 96), BF16),
             ((wide_rows, 3 * channels + -3 * channels % 96), BF16),
             ((2 * reach + 1, 8, width_y), F32),
+            (spatial_modes.shape, BF16),
         ],
         [
             pltpu.SMEM(kernel_east.shape, F32),
             pltpu.SMEM(kernel_north.shape, F32),
             pltpu.SMEM(field_mixing.shape, F32),
             pltpu.SMEM(time_mixing.shape, F32),
-            pltpu.SemaphoreType.DMA((4,)),
+            pltpu.SemaphoreType.DMA((6,)),
         ],
-        outside=4,
+        outside=5,
     )
     (s2,) = call(functools.partial(corner_kernel, reach), [t, core, chip], [((reach + 1, channels, width_y), F32)])
     r2 = lax.ppermute(s2, "gx", pairs(count_x, 1))
@@ -292,23 +298,23 @@
     core1 = lax.ppermute(core1, "gy", pairs(count_y, 0))
     chip1 = lax.ppermute(chip1, "gy", pairs(count_y, 1))
     share = ((wide_rows, modes), F32)
-    smooth, inner, held = call(
+    smooth, inner = call(
         functools.partial(tile_kernel, reach),
-        [spatial_modes, y, core, chip, eh, el, along, mix],
-        [full, share, (spatial_modes.shape, BF16)],
-        [pltpu.SemaphoreType.DMA((4,))],
-        outside=1,
+        [y, core, chip, eh, el, along, mix, held],
+        [full, share],
     )
     both = [smooth, taps, bh, bl, eh, el, mix, held]
+    room = [pltpu.VMEM(slab, F32), pltpu.VMEM((reach, wide_rows, width_y), BF16)]
     (partial,) = call(
-        functools.partial(first_kernel, reach), [inner, r1, core1, chip1, *both], [share], [pltpu.VMEM(slab, F32)]
+        functools.partial(first_kernel, reach), [inner, r1, core1, chip1, *both], [share], room
     )
-    folds = 128 // owned
+    rows = channels * owned // 128
+    high = 4 if rows % 4 == 0 else rows
     (out,) = call(
         functools.partial(second_kernel, reach, owned),
         [partial, r2, *both],
-        [((count_x, count_y, channels // folds, 128), F32)],
-        [pltpu.VMEM(slab, F32)],
+        [((count_x, count_y, rows // high, high, 128), F32)],
+        room,
     )
     out = out.reshape((count_x * count_y,) + out.shape[2:])
     parts = lax.all_to_all(out, ("gx", "gy"), 0, 0, tiled=True)

time: 53.9 us -> 36.1 us (0.67); the launches traced: 53 us -> 35.9 us
  waiting for transfers between devices: 9.16 us -> 0.22 us
  local copies, waits for them, and re-layouts: 7.14 us -> 1.15 us
  starting transfers between devices: 12.3 us -> 9.91 us
  blocking collectives: 15.3 us -> 16.4 us
  Pallas kernels: 8.96 us -> 8.1 us
    ppermute x1, waiting for transfers between devices: 7.4 us -> 0.01 us  [local(): r1 = lax.ppermute(s1, 'gx', pairs(count_x, 0))]
    unnamed x16 -> x4, local copies, waits for them, and re-layouts: 7.14 us -> 1.15 us
    ppermute x1, starting transfers between devices: 4.36 us -> 2.1 us  [local(): r1 = lax.ppermute(s1, 'gx', pairs(count_x, 0))]
    ppermute x1, waiting for transfers between devices: 1.75 us -> 0.04 us  [local(): chip = lax.ppermute(chip, 'gy', pairs(count_y, 1))]
    ppermute x1, starting transfers between devices: 4.49 us -> 3.05 us  [local(): chip = lax.ppermute(chip, 'gy', pairs(count_y, 1))]
    all_to_all x1, blocking collectives: 15.3 us -> 16.4 us  [local(): parts = lax.all_to_all(out, ('gx', 'gy'), 0, 0, tiled=True)]
    ppermute x1, starting transfers between devices: 0.07 us -> 0.97 us  [local(): core = lax.ppermute(core, 'gy', pairs(count_y, 0))]
    pallas_call x9, Pallas kernels: 8.96 us -> 8.1 us  [call(): pl.pallas_call(body, out_shape=[make(shape, dtype) for shape, dtype in ou...]
  transfers between devices with their start and end apart: 6 -> 6, of which waited for: 2 -> 1; matrix products, arithmetic and copies ran while one was open for 0% -> 0% of each run, Pallas kernels for 10% -> 17%
where the time goes in v3:
time: 36.1 us; the launch traced here: 35.9 us
  blocking collectives  16.4 us (45%)
  starting transfers between devices  9.91 us (27%)
  Pallas kernels  8.1 us (22%)
  local copies, waits for them, and re-layouts  1.15 us (3%)
    all_to_all x1, blocking collectives, local(): parts = lax.all_to_all(out, ('gx', 'gy'), 0, 0, tiled=True)  16.4 us
    pallas_call x9, Pallas kernels, call(): pl.pallas_call(body, out_shape=[make(shape, dtype) for shape, dtype in ou...  8.1 us
    ppermute x1, starting transfers between devices, local(): chip1 = lax.ppermute(chip1, 'gy', pairs(count_y, 1))  3.06 us
    ppermute x1, starting transfers between devices, local(): chip = lax.ppermute(chip, 'gy', pairs(count_y, 1))  3.05 us
    ppermute x1, starting transfers between devices, local(): r1 = lax.ppermute(s1, 'gx', pairs(count_x, 0))  2.1 us
    unnamed x4, local copies, waits for them, and re-layouts  1.15 us
    ppermute x1, starting transfers between devices, local(): core = lax.ppermute(core, 'gy', pairs(count_y, 0))  0.97 us
  transfers between devices with their start and end apart: 6, of which 1 were waited for; matrix products, arithmetic and copies ran while one was open for 0% of the time, Pallas kernels for 17%

profile of v3, /device:TPU:1, one launch (start us, length us, event | category | flops | bytes accessed | tf_op | source)
XLA Modules:
  0.0 35.9 jit_solution(17123649879693966632)
XLA Ops:
  0.0 0.0 copy-start
  0.0 1.1 %copy-done = f32[4,6,32,256]{3,2,1,0:T(8,128)S(1)} copy-done((f32[4,6,32,256]{3,2,1,0:T(8,128)S(1)}, f32[4,6,32,256]{3,2,1,0:T(8,128)}, u32[]{:S(2)}) %copy-start) | copy-done | bytes 786456
  1.1 0.2 shard_map.73
  1.3 2.1 %collective-permute-start.2 = (f32[10,24,256]{2,1,0:T(8,128)S(1)}, f32[10,24,256]{2,1,0:T(8,128)S(1)}, u32[]{:S(2)}, u32[]{:S(2)}) collective-permute-start(f32[10,24,256]{2,1,0:T(8,128)S(1)} %get-tuple-element.32), channel_id=1, source_target_pairs={{0,4},{4,0},{8,12},{12,8},{16,20},{20,16},{24,28},{28,24},{1,5},{5... | collective-permute-start | bytes 737288 | tf_op jit(solution)/shard_map/ppermute | solution.py:263
  3.4 0.5 %shard_map.75 = (f32[12,768]{1,0:T(8,128)S(1)}, f32[12,768]{1,0:T(8,128)S(1)}) custom-call(f32[32,24,256]{2,1,0:T(8,128)S(1)} %get-tuple-element.22.t_ref), custom_call_target="tpu_custom_call" | custom-call | flops 1000000000 | bytes 1048576 | tf_op jit(solution)/shard_map/pallas_call | solution.py:236
  3.9 1.0 %collective-permute-start = (f32[12,768]{1,0:T(8,128)S(1)}, f32[12,768]{1,0:T(8,128)S(1)}, u32[]{:S(2)}, u32[]{:S(2)}) collective-permute-start(f32[12,768]{1,0:T(8,128)S(1)} %get-tuple-element.24), channel_id=1, source_target_pairs={{0,1},{1,0},{2,3},{3,2},{4,5},{5,4},{6,7},{7,6},{8,9},{9,8},{10,11... | collective-permute-start | bytes 110600 | tf_op jit(solution)/shard_map/ppermute | solution.py:266
  4.9 3.0 %collective-permute-start.1 = (f32[12,768]{1,0:T(8,128)S(1)}, f32[12,768]{1,0:T(8,128)S(1)}, u32[]{:S(2)}, u32[]{:S(2)}) collective-permute-start(f32[12,768]{1,0:T(8,128)S(1)} %get-tuple-element.25), channel_id=1, source_target_pairs={{1,2},{2,1},{5,6},{6,5},{9,10},{10,9},{13,14},{14,13},{17,18},{18,... | collective-permute-start | bytes 110600 | tf_op jit(solution)/shard_map/ppermute | solution.py:267
  7.9 2.3 %shard_map.74 = (f32[24,32,256]{2,1,0:T(8,128)S(1)}, bf16[256,256]{1,0:T(8,128)(2,1)S(1)}, bf16[256,256]{1,0:T(8,128)(2,1)S(1)}, bf16[32,256]{1,0:T(8,128)(2,1)S...) custom-call(f32[21]{0:T(128)} %east_hbm.1, ...), custom_call_target="tpu_custom_call" | custom-call | flops 1000000000 | bytes 1048576 | tf_op jit(solution)/shard_map/pallas_call | solution.py:236
  10.2 0.0 collective-permute-done.core_ref
  10.2 0.0 collective-permute-done.1.chip_ref
  10.3 0.1 shard_map.79
  10.4 0.7 %collective-permute-start.5 = (f32[11,24,256]{2,1,0:T(8,128)S(1)}, f32[11,24,256]{2,1,0:T(8,128)S(1)}, u32[]{:S(2)}, u32[]{:S(2)}) collective-permute-start(f32[11,24,256]{2,1,0:T(8,128)S(1)} %shard_map.79), channel_id=1, source_target_pairs={{4,8},{8,4},{12,16},{16,12},{20,24},{24,20},{5,9},{9,5},{13,17},{1... | collective-permute-start | bytes 811016 | tf_op jit(solution)/shard_map/ppermute | solution.py:295
  11.1 0.0 collective-permute-done.2.t_ref.r_ref
  11.1 0.2 shard_map.77
  11.3 0.1 collective-permute-start.3
  11.4 3.1 %collective-permute-start.4 = (f32[12,240]{1,0:T(8,128)S(1)}, f32[12,240]{1,0:T(8,128)S(1)}, u32[]{:S(2)}, u32[]{:S(2)}) collective-permute-start(f32[12,240]{1,0:T(8,128)S(1)} %get-tuple-element.34), channel_id=1, source_target_pairs={{1,2},{2,1},{5,6},{6,5},{9,10},{10,9},{13,14},{14,13},{17,18},{18,... | collective-permute-start | bytes 34568 | tf_op jit(solution)/shard_map/ppermute | solution.py:299
  14.4 1.8 %shard_map.76 = (f32[32,24,256]{2,1,0:T(8,128)S(1)}, f32[32,256]{1,0:T(8,128)S(1)}) custom-call(f32[24,32,256]{2,1,0:T(8,128)S(1)} %get-tuple-element.23.y_ref, f32[12,768]{1,0:T(8,128)S(1)} %collective-permute-done.core_ref, f32[12,768]{1,0:T(8,128)S(1)} %collective-permute-done.1.chip_ref, bf16[32,256]{1,0:T(8,128)(2,1)S(1)} %get-tuple-element.26.eh_ref.rest_3_, ...), custom_call_target="tpu_custom_call" | custom-call | flops 1000000000 | bytes 1048576 | tf_op jit(solution)/shard_map/pallas_call | solution.py:236
  16.2 0.0 collective-permute-done.3.core_ref
  16.3 0.2 collective-permute-done.4.chip_ref
  16.4 1.1 %shard_map.78.p_ref = f32[32,256]{1,0:T(8,128)S(1)} custom-call(f32[32,256]{1,0:T(8,128)S(1)} %get-tuple-element.31.p_ref, f32[10,24,256]{2,1,0:T(8,128)S(1)} %collective-permute-done.2.t_ref.r_ref, f32[12,240]{1,0:T(8,128)S(1)} %collective-permute-done.3.core_ref, f32[12,240]{1,0:T(8,128)S(1)} %collective-permute-done.4.chip_ref, ...), custom_call_target="tpu_custom_call" | custom-call | flops 1000000000 | bytes 1048576 | tf_op jit(solution)/shard_map/pallas_call | solution.py:236
  17.5 0.0 copy-start.1
  17.5 0.0 collective-permute-done.5.r_ref
  17.6 1.2 %shard_map.80 = f32[8,4,3,4,128]{4,3,2,1,0:T(4,128)S(1)} custom-call(f32[32,256]{1,0:T(8,128)S(1)} %shard_map.78.p_ref, f32[11,24,256]{2,1,0:T(8,128)S(1)} %collective-permute-done.5.r_ref, f32[32,24,256]{2,1,0:T(8,128)S(1)} %get-tuple-element.35.s_ref, f32[21,8,256]{2,1,0:T(8,128)S(1)} %get-tuple-element.36.rest_0_, ...), custom_call_target="tpu_custom_call" | custom-call | flops 1000000000 | bytes 1048576 | tf_op jit(solution)/shard_map/pallas_call | solution.py:236
  18.8 16.4 %all_to_all.5.parts_ref = f32[32,3,4,128]{3,2,1,0:T(4,128)S(1)} all-to-all(f32[32,3,4,128]{3,2,1,0:T(4,128)S(1)} %bitcast.4), channel_id=1, replica_groups=mesh['gx'=8,'gy'=4] {'gx','gy'}, dimensions={0} | all-to-all | bytes 393216 | tf_op jit(solution)/shard_map/all_to_all | solution.py:320
  35.2 0.0 copy-done.1
  35.2 0.7 %shard_map.81 = f32[24,64]{1,0:T(8,128)} custom-call(f32[32,3,4,128]{3,2,1,0:T(4,128)S(1)} %all_to_all.5.parts_ref, f32[24,64]{1,0:T(8,128)S(1)} %bitcast.6), custom_call_target="tpu_custom_call" | custom-call | flops 1000000000 | bytes 1048576 | tf_op jit(solution)/shard_map/pallas_call | solution.py:236
Async XLA Ops:
  0.0 1.1 %copy-start = (f32[4,6,32,256]{3,2,1,0:T(8,128)S(1)}, f32[4,6,32,256]{3,2,1,0:T(8,128)}, u32[]{:S(2)}) copy-start(f32[4,6,32,256]{3,2,1,0:T(8,128)} %param.7) | copy-start | bytes 2359300
  1.3 9.8 %collective-permute-start.2 = (f32[10,24,256]{2,1,0:T(8,128)S(1)}, f32[10,24,256]{2,1,0:T(8,128)S(1)}, u32[]{:S(2)}, u32[]{:S(2)}) collective-permute-start(f32[10,24,256]{2,1,0:T(8,128)S(1)} %get-tuple-element.32), channel_id=1, source_target_pairs={{0,4},{4,0},{8,12},{12,8},{16,20},{20,16},{24,28},{28,24},{1,5},{5... | collective-permute-start | bytes 737288 | tf_op jit(solution)/shard_map/ppermute | solution.py:263
  3.9 6.3 %collective-permute-start = (f32[12,768]{1,0:T(8,128)S(1)}, f32[12,768]{1,0:T(8,128)S(1)}, u32[]{:S(2)}, u32[]{:S(2)}) collective-permute-start(f32[12,768]{1,0:T(8,128)S(1)} %get-tuple-element.24), channel_id=1, source_target_pairs={{0,1},{1,0},{2,3},{3,2},{4,5},{5,4},{6,7},{7,6},{8,9},{9,8},{10,11... | collective-permute-start | bytes 110600 | tf_op jit(solution)/shard_map/ppermute | solution.py:266
  4.9 5.4 %collective-permute-start.1 = (f32[12,768]{1,0:T(8,128)S(1)}, f32[12,768]{1,0:T(8,128)S(1)}, u32[]{:S(2)}, u32[]{:S(2)}) collective-permute-start(f32[12,768]{1,0:T(8,128)S(1)} %get-tuple-element.25), channel_id=1, source_target_pairs={{1,2},{2,1},{5,6},{6,5},{9,10},{10,9},{13,14},{14,13},{17,18},{18,... | collective-permute-start | bytes 110600 | tf_op jit(solution)/shard_map/ppermute | solution.py:267
  10.4 7.2 %collective-permute-start.5 = (f32[11,24,256]{2,1,0:T(8,128)S(1)}, f32[11,24,256]{2,1,0:T(8,128)S(1)}, u32[]{:S(2)}, u32[]{:S(2)}) collective-permute-start(f32[11,24,256]{2,1,0:T(8,128)S(1)} %shard_map.79), channel_id=1, source_target_pairs={{4,8},{8,4},{12,16},{16,12},{20,24},{24,20},{5,9},{9,5},{13,17},{1... | collective-permute-start | bytes 811016 | tf_op jit(solution)/shard_map/ppermute | solution.py:295
  11.3 5.0 %collective-permute-start.3 = (f32[12,240]{1,0:T(8,128)S(1)}, f32[12,240]{1,0:T(8,128)S(1)}, u32[]{:S(2)}, u32[]{:S(2)}) collective-permute-start(f32[12,240]{1,0:T(8,128)S(1)} %get-tuple-element.33), channel_id=1, source_target_pairs={{0,1},{1,0},{2,3},{3,2},{4,5},{5,4},{6,7},{7,6},{8,9},{9,8},{10,11... | collective-permute-start | bytes 34568 | tf_op jit(solution)/shard_map/ppermute | solution.py:298
  11.4 5.1 %collective-permute-start.4 = (f32[12,240]{1,0:T(8,128)S(1)}, f32[12,240]{1,0:T(8,128)S(1)}, u32[]{:S(2)}, u32[]{:S(2)}) collective-permute-start(f32[12,240]{1,0:T(8,128)S(1)} %get-tuple-element.34), channel_id=1, source_target_pairs={{1,2},{2,1},{5,6},{6,5},{9,10},{10,9},{13,14},{14,13},{17,18},{18,... | collective-permute-start | bytes 34568 | tf_op jit(solution)/shard_map/ppermute | solution.py:299
  17.5 17.7 %copy-start.1 = (f32[64,24]{0,1:T(8,128)S(1)}, f32[64,24]{0,1:T(8,128)}, u32[]{:S(2)}) copy-start(f32[64,24]{0,1:T(8,128)} %param.13) | copy-start | bytes 18436

commit v4 on v3

v4 whole, which is shorter than its diff:
```python
import functools

import jax
import jax.numpy as jnp
from jax import lax
from jax.experimental import pallas as pl
from jax.experimental.pallas import tpu as pltpu
from jax.sharding import PartitionSpec as P

F32, BF16 = jnp.float32, jnp.bfloat16
NN = (((1,), (0,)), ((), ()))
NT = (((1,), (1,)), ((), ()))
TN = (((0,), (0,)), ((), ()))
STRIP = 12
ROWS = 4
EDGE = 32
LANES = 128
PITCH = 16


def dot(a, b, dims=NN):
    return lax.dot_general(a, b, dims, preferred_element_type=F32)


def halves(v):
    high = v.astype(BF16)
    return high, (v - high.astype(F32)).astype(BF16)


def dot2(a, b, dims=NN):
    (ah, al), (bh, bl) = a, b
    return dot(ah, bh, dims) + dot(ah, bl, dims) + dot(al, bh, dims)


def iota(shape, dim):
    return lax.broadcasted_iota(jnp.int32, shape, dim)


def stacked(v):
    high = v.astype(BF16).astype(F32)
    parts = [high, v - high, high]
    if (3 * v.shape[0]) % 16:
        parts.append(jnp.zeros((-3 * v.shape[0] % 96, v.shape[1]), F32))
    return jnp.concatenate(parts, axis=0).astype(BF16)


def wide(m):
    high = m.astype(BF16).astype(F32)
    parts = [high, high, m - high]
    if (3 * m.shape[1]) % 16:
        parts.append(jnp.zeros((m.shape[0], -3 * m.shape[1] % 96), F32))
    return jnp.concatenate(parts, axis=1).astype(BF16)


def turn_kernel(reach, a_ref, t_ref, s1_ref):
    t_ref[...] = jnp.swapaxes(a_ref[...], 0, 1)
    odd = lax.axis_index("gx") % 2
    s1_ref[...] = t_ref[pl.ds((1 - odd) * (t_ref.shape[0] - reach), reach)]


def strip_kernel(reach, t_ref, core_ref, chip_ref):
    width_x, channels, width_y = t_ref.shape
    odd = lax.axis_index("gy") % 2
    row, col = iota((EDGE, width_y), 0), iota((EDGE, width_y), 1)
    to_core = row < STRIP
    at = jnp.where(to_core, row, row - STRIP)
    low = jnp.where(to_core, odd, 1 - odd) == 1
    wanted = at + jnp.where(low, 0, width_y - reach)
    pick = jnp.where((col == wanted) & (at < reach), 1.0, 0.0).astype(BF16)
    data = t_ref[...].reshape(width_x * channels, width_y)
    high, rest = halves(data)
    strips = dot(pick, high, NT) + dot(pick, rest, NT)
    for j in range(STRIP // ROWS):
        core_ref[j] = strips[j * ROWS : (j + 1) * ROWS]
        chip_ref[j] = strips[STRIP + j * ROWS : STRIP + (j + 1) * ROWS]


def band_kernel(reach, north_ref, t_ref, y_ref, bh_ref, bl_ref, eh_ref, el_ref, e_ref):
    width_x, channels, width_y = t_ref.shape
    span = 2 * reach + 1
    odd = lax.axis_index("gy") % 2
    shift = iota((width_y, width_y), 0) - iota((width_y, width_y), 1) + reach
    row = iota((EDGE, width_y), 0)
    edge_shifts = []
    for pitch in (STRIP, PITCH):
        from_core = row < pitch
        at = jnp.where(from_core, row, row - pitch)
        left = jnp.where(from_core, odd, 1 - odd) == 1
        source = jnp.where(left, at - reach, width_y + at)
        edge_shifts.append(jnp.where(at < reach, source - iota((EDGE, width_y), 1) + reach, -1))
    first = iota((8, width_y), 1)
    base = jnp.zeros((8, width_y), F32)
    edge = jnp.zeros((EDGE, width_y), F32)
    spread = edge
    for j in range(span):
        tap = north_ref[:, j : j + 1]
        base = jnp.where(first == (reach - j) % width_y, tap, base)
        edge = jnp.where(edge_shifts[0] == j, tap, edge)
        spread = jnp.where(edge_shifts[1] == j, tap, spread)
    e_ref[...] = spread
    rolled = pltpu.roll(jnp.broadcast_to(base[:1], (width_y, width_y)), 0, 1, stride=1, stride_axis=0)
    band = halves(jnp.where((shift >= 0) & (shift < span), rolled, 0.0))
    bh_ref[...], bl_ref[...] = band
    eh_ref[...], el_ref[...] = halves(edge)
    y_ref[...] = dot2(halves(t_ref[...].reshape(width_x * channels, width_y)), band).reshape(t_ref.shape)


def own_kernel(reach, east_ref, field_ref, time_ref, y_ref, s_ref, x_ref, mix_ref, taps_ref):
    width_x, channels, width_y = y_ref.shape
    x_shift = iota((width_x, width_x), 1) - iota((width_x, width_x), 0) + reach
    along = jnp.zeros((width_x, width_x), F32)
    for j in range(2 * reach + 1):
        tap = east_ref[:, j : j + 1]
        along = jnp.where(x_shift == j, tap, along)
        taps_ref[j] = jnp.broadcast_to(tap, taps_ref.shape[1:])
    along = wide(along)
    x_ref[...] = along
    s_ref[...] = along_x(along, y_ref[...])
    fields, levels = field_ref.shape[0], time_ref.shape[0]
    rows = mix_ref.shape[0]
    out, into = iota((rows, channels), 0), iota((rows, channels), 1)
    by_field = jnp.zeros((rows, channels), F32)
    by_time = jnp.zeros((rows, channels), F32)
    for g in range(fields):
        for f in range(fields):
            here = (into // levels == g) & (out // levels == f)
            by_field = jnp.where(here, field_ref[g : g + 1, f : f + 1], by_field)
    for s in range(levels):
        for t in range(levels):
            here = (into % levels == s) & (out % levels == t)
            by_time = jnp.where(here, time_ref[s : s + 1, t : t + 1], by_time)
    mix_ref[...] = wide(by_field * by_time)


def outer_kernel(reach, r_ref, core_ref, chip_ref):
    _, channels, width_y = r_ref.shape
    lane = iota((channels, LANES), 1)
    low = [jnp.zeros((channels, LANES), F32) for _ in range(core_ref.shape[1] // LANES)]
    high = list(low)
    for n in range(reach):
        tile, at = divmod(PITCH * n, LANES)
        first = jnp.where(lane < reach, r_ref[n, :, :LANES], 0.0)
        last = jnp.where(lane >= LANES - reach, r_ref[n, :, width_y - LANES :], 0.0)
        low[tile] += pltpu.roll(first, at, 1) if at else first
        high[tile] += pltpu.roll(last, at + reach, 1)
    odd = lax.axis_index("gy") % 2
    for tile, (a, b) in enumerate(zip(low, high)):
        lanes = slice(tile * LANES, (tile + 1) * LANES)
        core_ref[:, lanes] = jnp.where(odd == 1, a, b)
        chip_ref[:, lanes] = jnp.where(odd == 1, b, a)


def corner_modes_kernel(reach, e_ref, taps_ref, modes_ref, ch_ref, cl_ref, nh_ref, nl_ref, g_ref, h_ref):
    width_x, width_y, modes = modes_ref.shape
    left = lax.axis_index("gx") % 2
    both = jnp.concatenate(halves(e_ref[...]), axis=0)
    half = e_ref.shape[0]
    for m in range(reach):
        g = dot(both, modes_ref[place(reach, left, width_x, m)])
        g_ref[m] = g[:half] + g[half:]
    for n in range(reach):
        value = None
        for m in range(n, reach):
            d = m - n
            tap = taps_ref[left * d + (1 - left) * (2 * reach - d)][None]
            term = tap * g_ref[m].reshape(half // 8, 8, modes)
            value = term if value is None else value + term
        value = value.reshape(half, modes)
        i = left * (reach - 1 - n) + (1 - left) * n
        for side in range(2):
            h_ref[side, i] = value[side * PITCH : (side + 1) * PITCH]
    for side, (high_ref, low_ref) in enumerate(((ch_ref, cl_ref), (nh_ref, nl_ref))):
        high_ref[...], low_ref[...] = halves(h_ref[side].reshape(reach * PITCH, modes))


def joined(core, chip):
    pieces = [piece[j] for piece in (core, chip) for j in range(STRIP // ROWS)]
    return jnp.concatenate(pieces + [jnp.zeros((EDGE - 2 * STRIP, core.shape[2]), F32)], axis=0)


def corner_kernel(reach, y_ref, core_ref, chip_ref, eh_ref, el_ref, before_ref, s2_ref):
    del before_ref
    width_x, channels, width_y = y_ref.shape
    odd = lax.axis_index("gx") % 2
    strips = joined(core_ref[...], chip_ref[...])
    top = strips[:, : reach * channels]
    bottom = strips[:, (width_x - reach) * channels :]
    more = dot2(halves(jnp.where(odd == 1, bottom, top)), (eh_ref[...], el_ref[...]), TN)
    s2_ref[...] = y_ref[pl.ds(odd * (width_x - reach), reach)] + more.reshape(s2_ref.shape)


def along_x(matrix, y):
    by_channel = jnp.swapaxes(y, 0, 1)
    return jnp.swapaxes(jnp.stack([dot(matrix, stacked(by_channel[c])) for c in range(y.shape[1])]), 0, 1)


def tile_kernel(
    reach, own_ref, core_ref, chip_ref, next_ref, eh_ref, el_ref, x_ref, mix_ref, modes_ref, s_ref, p_ref
):
    del next_ref
    width_x, channels, width_y = own_ref.shape
    edge = tuple(ref[:, :LANES] + ref[:, width_y - LANES :] for ref in (eh_ref, el_ref))
    more = dot2(halves(joined(core_ref[...], chip_ref[...])), edge, TN).reshape(width_x, channels, LANES)
    more = along_x(x_ref[...], more)
    left = iota((1, 1, LANES), 2) < LANES // 2
    s_ref[...] = own_ref[...]
    s_ref[:, :, :LANES] += jnp.where(left, more, 0.0)
    s_ref[:, :, width_y - LANES :] += jnp.where(left, 0.0, more)
    mix = mix_ref[...]
    inner = [dot(mix, stacked(s_ref[x])).astype(BF16) for x in range(reach, width_x - reach)]
    acc = dot(inner[0], modes_ref[reach])
    for x in range(1, width_x - 2 * reach):
        acc = acc + dot(inner[x], modes_ref[reach + x])
    p_ref[...] = acc


def place(reach, left, width_x, m):
    return left * (reach - 1 - m) + (1 - left) * (width_x - reach + m)


def added(reach, left, rows, taps_ref, m, count, lanes):
    value = None
    for n in range(m + 1):
        d = m - n
        tap = taps_ref[left * d + (1 - left) * (2 * reach - d), :, :lanes][None]
        term = tap * rows[left * (reach - 1 - n) + (1 - left) * n].reshape(count // 8, 8, lanes)
        value = term if value is None else value + term
    return value.reshape(count, lanes)


def rows_kernel(reach, p_ref, r_ref, bh_ref, bl_ref, s_ref, taps_ref, mix_ref, modes_ref, out_ref, by, mixed):
    left = lax.axis_index("gx") % 2
    rows = dot2(halves(r_ref[...].reshape(-1, r_ref.shape[2])), (bh_ref[...], bl_ref[...]))
    by[...] = rows.reshape(r_ref.shape)
    out_ref[...] = p_ref[...] + side(reach, left, by, s_ref, taps_ref, mix_ref, modes_ref, mixed)


def side(reach, left, rows, s_ref, taps_ref, mix_ref, modes_ref, mixed):
    width_x, channels, width_y = s_ref.shape
    mix = mix_ref[...]
    for m in range(reach):
        value = s_ref[place(reach, left, width_x, m)] + added(reach, left, rows, taps_ref, m, channels, width_y)
        mixed[m] = dot(mix, stacked(value)).astype(BF16)
    total = None
    for m in range(reach):
        term = dot(mixed[m], modes_ref[place(reach, left, width_x, m)])
        total = term if total is None else total + term
    return total


def last_kernel(
    reach, p_ref, r_ref, core_ref, chip_ref, ch_ref, cl_ref, nh_ref, nl_ref, s_ref, taps_ref, mix_ref, modes_ref, out_ref, mixed
):
    odd = lax.axis_index("gx") % 2
    width = ch_ref.shape[0]
    corners = dot2(halves(core_ref[:, :width]), (ch_ref[...], cl_ref[...]))
    corners = corners + dot2(halves(chip_ref[:, :width]), (nh_ref[...], nl_ref[...]))
    total = p_ref[...] + dot(mix_ref[...], stacked(corners))
    total = total + side(reach, 1 - odd, r_ref, s_ref, taps_ref, mix_ref, modes_ref, mixed)
    deliver(total, s_ref.shape[1], out_ref)


def deliver(total, channels, out_ref):
    if len(out_ref.shape) == 2:
        out_ref[...] = total
        return
    _, parts, count, high, lanes = out_ref.shape
    owned = total.shape[1] // parts
    rows = count * high
    for g in range(parts):
        piece = jnp.concatenate(
            [total[k * rows : (k + 1) * rows, g * owned : (g + 1) * owned] for k in range(lanes // owned)], axis=1
        )
        for k in range(out_ref.shape[0]):
            for j in range(count):
                out_ref[k, g, j] = piece[j * high : (j + 1) * high]


def sum_kernel(parts_ref, coefficients_ref, out_ref):
    channels, owned = out_ref.shape
    _, count, high, lanes = parts_ref.shape
    total = jnp.sum(parts_ref[...], axis=0)
    for k in range(lanes // owned):
        for j in range(count):
            rows = pl.ds((k * count + j) * high, high)
            out_ref[rows] = coefficients_ref[rows] + total[j, :, k * owned : (k + 1) * owned]


def vmem(array):
    return pltpu.with_memory_space_constraint(array, pltpu.VMEM)


def call(body, ins, outs, scratch=(), keep=True, weight=1e9):
    args = [vmem(item) for item in ins]
    specs = [pl.BlockSpec(memory_space=pltpu.VMEM)] * len(ins)
    make = pltpu.VMEM if keep else jax.ShapeDtypeStruct
    return pl.pallas_call(
        body,
        out_shape=[make(shape, dtype) for shape, dtype in outs],
        in_specs=specs,
        out_specs=[pl.BlockSpec(memory_space=pltpu.VMEM)] * len(outs),
        scratch_shapes=list(scratch),
        compiler_params=pltpu.CompilerParams(vmem_limit_bytes=24 << 20),
        cost_estimate=pl.CostEstimate(flops=int(weight), bytes_accessed=1 << 20, transcendentals=0),
    )(*args)


def pairs(count, first):
    found = []
    for low in range(first, count - 1, 2):
        found += [(low, low + 1), (low + 1, low)]
    return found


def local(adjoint_forcing, field_mixing, time_mixing, kernel_east, kernel_north, spatial_modes, coefficients):
    fields, levels, width_x, width_y = adjoint_forcing.shape
    channels, modes, owned = fields * levels, spatial_modes.shape[2], coefficients.shape[0]
    reach = (kernel_east.shape[0] - 1) // 2
    count_x, count_y = lax.axis_size("gx"), lax.axis_size("gy")
    raw = adjoint_forcing.reshape(channels, width_x, width_y)
    slab = (reach, channels, width_y)
    full = ((width_x, channels, width_y), F32)
    t, s1 = call(functools.partial(turn_kernel, reach), [raw], [full, (slab, F32)])
    r1 = lax.ppermute(s1, "gx", pairs(count_x, 0))
    strip = ((STRIP // ROWS, ROWS, width_x * channels), F32)
    core, chip = call(functools.partial(strip_kernel, reach), [t], [strip, strip], weight=1e9)
    core = lax.ppermute(core, "gy", pairs(count_y, 0))
    chip = lax.ppermute(chip, "gy", pairs(count_y, 1))
    edge = ((EDGE, width_y), BF16)
    band = ((width_y, width_y), BF16)
    wide_rows = -(-channels // 16) * 16
    y, bh, bl, eh, el, spread = call(
        functools.partial(band_kernel, reach), [kernel_north.reshape(1, -1), t], [full, band, band, edge, edge, ((EDGE, width_y), F32)], weight=1e9)
    own, along, mix, taps = call(
        functools.partial(own_kernel, reach),
        [kernel_east.reshape(1, -1), field_mixing, time_mixing, y],
        [
            full,
            ((width_x, 3 * width_x + -3 * width_x % 96), BF16),
            ((wide_rows, 3 * channels + -3 * channels % 96), BF16),
            ((2 * reach + 1, 8, width_y), F32),
        ], weight=1e9)
    held = vmem(spatial_modes)
    corner = ((reach * PITCH, modes), BF16)
    corner_modes = call(
        functools.partial(corner_modes_kernel, reach),
        [spread, taps, held],
        [corner] * 4,
        [pltpu.VMEM((reach, EDGE, modes), F32), pltpu.VMEM((2, reach, PITCH, modes), F32)],
        weight=1e7,
    )
    (s2,) = call(functools.partial(corner_kernel, reach), [y, core, chip, eh, el, corner_modes[0]], [(slab, F32)], weight=1e7)
    r2 = lax.ppermute(s2, "gx", pairs(count_x, 1))
    strip = ((channels, -(-reach * PITCH // LANES) * LANES), F32)
    core1, chip1 = call(functools.partial(outer_kernel, reach), [r1], [strip, strip], weight=3e8)
    core2 = lax.ppermute(core1, "gy", pairs(count_y, 0))
    chip2 = lax.ppermute(chip1, "gy", pairs(count_y, 1))
    share = ((wide_rows, modes), F32)
    smooth, inner = call(
        functools.partial(tile_kernel, reach),
        [own, core, chip, core1, eh, el, along, mix, held],
        [full, share], weight=1e8)
    both = [smooth, taps, mix, held]
    mixed = pltpu.VMEM((reach, wide_rows, width_y), BF16)
    (partial,) = call(
        functools.partial(rows_kernel, reach),
        [inner, r1, bh, bl, *both],
        [share],
        [pltpu.VMEM(slab, F32), mixed],
        weight=3e8,
    )
    rows = channels * owned // 128
    high = 4 if rows % 4 == 0 else rows
    (out,) = call(
        functools.partial(last_kernel, reach),
        [partial, r2, core2, chip2, *corner_modes, *both],
        [((count_x, count_y, rows // high, high, 128), F32)],
        [mixed],
    )
    out = out.reshape((count_x * count_y,) + out.shape[2:])
    parts = lax.all_to_all(out, ("gx", "gy"), 0, 0, tiled=True)
    (gradient,) = call(sum_kernel, [parts, coefficients.T], [((channels, owned), F32)], keep=False)
    return gradient.T


def solution(mesh):
    in_specs = (P(None, None, "gx", "gy"), P(), P(), P(), P(), P("gx", "gy", None), P("gy", None))
    out_specs = P("gy", None)
    return jax.shard_map(local, mesh=mesh, in_specs=in_specs, out_specs=out_specs, check_vma=False)
```

time: 36.1 us -> 34.3 us (0.950)
  blocking collectives: 16.4 us -> 14.4 us
  Pallas kernels: 8.1 us -> 6.75 us
  starting transfers between devices: 9.91 us -> 10.7 us
  waiting for transfers between devices: 0.22 us -> 0.86 us
    all_to_all x1, blocking collectives: 16.4 us -> 14.4 us  [local(): parts = lax.all_to_all(out, ('gx', 'gy'), 0, 0, tiled=True)]
    ppermute x1, starting transfers between devices: 3.05 us -> 4.76 us  [local(): chip = lax.ppermute(chip, 'gy', pairs(count_y, 1))]
    pallas_call x9 -> x11, Pallas kernels: 8.1 us -> 6.75 us  [call(): pl.pallas_call(body, out_shape=[make(shape, dtype) for shape, dtype in ou...]
    ppermute x1, starting transfers between devices: 0.97 us -> 0.12 us  [local(): core = lax.ppermute(core, 'gy', pairs(count_y, 0))]
    ppermute x1, waiting for transfers between devices: 0.01 us -> 0.85 us  [local(): r1 = lax.ppermute(s1, 'gx', pairs(count_x, 0))]
    ppermute x1, starting transfers between devices: 2.1 us -> 1.27 us  [local(): r1 = lax.ppermute(s1, 'gx', pairs(count_x, 0))]
    ppermute x2, starting transfers between devices: 3.13 us -> 3.84 us  [the longest x1 3.77 us: local(): chip2 = lax.ppermute(chip1, 'gy', pairs(count_y, 1))]
    unnamed x4 -> x14, local copies, waits for them, and re-layouts: 1.15 us -> 1.18 us
  transfers between devices with their start and end apart: 6 -> 6, of which waited for: 1 -> 1; matrix products, arithmetic and copies ran while one was open for 0% -> 0% of each run, Pallas kernels for 17% -> 14%
where the time goes in v4:
time: 34.3 us; the launch traced here: 34.1 us
  blocking collectives  14.4 us (42%)
  starting transfers between devices  10.7 us (31%)
  Pallas kernels  6.75 us (20%)
  local copies, waits for them, and re-layouts  1.18 us (3%)
  waiting for transfers between devices  0.86 us (3%)
    all_to_all x1, blocking collectives, local(): parts = lax.all_to_all(out, ('gx', 'gy'), 0, 0, tiled=True)  14.4 us
    pallas_call x11, Pallas kernels, call(): pl.pallas_call(body, out_shape=[make(shape, dtype) for shape, dtype in ou...  6.75 us
    ppermute x1, starting transfers between devices, local(): chip = lax.ppermute(chip, 'gy', pairs(count_y, 1))  4.76 us
    ppermute x1, starting transfers between devices, local(): chip2 = lax.ppermute(chip1, 'gy', pairs(count_y, 1))  3.77 us
    ppermute x1, starting transfers between devices, local(): r1 = lax.ppermute(s1, 'gx', pairs(count_x, 0))  1.27 us
    unnamed x14, local copies, waits for them, and re-layouts  1.18 us
    ppermute x1, waiting for transfers between devices, local(): r1 = lax.ppermute(s1, 'gx', pairs(count_x, 0))  0.85 us
  transfers between devices with their start and end apart: 6, of which 1 were waited for; matrix products, arithmetic and copies ran while one was open for 0% of the time, Pallas kernels for 14%

profile of v4, /device:TPU:1, one launch (start us, length us, event | category | flops | bytes accessed | tf_op | source)
XLA Modules:
  0.0 34.1 jit_solution(16092778012166125848)
XLA Ops:
  0.0 0.0 copy-start.5
  0.0 0.0 copy-start.1
  0.0 1.1 %copy-done.1 = f32[4,6,32,256]{3,2,1,0:T(8,128)S(1)} copy-done((f32[4,6,32,256]{3,2,1,0:T(8,128)S(1)}, f32[4,6,32,256]{3,2,1,0:T(8,128)}, u32[]{:S(2)}) %copy-start.1) | copy-done | bytes 786456
  1.1 0.2 shard_map.73
  1.3 0.0 copy-start.3
  1.3 0.0 copy-start.4
  1.3 0.0 copy-start.6
  1.4 0.3 shard_map.76
  1.7 0.0 copy-start
  1.7 0.1 collective-permute-start
  1.8 4.8 %collective-permute-start.1 = (f32[3,4,768]{2,1,0:T(4,128)S(1)}, f32[3,4,768]{2,1,0:T(4,128)S(1)}, u32[]{:S(2)}, u32[]{:S(2)}) collective-permute-start(f32[3,4,768]{2,1,0:T(4,128)S(1)} %get-tuple-element.31), channel_id=1, source_target_pairs={{1,2},{2,1},{5,6},{6,5},{9,10},{10,9},{13,14},{14,13},{17,18},{18,... | collective-permute-start | bytes 110600 | tf_op jit(solution)/shard_map/ppermute | solution.py:328
  6.6 1.3 %collective-permute-start.2 = (f32[10,24,256]{2,1,0:T(8,128)S(1)}, f32[10,24,256]{2,1,0:T(8,128)S(1)}, u32[]{:S(2)}, u32[]{:S(2)}) collective-permute-start(f32[10,24,256]{2,1,0:T(8,128)S(1)} %get-tuple-element.32), channel_id=1, source_target_pairs={{0,4},{4,0},{8,12},{12,8},{16,20},{20,16},{24,28},{28,24},{1,5},{5... | collective-permute-start | bytes 737288 | tf_op jit(solution)/shard_map/ppermute | solution.py:324
  7.9 0.0 copy-done.5
  7.9 0.7 %shard_map.74 = (f32[32,24,256]{2,1,0:T(8,128)S(1)}, bf16[256,256]{1,0:T(8,128)(2,1)S(1)}, bf16[256,256]{1,0:T(8,128)(2,1)S(1)}, bf16[32,256]{1,0:T(8,128)(2,1)S...) custom-call(f32[1,21]{1,0:T(1,128)S(1)} %bitcast.9, f32[32,24,256]{2,1,0:T(8,128)S(1)} %get-tuple-element.27.t_ref), custom_call_target="tpu_custom_call" | custom-call | flops 1000000000 | bytes 1048576 | tf_op jit(solution)/shard_map/pallas_call | solution.py:297
  8.6 0.0 copy-done.3
  8.6 0.0 copy-done.4
  8.6 0.0 copy-done.6
  8.6 0.7 %shard_map.75 = (f32[32,24,256]{2,1,0:T(8,128)S(1)}, bf16[32,96]{1,0:T(8,128)(2,1)S(1)}, bf16[32,96]{1,0:T(8,128)(2,1)S(1)}, f32[21,8,256]{2,1,0:T(8,128)S(1)}) custom-call(f32[1,21]{1,0:T(1,128)S(1)} %bitcast.10, f32[4,4]{1,0:T(4,128)S(1)} %copy-done.4, f32[6,6]{1,0:T(8,128)S(1)} %copy-done.3, f32[32,24,256]{2,1,0:T(8,128)S(1)} %get-tuple-element.28.y_ref), custom_call_target="tpu_custom_call" | custom-call | flops 1000000000 | bytes 1048576 | tf_op jit(solution)/shard_map/pallas_call | solution.py:297
  9.3 0.0 copy-done
  9.3 0.5 %shard_map.80 = (bf16[160,256]{1,0:T(8,128)(2,1)S(1)}, bf16[160,256]{1,0:T(8,128)(2,1)S(1)}, bf16[160,256]{1,0:T(8,128)(2,1)S(1)}, bf16[160,256]{1,0:T(8,128)(2,1)S(1)}) custom-call(f32[32,256]{1,0:T(8,128)S(1)} %get-tuple-element.43.e_ref, f32[21,8,256]{2,1,0:T(8,128)S(1)} %get-tuple-element.42.taps_ref, bf16[32,256,256]{2,1,0:T(8,128)(2,1)S(1)} %copy-done), custom_call_target="tpu_custom_call" | custom-call | flops 10000000 | bytes 1048576 | tf_op jit(solution)/shard_map/pallas_call | solution.py:297
  9.8 0.0 collective-permute-done.core_ref
  9.8 0.0 collective-permute-done.1.chip_ref
  9.8 0.4 %shard_map.81 = f32[10,24,256]{2,1,0:T(8,128)S(1)} custom-call(f32[32,24,256]{2,1,0:T(8,128)S(1)} %get-tuple-element.28.y_ref, f32[3,4,768]{2,1,0:T(4,128)S(1)} %collective-permute-done.core_ref, f32[3,4,768]{2,1,0:T(4,128)S(1)} %collective-permute-done.1.chip_ref, bf16[32,256]{1,0:T(8,128)(2,1)S(1)} %get-tuple-element.34.eh_ref, ...), custom_call_target="tpu_custom_call" | custom-call | flops 10000000 | bytes 1048576 | tf_op jit(solution)/shard_map/pallas_call | solution.py:297
  10.2 0.7 %collective-permute-start.3 = (f32[10,24,256]{2,1,0:T(8,128)S(1)}, f32[10,24,256]{2,1,0:T(8,128)S(1)}, u32[]{:S(2)}, u32[]{:S(2)}) collective-permute-start(f32[10,24,256]{2,1,0:T(8,128)S(1)} %shard_map.81), channel_id=1, source_target_pairs={{4,8},{8,4},{12,16},{16,12},{20,24},{24,20},{5,9},{9,5},{13,17},{1... | collective-permute-start | bytes 737288 | tf_op jit(solution)/shard_map/ppermute | solution.py:353
  10.9 0.8 %collective-permute-done.2.r_ref = f32[10,24,256]{2,1,0:T(8,128)S(1)} collective-permute-done((f32[10,24,256]{2,1,0:T(8,128)S(1)}, f32[10,24,256]{2,1,0:T(8,128)S(1)}, u32[]{:S(2)}, u32[]{:S(2)}) %collective-permute-start.2) | collective-permute-done | bytes 245792 | tf_op jit(solution)/shard_map/ppermute | solution.py:324
  11.8 0.1 shard_map.77
  11.9 0.1 collective-permute-start.4
  12.0 3.8 %collective-permute-start.5 = (f32[24,256]{1,0:T(8,128)S(1)}, f32[24,256]{1,0:T(8,128)S(1)}, u32[]{:S(2)}, u32[]{:S(2)}) collective-permute-start(f32[24,256]{1,0:T(8,128)S(1)} %get-tuple-element.45), channel_id=1, source_target_pairs={{1,2},{2,1},{5,6},{6,5},{9,10},{10,9},{13,14},{14,13},{17,18},{18,... | collective-permute-start | bytes 73736 | tf_op jit(solution)/shard_map/ppermute | solution.py:357
  15.7 1.5 %shard_map.78 = (f32[32,24,256]{2,1,0:T(8,128)S(1)}, f32[32,256]{1,0:T(8,128)S(1)}) custom-call(f32[32,24,256]{2,1,0:T(8,128)S(1)} %get-tuple-element.29.own_ref, f32[3,4,768]{2,1,0:T(4,128)S(1)} %collective-permute-done.core_ref, f32[3,4,768]{2,1,0:T(4,128)S(1)} %collective-permute-done.1.chip_ref, f32[24,256]{1,0:T(8,128)S(1)} %get-tuple-element.33.next_ref, ...), custom_call_target="tpu_custom_call" | custom-call | flops 100000000 | bytes 1048576 | tf_op jit(solution)/shard_map/pallas_call | solution.py:297
  17.2 0.9 %shard_map.79.p_ref = f32[32,256]{1,0:T(8,128)S(1)} custom-call(f32[32,256]{1,0:T(8,128)S(1)} %get-tuple-element.38.p_ref, f32[10,24,256]{2,1,0:T(8,128)S(1)} %collective-permute-done.2.r_ref, bf16[256,256]{1,0:T(8,128)(2,1)S(1)} %get-tuple-element.39.bh_ref, bf16[256,256]{1,0:T(8,128)(2,1)S(1)} %get-tuple-element.40.bl_ref, ...), custom_call_target="tpu_custom_call" | custom-call | flops 300000000 | bytes 1048576 | tf_op jit(solution)/shard_map/pallas_call | solution.py:297
  18.1 0.0 copy-start.2
  18.1 0.0 collective-permute-done.4.core_ref
  18.1 0.0 collective-permute-done.5.chip_ref
  18.1 0.0 collective-permute-done.3.r_ref
  18.1 0.8 %shard_map.82 = f32[8,4,3,4,128]{4,3,2,1,0:T(4,128)S(1)} custom-call(f32[32,256]{1,0:T(8,128)S(1)} %shard_map.79.p_ref, f32[10,24,256]{2,1,0:T(8,128)S(1)} %collective-permute-done.3.r_ref, f32[24,256]{1,0:T(8,128)S(1)} %collective-permute-done.4.core_ref, f32[24,256]{1,0:T(8,128)S(1)} %collective-permute-done.5.chip_ref, ...), custom_call_target="tpu_custom_call" | custom-call | flops 1000000000 | bytes 1048576 | tf_op jit(solution)/shard_map/pallas_call | solution.py:297
  18.9 14.4 %all_to_all.5.parts_ref = f32[32,3,4,128]{3,2,1,0:T(4,128)S(1)} all-to-all(f32[32,3,4,128]{3,2,1,0:T(4,128)S(1)} %bitcast.6), channel_id=1, replica_groups=mesh['gx'=8,'gy'=4] {'gx','gy'}, dimensions={0} | all-to-all | bytes 393216 | tf_op jit(solution)/shard_map/all_to_all | solution.py:381
  33.4 0.0 copy-done.2
  33.4 0.7 %shard_map.83 = f32[24,64]{1,0:T(8,128)} custom-call(f32[32,3,4,128]{3,2,1,0:T(4,128)S(1)} %all_to_all.5.parts_ref, f32[24,64]{1,0:T(8,128)S(1)} %bitcast.8), custom_call_target="tpu_custom_call" | custom-call | flops 1000000000 | bytes 1048576 | tf_op jit(solution)/shard_map/pallas_call | solution.py:297
Async XLA Ops:
  0.0 7.9 %copy-start.5 = (f32[21]{0:T(128)S(1)}, f32[21]{0:T(128)}, u32[]{:S(2)}) copy-start(f32[21]{0:T(128)} %param.11) | copy-start | bytes 256
  0.0 1.1 %copy-start.1 = (f32[4,6,32,256]{3,2,1,0:T(8,128)S(1)}, f32[4,6,32,256]{3,2,1,0:T(8,128)}, u32[]{:S(2)}) copy-start(f32[4,6,32,256]{3,2,1,0:T(8,128)} %param.7) | copy-start | bytes 2359300
  1.3 7.3 %copy-start.3 = (f32[6,6]{1,0:T(8,128)S(1)}, f32[6,6]{1,0:T(8,128)}, u32[]{:S(2)}) copy-start(f32[6,6]{1,0:T(8,128)} %time_ref.1) | copy-start | bytes 436
  1.3 7.3 %copy-start.4 = (f32[4,4]{1,0:T(4,128)S(1)}, f32[4,4]{1,0:T(4,128)}, u32[]{:S(2)}) copy-start(f32[4,4]{1,0:T(4,128)} %field_ref.1) | copy-start | bytes 196
  1.3 7.3 %copy-start.6 = (f32[21]{0:T(128)S(1)}, f32[21]{0:T(128)}, u32[]{:S(2)}) copy-start(f32[21]{0:T(128)} %param.10) | copy-start | bytes 256
  1.7 7.6 %copy-start = (bf16[32,256,256]{2,1,0:T(8,128)(2,1)S(1)}, bf16[32,256,256]{2,1,0:T(8,128)(2,1)}, u32[]{:S(2)}) copy-start(bf16[32,256,256]{2,1,0:T(8,128)(2,1)} %modes_ref.7) | copy-start | bytes 12582916
  1.7 8.1 %collective-permute-start = (f32[3,4,768]{2,1,0:T(4,128)S(1)}, f32[3,4,768]{2,1,0:T(4,128)S(1)}, u32[]{:S(2)}, u32[]{:S(2)}) collective-permute-start(f32[3,4,768]{2,1,0:T(4,128)S(1)} %get-tuple-element.30), channel_id=1, source_target_pairs={{0,1},{1,0},{2,3},{3,2},{4,5},{5,4},{6,7},{7,6},{8,9},{9,8},{10,11... | collective-permute-start | bytes 110600 | tf_op jit(solution)/shard_map/ppermute | solution.py:327
  1.8 8.0 %collective-permute-start.1 = (f32[3,4,768]{2,1,0:T(4,128)S(1)}, f32[3,4,768]{2,1,0:T(4,128)S(1)}, u32[]{:S(2)}, u32[]{:S(2)}) collective-permute-start(f32[3,4,768]{2,1,0:T(4,128)S(1)} %get-tuple-element.31), channel_id=1, source_target_pairs={{1,2},{2,1},{5,6},{6,5},{9,10},{10,9},{13,14},{14,13},{17,18},{18,... | collective-permute-start | bytes 110600 | tf_op jit(solution)/shard_map/ppermute | solution.py:328
  6.6 5.2 %collective-permute-start.2 = (f32[10,24,256]{2,1,0:T(8,128)S(1)}, f32[10,24,256]{2,1,0:T(8,128)S(1)}, u32[]{:S(2)}, u32[]{:S(2)}) collective-permute-start(f32[10,24,256]{2,1,0:T(8,128)S(1)} %get-tuple-element.32), channel_id=1, source_target_pairs={{0,4},{4,0},{8,12},{12,8},{16,20},{20,16},{24,28},{28,24},{1,5},{5... | collective-permute-start | bytes 737288 | tf_op jit(solution)/shard_map/ppermute | solution.py:324
  10.2 7.9 %collective-permute-start.3 = (f32[10,24,256]{2,1,0:T(8,128)S(1)}, f32[10,24,256]{2,1,0:T(8,128)S(1)}, u32[]{:S(2)}, u32[]{:S(2)}) collective-permute-start(f32[10,24,256]{2,1,0:T(8,128)S(1)} %shard_map.81), channel_id=1, source_target_pairs={{4,8},{8,4},{12,16},{16,12},{20,24},{24,20},{5,9},{9,5},{13,17},{1... | collective-permute-start | bytes 737288 | tf_op jit(solution)/shard_map/ppermute | solution.py:353
  11.9 6.2 %collective-permute-start.4 = (f32[24,256]{1,0:T(8,128)S(1)}, f32[24,256]{1,0:T(8,128)S(1)}, u32[]{:S(2)}, u32[]{:S(2)}) collective-permute-start(f32[24,256]{1,0:T(8,128)S(1)} %get-tuple-element.33.next_ref), channel_id=1, source_target_pairs={{0,1},{1,0},{2,3},{3,2},{4,5},{5,4},{6,7},{7,6},{8,9},{9,8},{10,11... | collective-permute-start | bytes 73736 | tf_op jit(solution)/shard_map/ppermute | solution.py:356
  12.0 6.2 %collective-permute-start.5 = (f32[24,256]{1,0:T(8,128)S(1)}, f32[24,256]{1,0:T(8,128)S(1)}, u32[]{:S(2)}, u32[]{:S(2)}) collective-permute-start(f32[24,256]{1,0:T(8,128)S(1)} %get-tuple-element.45), channel_id=1, source_target_pairs={{1,2},{2,1},{5,6},{6,5},{9,10},{10,9},{13,14},{14,13},{17,18},{18,... | collective-permute-start | bytes 73736 | tf_op jit(solution)/shard_map/ppermute | solution.py:357
  18.1 15.3 %copy-start.2 = (f32[64,24]{0,1:T(8,128)S(1)}, f32[64,24]{0,1:T(8,128)}, u32[]{:S(2)}) copy-start(f32[64,24]{0,1:T(8,128)} %param.13) | copy-start | bytes 18436

commit v5 on v4

v5 whole, which is shorter than its diff:
```python
import functools

import jax
import jax.numpy as jnp
from jax import lax
from jax.experimental import pallas as pl
from jax.experimental.pallas import tpu as pltpu
from jax.sharding import PartitionSpec as P

F32, BF16 = jnp.float32, jnp.bfloat16
NN = (((1,), (0,)), ((), ()))
LANES = 128
PITCH = 16


def dot(a, b, dims=NN):
    return lax.dot_general(a, b, dims, preferred_element_type=F32)


def halves(v):
    high = v.astype(BF16)
    return high, (v - high.astype(F32)).astype(BF16)


def dot2(a, b, dims=NN):
    (ah, al), (bh, bl) = a, b
    return dot(ah, bh, dims) + dot(ah, bl, dims) + dot(al, bh, dims)


def iota(shape, dim):
    return lax.broadcasted_iota(jnp.int32, shape, dim)


def stacked(v):
    high = v.astype(BF16).astype(F32)
    parts = [high, v - high, high]
    if (3 * v.shape[0]) % 16:
        parts.append(jnp.zeros((-3 * v.shape[0] % 96, v.shape[1]), F32))
    return jnp.concatenate(parts, axis=0).astype(BF16)


def wide(m):
    high = m.astype(BF16).astype(F32)
    parts = [high, high, m - high]
    if (3 * m.shape[1]) % 16:
        parts.append(jnp.zeros((m.shape[0], -3 * m.shape[1] % 96), F32))
    return jnp.concatenate(parts, axis=1).astype(BF16)


def turn_kernel(reach, a_hbm, *refs):
    count = (len(refs) - 5) // 2
    small, (t_ref, s1_ref, s2_ref), held, (a_ref, sem) = refs[:count], refs[count : count + 3], refs[count + 3 : -2], refs[-2:]
    copies = [pltpu.make_async_copy(a_hbm, a_ref, sem.at[0])]
    copies += [pltpu.make_async_copy(x, y, sem.at[i + 1]) for i, (x, y) in enumerate(zip(small, held))]
    for copy in copies:
        copy.start()
    for copy in copies:
        copy.wait()
    t_ref[...] = jnp.swapaxes(a_ref[...], 0, 1)
    odd = lax.axis_index("gx") % 2
    far = t_ref.shape[0] - reach
    s1_ref[...] = t_ref[pl.ds((1 - odd) * far, reach)]
    s2_ref[...] = t_ref[pl.ds(odd * far, reach)]


def block_kernel(reach, modes_ref, core_ref, chip_ref):
    width_y = modes_ref.shape[1]
    odd = lax.axis_index("gy") % 2
    low = jnp.swapaxes(modes_ref[:, :PITCH].astype(F32), 0, 1)
    high = jnp.swapaxes(modes_ref[:, width_y - PITCH :].astype(F32), 0, 1)
    for i in range(reach):
        a, b = low[i], high[PITCH - reach + i]
        core_ref[i] = jnp.where(odd == 1, a, b)
        chip_ref[i] = jnp.where(odd == 1, b, a)


def band_kernel(reach, north_ref, t_ref, y_ref, z_ref, bh_ref, bl_ref, ch_ref, cl_ref):
    width_x, channels, width_y = t_ref.shape
    span = 2 * reach + 1
    odd = lax.axis_index("gy") % 2
    shift = iota((width_y, width_y), 0) - iota((width_y, width_y), 1) + reach
    lane = iota((width_y, LANES), 1)
    at = lane % PITCH
    right = jnp.where(lane < PITCH, 1 - odd, odd) == 1
    over = iota((width_y, LANES), 0) - at + jnp.where(right, reach - width_y, 2 * reach)
    over = jnp.where((at < reach) & (lane < 2 * PITCH), over, -1)
    first = iota((8, width_y), 1)
    base = jnp.zeros((8, width_y), F32)
    cross = jnp.zeros((width_y, LANES), F32)
    for j in range(span):
        tap = north_ref[:, j : j + 1]
        base = jnp.where(first == (reach - j) % width_y, tap, base)
        cross = jnp.where(over == j, tap, cross)
    rolled = pltpu.roll(jnp.broadcast_to(base[:1], (width_y, width_y)), 0, 1, stride=1, stride_axis=0)
    band = halves(jnp.where((shift >= 0) & (shift < span), rolled, 0.0))
    cross = halves(cross)
    bh_ref[...], bl_ref[...] = band
    ch_ref[...], cl_ref[...] = cross
    data = halves(t_ref[...].reshape(width_x * channels, width_y))
    y_ref[...] = dot2(data, band).reshape(y_ref.shape)
    z_ref[...] = dot2(data, cross).reshape(z_ref.shape)


def own_kernel(reach, east_ref, field_ref, time_ref, y_ref, z_ref, s_ref, sz_ref, mix_ref, taps_ref):
    width_x, channels, width_y = y_ref.shape
    x_shift = iota((width_x, width_x), 1) - iota((width_x, width_x), 0) + reach
    along = jnp.zeros((width_x, width_x), F32)
    for j in range(2 * reach + 1):
        tap = east_ref[:, j : j + 1]
        along = jnp.where(x_shift == j, tap, along)
        taps_ref[j] = jnp.broadcast_to(tap, taps_ref.shape[1:])
    along = wide(along)
    s_ref[...] = along_x(along, y_ref[...])
    sz_ref[...] = along_x(along, z_ref[...])
    fields, levels = field_ref.shape[0], time_ref.shape[0]
    rows = mix_ref.shape[0]
    out, into = iota((rows, channels), 0), iota((rows, channels), 1)
    by_field = jnp.zeros((rows, channels), F32)
    by_time = jnp.zeros((rows, channels), F32)
    for g in range(fields):
        for f in range(fields):
            here = (into // levels == g) & (out // levels == f)
            by_field = jnp.where(here, field_ref[g : g + 1, f : f + 1], by_field)
    for s in range(levels):
        for t in range(levels):
            here = (into % levels == s) & (out % levels == t)
            by_time = jnp.where(here, time_ref[s : s + 1, t : t + 1], by_time)
    mix_ref[...] = wide(by_field * by_time)


def along_x(matrix, y):
    by_channel = jnp.swapaxes(y, 0, 1)
    return jnp.swapaxes(jnp.stack([dot(matrix, stacked(by_channel[c])) for c in range(y.shape[1])]), 0, 1)


def tile_kernel(reach, s_ref, z_ref, mix_ref, modes_ref, p_ref, l_ref):
    width_x = s_ref.shape[0]
    mix = mix_ref[...]
    inner = [dot(mix, stacked(s_ref[x])).astype(BF16) for x in range(reach, width_x - reach)]
    acc = dot(inner[0], modes_ref[reach])
    for x in range(1, width_x - 2 * reach):
        acc = acc + dot(inner[x], modes_ref[reach + x])
    p_ref[...] = acc
    packed(l_ref, [dot(mix, stacked(z_ref[x])) for x in range(reach, width_x - reach)])


def packed(l_ref, values):
    each = LANES // (2 * PITCH)
    for tile in range(l_ref.shape[1] // LANES):
        total = None
        for k, value in enumerate(values[tile * each : (tile + 1) * each]):
            value = pltpu.roll(value, k * 2 * PITCH, 1) if k else value
            total = value if total is None else total + value
        l_ref[:, tile * LANES : (tile + 1) * LANES] = total


def place(reach, left, width_x, m):
    return left * (reach - 1 - m) + (1 - left) * (width_x - reach + m)


def added(reach, left, rows, taps_ref, m, count, lanes):
    value = None
    for n in range(m + 1):
        d = m - n
        tap = taps_ref[left * d + (1 - left) * (2 * reach - d), :, :lanes][None]
        term = tap * rows[left * (reach - 1 - n) + (1 - left) * n].reshape(count // 8, 8, lanes)
        value = term if value is None else value + term
    return value.reshape(count, lanes)


def side(reach, left, rows, s_ref, taps_ref, mix_ref, modes_ref, mixed):
    width_x, channels, width_y = s_ref.shape
    mix = mix_ref[...]
    for m in range(reach):
        value = s_ref[place(reach, left, width_x, m)] + added(reach, left, rows, taps_ref, m, channels, width_y)
        mixed[m] = dot(mix, stacked(value)).astype(BF16)
    total = None
    for m in range(reach):
        term = dot(mixed[m], modes_ref[place(reach, left, width_x, m)])
        total = term if total is None else total + term
    return total


def smoothed(r_ref, wide_ref, high_ref, low_ref):
    rows = halves(r_ref[...].reshape(-1, r_ref.shape[2]))
    return dot2(rows, (high_ref[...], low_ref[...])).reshape(wide_ref.shape)


def rows_kernel(
    reach, second, p_ref, r_ref, bh_ref, bl_ref, ch_ref, cl_ref, s_ref, z_ref, taps_ref, mix_ref, modes_ref, out_ref, l_ref, by, bz, mixed
):
    width_x, channels, _ = s_ref.shape
    odd = lax.axis_index("gx") % 2
    left = 1 - odd if second else odd
    by[...] = smoothed(r_ref, by, bh_ref, bl_ref)
    bz[...] = smoothed(r_ref, bz, ch_ref, cl_ref)
    mix = mix_ref[...]
    over = []
    for m in range(reach):
        value = z_ref[place(reach, left, width_x, m)] + added(reach, left, bz, taps_ref, m, channels, LANES)
        over.append(dot(mix, stacked(value)))
    over += [jnp.zeros(over[0].shape, F32)] * (-reach % (LANES // (2 * PITCH)))
    packed(l_ref, over)
    out_ref[...] = p_ref[...] + side(reach, left, by, s_ref, taps_ref, mix_ref, modes_ref, mixed)


def gather_kernel(reach, core_ref, chip_ref, out_ref, both):
    _, width_x, modes = core_ref.shape
    odd = lax.axis_index("gx") % 2
    gap = jnp.zeros((PITCH - reach, width_x, modes), F32)
    both[:, :PITCH] = jnp.swapaxes(jnp.concatenate([core_ref[...], gap], axis=0), 0, 1)
    both[:, PITCH:] = jnp.swapaxes(jnp.concatenate([chip_ref[...], gap], axis=0), 0, 1)
    inner = width_x - 2 * reach
    room = -(-reach // (LANES // (2 * PITCH))) * (LANES // (2 * PITCH))
    for x in range(inner):
        out_ref[x] = both[reach + x].astype(BF16)
    for i in range(2):
        left = odd if i == 0 else 1 - odd
        for m in range(room):
            if m < reach:
                out_ref[inner + i * room + m] = both[place(reach, left, width_x, m)].astype(BF16)
            else:
                out_ref[inner + i * room + m] = jnp.zeros(out_ref.shape[1:], BF16)


def over_kernel(reach, p_ref, l0_ref, l1_ref, core_ref, chip_ref, out_ref, blocks_ref, both, blocks):
    gather_kernel(reach, core_ref, chip_ref, blocks, both)
    total = p_ref[...]
    start = 0
    for l_ref in (l0_ref, l1_ref):
        count = l_ref.shape[1] // (2 * PITCH)
        total = total + over(l_ref[...], blocks[start : start + count])
        start += count
    out_ref[...] = total
    blocks_ref[...] = blocks[start:]


def over(rows, blocks):
    value = dot(jnp.concatenate(halves(rows), axis=0), blocks.reshape(-1, blocks.shape[2]))
    half = rows.shape[0]
    return value[:half] + value[half:]


def last_kernel(reach, p_ref, r_ref, blocks_ref, *rest):
    *refs, out_ref, total, l_ref, by, bz, mixed = rest
    rows_kernel(reach, True, p_ref, r_ref, *refs, total, l_ref, by, bz, mixed)
    deliver(total[...] + over(l_ref[...], blocks_ref[...]), r_ref.shape[1], out_ref)


def deliver(total, channels, out_ref):
    if len(out_ref.shape) == 2:
        out_ref[...] = total
        return
    _, parts, count, high, lanes = out_ref.shape
    owned = total.shape[1] // parts
    rows = count * high
    for g in range(parts):
        piece = jnp.concatenate(
            [total[k * rows : (k + 1) * rows, g * owned : (g + 1) * owned] for k in range(lanes // owned)], axis=1
        )
        for k in range(out_ref.shape[0]):
            for j in range(count):
                out_ref[k, g, j] = piece[j * high : (j + 1) * high]


def sum_kernel(parts_ref, coefficients_ref, out_ref):
    channels, owned = out_ref.shape
    _, count, high, lanes = parts_ref.shape
    total = jnp.sum(parts_ref[...], axis=0)
    for k in range(lanes // owned):
        for j in range(count):
            rows = pl.ds((k * count + j) * high, high)
            out_ref[rows] = coefficients_ref[rows] + total[j, :, k * owned : (k + 1) * owned]


def vmem(array):
    return pltpu.with_memory_space_constraint(array, pltpu.VMEM)


def call(body, ins, outs, scratch=(), keep=True, outside=False, weight=1e9):
    place_in = pltpu.HBM if outside else pltpu.VMEM
    make = pltpu.VMEM if keep else jax.ShapeDtypeStruct
    return pl.pallas_call(
        body,
        out_shape=[make(shape, dtype) for shape, dtype in outs],
        in_specs=[pl.BlockSpec(memory_space=place_in)] * len(ins),
        out_specs=[pl.BlockSpec(memory_space=pltpu.VMEM)] * len(outs),
        scratch_shapes=list(scratch),
        compiler_params=pltpu.CompilerParams(vmem_limit_bytes=24 << 20),
        cost_estimate=pl.CostEstimate(flops=int(weight), bytes_accessed=1 << 20, transcendentals=0),
    )(*[pltpu.with_memory_space_constraint(array, place_in) for array in ins])


def pairs(count, first):
    found = []
    for low in range(first, count - 1, 2):
        found += [(low, low + 1), (low + 1, low)]
    return found


def local(adjoint_forcing, field_mixing, time_mixing, kernel_east, kernel_north, spatial_modes, coefficients):
    fields, levels, width_x, width_y = adjoint_forcing.shape
    channels, modes, owned = fields * levels, spatial_modes.shape[2], coefficients.shape[0]
    reach = (kernel_east.shape[0] - 1) // 2
    count_x, count_y = lax.axis_size("gx"), lax.axis_size("gy")
    raw = adjoint_forcing.reshape(channels, width_x, width_y)
    slab = ((reach, channels, width_y), F32)
    full = ((width_x, channels, width_y), F32)
    narrow = ((width_x, channels, LANES), F32)
    band = ((width_y, width_y), BF16)
    cross = ((width_y, LANES), BF16)
    wide_rows = -(-channels // 16) * 16
    share = ((wide_rows, modes), F32)
    each = LANES // (2 * PITCH)
    inner = width_x - 2 * reach
    small = [kernel_north.reshape(1, -1), kernel_east.reshape(1, -1), field_mixing, time_mixing]
    t, s1, s2, *small = call(
        functools.partial(turn_kernel, reach),
        [raw, *small],
        [full, slab, slab] + [(array.shape, F32) for array in small],
        [pltpu.VMEM(raw.shape, F32), pltpu.SemaphoreType.DMA((1 + len(small),))],
        outside=True,
        weight=3e9,
    )
    held = vmem(spatial_modes)
    r1 = lax.ppermute(s1, "gx", pairs(count_x, 0))
    r2 = lax.ppermute(s2, "gx", pairs(count_x, 1))
    y, z, bh, bl, ch, cl = call(
        functools.partial(band_kernel, reach),
        [small[0], t],
        [full, narrow, band, band, cross, cross],
        weight=1e7,
    )
    block = ((reach, width_x, modes), F32)
    core, chip = call(functools.partial(block_kernel, reach), [held], [block, block], weight=3e8)
    core = lax.ppermute(core, "gy", pairs(count_y, 0))
    chip = lax.ppermute(chip, "gy", pairs(count_y, 1))
    s, sz, mix, taps = call(
        functools.partial(own_kernel, reach),
        [*small[1:], y, z],
        [
            full,
            narrow,
            ((wide_rows, 3 * channels + -3 * channels % 96), BF16),
            ((2 * reach + 1, 8, width_y), F32),
        ],
        weight=1e7,
    )
    p, l0 = call(
        functools.partial(tile_kernel, reach),
        [s, sz, mix, held],
        [share, ((wide_rows, inner // each * LANES), F32)],
        weight=1e7,
    )
    both = [bh, bl, ch, cl, s, sz, taps, mix, held]
    layer = (wide_rows, -(-reach // each) * LANES)
    room = [pltpu.VMEM(slab[0], F32), pltpu.VMEM((reach, channels, LANES), F32), pltpu.VMEM((reach, wide_rows, width_y), BF16)]
    p, l1 = call(
        functools.partial(rows_kernel, reach, False), [p, r1, *both], [share, (layer, F32)], room, weight=1e9
    )
    slots = inner + 2 * (layer[1] // (2 * PITCH))
    p, blocks = call(
        functools.partial(over_kernel, reach),
        [p, l0, l1, core, chip],
        [share, ((layer[1] // (2 * PITCH), 2 * PITCH, modes), BF16)],
        [pltpu.VMEM((width_x, 2 * PITCH, modes), F32), pltpu.VMEM((slots, 2 * PITCH, modes), BF16)],
        weight=1e7,
    )
    rows = channels * owned // 128
    high = 4 if rows % 4 == 0 else rows
    (out,) = call(
        functools.partial(last_kernel, reach),
        [p, r2, blocks, *both],
        [((count_x, count_y, rows // high, high, 128), F32)],
        [pltpu.VMEM(share[0], F32), pltpu.VMEM(layer, F32), *room],
    )
    out = out.reshape((count_x * count_y,) + out.shape[2:])
    parts = lax.all_to_all(out, ("gx", "gy"), 0, 0, tiled=True)
    (gradient,) = call(sum_kernel, [parts, coefficients.T], [((channels, owned), F32)], keep=False)
    return gradient.T


def solution(mesh):
    in_specs = (P(None, None, "gx", "gy"), P(), P(), P(), P(), P("gx", "gy", None), P("gy", None))
    out_specs = P("gy", None)
    return jax.shard_map(local, mesh=mesh, in_specs=in_specs, out_specs=out_specs, check_vma=False)
```

time: 34.3 us -> 32.7 us (0.953)
  starting transfers between devices: 10.7 us -> 6.84 us
  blocking collectives: 14.4 us -> 16.8 us
  local copies, waits for them, and re-layouts: 1.18 us -> 0.01 us
  Pallas kernels: 6.75 us -> 7.81 us
    ppermute x2 -> x0, starting transfers between devices: 3.84 us -> none  [the longest x1 3.77 us: local(): chip2 = lax.ppermute(chip1, 'gy', pairs(count_y, 1))]
    all_to_all x1, blocking collectives: 14.4 us -> 16.8 us  [local(): parts = lax.all_to_all(out, ('gx', 'gy'), 0, 0, tiled=True)]
    ppermute x1, starting transfers between devices: 4.76 us -> 3.05 us  [local(): chip = lax.ppermute(chip, 'gy', pairs(count_y, 1))]
    unnamed x14 -> x4, local copies, waits for them, and re-layouts: 1.18 us -> 0.01 us
    pallas_call x11 -> x9, Pallas kernels: 6.75 us -> 7.81 us  [call(): pl.pallas_call(body, out_shape=[make(shape, dtype) for shape, dtype in ou...]
    ppermute x1, waiting for transfers between devices: 0.01 us -> 0.92 us  [local(): chip = lax.ppermute(chip, 'gy', pairs(count_y, 1))]
    ppermute x1, starting transfers between devices: 0.12 us -> 1.02 us  [local(): core = lax.ppermute(core, 'gy', pairs(count_y, 0))]
    ppermute x1, waiting for transfers between devices: 0.85 us -> 0.01 us  [local(): r1 = lax.ppermute(s1, 'gx', pairs(count_x, 0))]
  transfers between devices with their start and end apart: 6 -> 4, of which waited for: 1 -> 1; matrix products, arithmetic and copies ran while one was open for 0% -> 0% of each run, Pallas kernels for 14% -> 13%
where the time goes in v5:
time: 32.7 us; the launch traced here: 32.5 us
  blocking collectives  16.8 us (51%)
  Pallas kernels  7.81 us (24%)
  starting transfers between devices  6.84 us (21%)
  waiting for transfers between devices  0.93 us (3%)
    all_to_all x1, blocking collectives, local(): parts = lax.all_to_all(out, ('gx', 'gy'), 0, 0, tiled=True)  16.8 us
    pallas_call x9, Pallas kernels, call(): pl.pallas_call(body, out_shape=[make(shape, dtype) for shape, dtype in ou...  7.81 us
    ppermute x1, starting transfers between devices, local(): chip = lax.ppermute(chip, 'gy', pairs(count_y, 1))  3.05 us
    ppermute x1, starting transfers between devices, local(): r1 = lax.ppermute(s1, 'gx', pairs(count_x, 0))  2.1 us
    ppermute x1, starting transfers between devices, local(): core = lax.ppermute(core, 'gy', pairs(count_y, 0))  1.02 us
    ppermute x1, waiting for transfers between devices, local(): chip = lax.ppermute(chip, 'gy', pairs(count_y, 1))  0.92 us
    ppermute x1, starting transfers between devices, local(): r2 = lax.ppermute(s2, 'gx', pairs(count_x, 1))  0.68 us
  transfers between devices with their start and end apart: 4, of which 1 were waited for; matrix products, arithmetic and copies ran while one was open for 0% of the time, Pallas kernels for 13%

profile of v5, /device:TPU:1, one launch (start us, length us, event | category | flops | bytes accessed | tf_op | source)
XLA Modules:
  0.0 32.5 jit_solution(16531954913070218242)
XLA Ops:
  0.0 0.0 copy-start
  0.0 1.5 %shard_map.73 = (f32[32,24,256]{2,1,0:T(8,128)S(1)}, f32[10,24,256]{2,1,0:T(8,128)S(1)}, f32[10,24,256]{2,1,0:T(8,128)S(1)}, f32[1,21]{1,0:T(1,128)S(1)}, f32[1,...) custom-call(f32[24,32,256]{2,1,0:T(8,128)} %bitcast.8, f32[1,21]{1,0:T(1,128)} %bitcast.9, ...), custom_call_target="tpu_custom_call" | custom-call | flops 3000000000 | bytes 1048576 | tf_op jit(solution)/shard_map/pallas_call | solution.py:283
  1.5 2.1 %collective-permute-start = (f32[10,24,256]{2,1,0:T(8,128)S(1)}, f32[10,24,256]{2,1,0:T(8,128)S(1)}, u32[]{:S(2)}, u32[]{:S(2)}) collective-permute-start(f32[10,24,256]{2,1,0:T(8,128)S(1)} %get-tuple-element.41), channel_id=1, source_target_pairs={{0,4},{4,0},{8,12},{12,8},{16,20},{20,16},{24,28},{28,24},{1,5},{5... | collective-permute-start | bytes 737288 | tf_op jit(solution)/shard_map/ppermute | solution.py:326
  3.6 0.0 copy-done
  3.6 0.2 shard_map.78
  3.8 1.0 %collective-permute-start.1 = (f32[10,32,256]{2,1,0:T(8,128)S(1)}, f32[10,32,256]{2,1,0:T(8,128)S(1)}, u32[]{:S(2)}, u32[]{:S(2)}) collective-permute-start(f32[10,32,256]{2,1,0:T(8,128)S(1)} %get-tuple-element.50), channel_id=1, source_target_pairs={{0,1},{1,0},{2,3},{3,2},{4,5},{5,4},{6,7},{7,6},{8,9},{9,8},{10,11... | collective-permute-start | bytes 983048 | tf_op jit(solution)/shard_map/ppermute | solution.py:336
  4.9 3.0 %collective-permute-start.2 = (f32[10,32,256]{2,1,0:T(8,128)S(1)}, f32[10,32,256]{2,1,0:T(8,128)S(1)}, u32[]{:S(2)}, u32[]{:S(2)}) collective-permute-start(f32[10,32,256]{2,1,0:T(8,128)S(1)} %get-tuple-element.51), channel_id=1, source_target_pairs={{1,2},{2,1},{5,6},{6,5},{9,10},{10,9},{13,14},{14,13},{17,18},{18,... | collective-permute-start | bytes 983048 | tf_op jit(solution)/shard_map/ppermute | solution.py:337
  7.9 0.7 %collective-permute-start.3 = (f32[10,24,256]{2,1,0:T(8,128)S(1)}, f32[10,24,256]{2,1,0:T(8,128)S(1)}, u32[]{:S(2)}, u32[]{:S(2)}) collective-permute-start(f32[10,24,256]{2,1,0:T(8,128)S(1)} %get-tuple-element.53), channel_id=1, source_target_pairs={{4,8},{8,4},{12,16},{16,12},{20,24},{24,20},{5,9},{9,5},{13,17},{1... | collective-permute-start | bytes 737288 | tf_op jit(solution)/shard_map/ppermute | solution.py:327
  8.6 1.1 %shard_map.74 = (f32[32,24,256]{2,1,0:T(8,128)S(1)}, f32[32,24,128]{2,1,0:T(8,128)S(1)}, bf16[256,256]{1,0:T(8,128)(2,1)S(1)}, bf16[256,256]{1,0:T(8,128)(2,1)S(...) custom-call(f32[1,21]{1,0:T(1,128)S(1)} %get-tuple-element.33.north_ref, ...), custom_call_target="tpu_custom_call" | custom-call | flops 10000000 | bytes 1048576 | tf_op jit(solution)/shard_map/pallas_call | solution.py:283
  9.7 0.8 %shard_map.75 = (f32[32,24,256]{2,1,0:T(8,128)S(1)}, f32[32,24,128]{2,1,0:T(8,128)S(1)}, bf16[32,96]{1,0:T(8,128)(2,1)S(1)}, f32[21,8,256]{2,1,0:T(8,128)S(1)}) custom-call(f32[1,21]{1,0:T(1,128)S(1)} %get-tuple-element.30.east_ref, f32[4,4]{1,0:T(4,128)S(1)} %get-tuple-element.31.field_ref, f32[6,6]{1,0:T(8,128)S(1)} %get-tuple-element.32.time_ref, ...), custom_call_target="tpu_custom_call" | custom-call | flops 10000000 | bytes 1048576 | tf_op jit(solution)/shard_map/pallas_call | solution.py:283
  10.5 0.6 %shard_map.76 = (f32[32,256]{1,0:T(8,128)S(1)}, f32[32,384]{1,0:T(8,128)S(1)}) custom-call(f32[32,24,256]{2,1,0:T(8,128)S(1)} %get-tuple-element.37.s_ref.rest_4_, f32[32,24,128]{2,1,0:T(8,128)S(1)} %get-tuple-element.38.z_ref.rest_5_, bf16[32,96]{1,0:T(8,128)(2,1)S(1)} %get-tuple-element.39.mix_ref.rest_7_, bf16[32,256,256]{2,1,0:T(8,128)(2,1)S(1)} %copy-done), custom_call_target="tpu_custom_call" | custom-call | flops 10000000 | bytes 1048576 | tf_op jit(solution)/shard_map/pallas_call | solution.py:283
  11.1 0.0 collective-permute-done.r_ref
  11.1 1.2 %shard_map.77 = (f32[32,256]{1,0:T(8,128)S(1)}, f32[32,384]{1,0:T(8,128)S(1)}) custom-call(f32[32,256]{1,0:T(8,128)S(1)} %get-tuple-element.40.p_ref, f32[10,24,256]{2,1,0:T(8,128)S(1)} %collective-permute-done.r_ref, bf16[256,256]{1,0:T(8,128)(2,1)S(1)} %get-tuple-element.42.bh_ref.rest_0_, bf16[256,256]{1,0:T(8,128)(2,1)S(1)} %get-tuple-element.43.bl_ref.rest_1_, ...), custom_call_target="tpu_custom_call" | custom-call | flops 1000000000 | bytes 1048576 | tf_op jit(solution)/shard_map/pallas_call | solution.py:283
  12.3 0.0 copy-start.1
  12.3 0.0 collective-permute-done.1.core_ref
  12.3 0.9 %collective-permute-done.2.chip_ref = f32[10,32,256]{2,1,0:T(8,128)S(1)} collective-permute-done((f32[10,32,256]{2,1,0:T(8,128)S(1)}, f32[10,32,256]{2,1,0:T(8,128)S(1)}, u32[]{:S(2)}, u32[]{:S(2)}) %collective-permute-start.2) | collective-permute-done | bytes 327712 | tf_op jit(solution)/shard_map/ppermute | solution.py:337
  13.2 0.3 %shard_map.79 = (f32[32,256]{1,0:T(8,128)S(1)}, bf16[12,32,256]{2,1,0:T(8,128)(2,1)S(1)}) custom-call(f32[32,256]{1,0:T(8,128)S(1)} %get-tuple-element.47.p_ref, f32[32,384]{1,0:T(8,128)S(1)} %get-tuple-element.48.l0_ref, f32[32,384]{1,0:T(8,128)S(1)} %get-tuple-element.49.l1_ref, f32[10,32,256]{2,1,0:T(8,128)S(1)} %collective-permute-done.1.core_ref, ...), custom_call_target="tpu_custom_call" | custom-call | flops 10000000 | bytes 1048576 | tf_op jit(solution)/shard_map/pallas_call | solution.py:283
  13.6 0.0 collective-permute-done.3.r_ref
  13.6 1.4 %shard_map.80 = f32[8,4,3,4,128]{4,3,2,1,0:T(4,128)S(1)} custom-call(f32[32,256]{1,0:T(8,128)S(1)} %get-tuple-element.52.p_ref, f32[10,24,256]{2,1,0:T(8,128)S(1)} %collective-permute-done.3.r_ref, bf16[12,32,256]{2,1,0:T(8,128)(2,1)S(1)} %get-tuple-element.54.blocks_ref, bf16[256,256]{1,0:T(8,128)(2,1)S(1)} %get-tuple-element.42.bh_ref.rest_0_, ...), custom_call_target="tpu_custom_call" | custom-call | flops 1000000000 | bytes 1048576 | tf_op jit(solution)/shard_map/pallas_call | solution.py:283
  15.0 16.8 %all_to_all.5.parts_ref = f32[32,3,4,128]{3,2,1,0:T(4,128)S(1)} all-to-all(f32[32,3,4,128]{3,2,1,0:T(4,128)S(1)} %bitcast.6), channel_id=1, replica_groups=mesh['gx'=8,'gy'=4] {'gx','gy'}, dimensions={0} | all-to-all | bytes 393216 | tf_op jit(solution)/shard_map/all_to_all | solution.py:378
  31.8 0.0 copy-done.1
  31.8 0.7 %shard_map.81 = f32[24,64]{1,0:T(8,128)} custom-call(f32[32,3,4,128]{3,2,1,0:T(4,128)S(1)} %all_to_all.5.parts_ref, f32[24,64]{1,0:T(8,128)S(1)} %bitcast.7), custom_call_target="tpu_custom_call" | custom-call | flops 1000000000 | bytes 1048576 | tf_op jit(solution)/shard_map/pallas_call | solution.py:283
Async XLA Ops:
  0.0 3.6 %copy-start = (bf16[32,256,256]{2,1,0:T(8,128)(2,1)S(1)}, bf16[32,256,256]{2,1,0:T(8,128)(2,1)}, u32[]{:S(2)}) copy-start(bf16[32,256,256]{2,1,0:T(8,128)(2,1)} %rest_8_.1) | copy-start | bytes 12582916
  1.5 9.6 %collective-permute-start = (f32[10,24,256]{2,1,0:T(8,128)S(1)}, f32[10,24,256]{2,1,0:T(8,128)S(1)}, u32[]{:S(2)}, u32[]{:S(2)}) collective-permute-start(f32[10,24,256]{2,1,0:T(8,128)S(1)} %get-tuple-element.41), channel_id=1, source_target_pairs={{0,4},{4,0},{8,12},{12,8},{16,20},{20,16},{24,28},{28,24},{1,5},{5... | collective-permute-start | bytes 737288 | tf_op jit(solution)/shard_map/ppermute | solution.py:326
  3.8 8.5 %collective-permute-start.1 = (f32[10,32,256]{2,1,0:T(8,128)S(1)}, f32[10,32,256]{2,1,0:T(8,128)S(1)}, u32[]{:S(2)}, u32[]{:S(2)}) collective-permute-start(f32[10,32,256]{2,1,0:T(8,128)S(1)} %get-tuple-element.50), channel_id=1, source_target_pairs={{0,1},{1,0},{2,3},{3,2},{4,5},{5,4},{6,7},{7,6},{8,9},{9,8},{10,11... | collective-permute-start | bytes 983048 | tf_op jit(solution)/shard_map/ppermute | solution.py:336
  4.9 8.4 %collective-permute-start.2 = (f32[10,32,256]{2,1,0:T(8,128)S(1)}, f32[10,32,256]{2,1,0:T(8,128)S(1)}, u32[]{:S(2)}, u32[]{:S(2)}) collective-permute-start(f32[10,32,256]{2,1,0:T(8,128)S(1)} %get-tuple-element.51), channel_id=1, source_target_pairs={{1,2},{2,1},{5,6},{6,5},{9,10},{10,9},{13,14},{14,13},{17,18},{18,... | collective-permute-start | bytes 983048 | tf_op jit(solution)/shard_map/ppermute | solution.py:337
  7.9 5.7 %collective-permute-start.3 = (f32[10,24,256]{2,1,0:T(8,128)S(1)}, f32[10,24,256]{2,1,0:T(8,128)S(1)}, u32[]{:S(2)}, u32[]{:S(2)}) collective-permute-start(f32[10,24,256]{2,1,0:T(8,128)S(1)} %get-tuple-element.53), channel_id=1, source_target_pairs={{4,8},{8,4},{12,16},{16,12},{20,24},{24,20},{5,9},{9,5},{13,17},{1... | collective-permute-start | bytes 737288 | tf_op jit(solution)/shard_map/ppermute | solution.py:327
  12.3 19.5 %copy-start.1 = (f32[64,24]{0,1:T(8,128)S(1)}, f32[64,24]{0,1:T(8,128)}, u32[]{:S(2)}) copy-start(f32[64,24]{0,1:T(8,128)} %param.13) | copy-start | bytes 18436

commit v6 on v5

--- a/solution.py
+++ b/solution.py
@@ -47,27 +47,35 @@
     return jnp.concatenate(parts, axis=1).astype(BF16)
 
 
-def turn_kernel(reach, a_hbm, *refs):
+def first_kernel(reach, a_hbm, modes_hbm, *refs):
     count = (len(refs) - 5) // 2
-    small, (t_ref, s1_ref, s2_ref), held, (a_ref, sem) = refs[:count], refs[count : count + 3], refs[count + 3 : -2], refs[-2:]
-    copies = [pltpu.make_async_copy(a_hbm, a_ref, sem.at[0])]
-    copies += [pltpu.make_async_copy(x, y, sem.at[i + 1]) for i, (x, y) in enumerate(zip(small, held))]
+    small, s1_ref, ends, held = refs[:count], refs[count], refs[count + 1 : count + 3], refs[count + 3 : -2]
+    rows_ref, sem = refs[-2:]
+    window, width_x, width_y = rows_ref.shape[1], a_hbm.shape[1], a_hbm.shape[2]
+    odd = lax.axis_index("gx") % 2
+    start = pl.multiple_of((1 - odd) * (width_x - window), 8)
+    pairs_of = [(a_hbm.at[:, pl.ds(start, window)], rows_ref)]
+    pairs_of += [(modes_hbm.at[:, pl.ds(i * (width_y - PITCH), PITCH)], ends[i]) for i in range(2)]
+    pairs_of += list(zip(small, held))
+    copies = [pltpu.make_async_copy(x, y, sem.at[i]) for i, (x, y) in enumerate(pairs_of)]
     for copy in copies:
         copy.start()
     for copy in copies:
         copy.wait()
+    rows = jnp.swapaxes(rows_ref[...], 0, 1)
+    s1_ref[...] = jnp.where(odd == 1, rows[:reach], rows[window - reach :])
+
+
+def turn_kernel(reach, a_ref, before_ref, t_ref, s2_ref):
+    del before_ref
     t_ref[...] = jnp.swapaxes(a_ref[...], 0, 1)
-    odd = lax.axis_index("gx") % 2
-    far = t_ref.shape[0] - reach
-    s1_ref[...] = t_ref[pl.ds((1 - odd) * far, reach)]
-    s2_ref[...] = t_ref[pl.ds(odd * far, reach)]
-
-
-def block_kernel(reach, modes_ref, core_ref, chip_ref):
-    width_y = modes_ref.shape[1]
+    s2_ref[...] = t_ref[pl.ds(lax.axis_index("gx") % 2 * (t_ref.shape[0] - reach), reach)]
+
+
+def block_kernel(reach, low_ref, high_ref, core_ref, chip_ref):
     odd = lax.axis_index("gy") % 2
-    low = jnp.swapaxes(modes_ref[:, :PITCH].astype(F32), 0, 1)
-    high = jnp.swapaxes(modes_ref[:, width_y - PITCH :].astype(F32), 0, 1)
+    low = jnp.swapaxes(low_ref[...].astype(F32), 0, 1)
+    high = jnp.swapaxes(high_ref[...].astype(F32), 0, 1)
     for i in range(reach):
         a, b = low[i], high[PITCH - reach + i]
         core_ref[i] = jnp.where(odd == 1, a, b)
@@ -141,7 +149,7 @@
     for x in range(1, width_x - 2 * reach):
         acc = acc + dot(inner[x], modes_ref[reach + x])
     p_ref[...] = acc
-    packed(l_ref, [dot(mix, stacked(z_ref[x])) for x in range(reach, width_x - reach)])
+    packed(l_ref, [z_ref[x] for x in range(reach, width_x - reach)])
 
 
 def packed(l_ref, values):
@@ -194,11 +202,9 @@
     left = 1 - odd if second else odd
     by[...] = smoothed(r_ref, by, bh_ref, bl_ref)
     bz[...] = smoothed(r_ref, bz, ch_ref, cl_ref)
-    mix = mix_ref[...]
     over = []
     for m in range(reach):
-        value = z_ref[place(reach, left, width_x, m)] + added(reach, left, bz, taps_ref, m, channels, LANES)
-        over.append(dot(mix, stacked(value)))
+        over.append(z_ref[place(reach, left, width_x, m)] + added(reach, left, bz, taps_ref, m, channels, LANES))
     over += [jnp.zeros(over[0].shape, F32)] * (-reach % (LANES // (2 * PITCH)))
     packed(l_ref, over)
     out_ref[...] = p_ref[...] + side(reach, left, by, s_ref, taps_ref, mix_ref, modes_ref, mixed)
@@ -223,28 +229,31 @@
                 out_ref[inner + i * room + m] = jnp.zeros(out_ref.shape[1:], BF16)
 
 
-def over_kernel(reach, p_ref, l0_ref, l1_ref, core_ref, chip_ref, out_ref, blocks_ref, both, blocks):
+def over_kernel(reach, l0_ref, l1_ref, core_ref, chip_ref, out_ref, blocks_ref, both, blocks):
     gather_kernel(reach, core_ref, chip_ref, blocks, both)
-    total = p_ref[...]
     start = 0
+    total = None
     for l_ref in (l0_ref, l1_ref):
         count = l_ref.shape[1] // (2 * PITCH)
-        total = total + over(l_ref[...], blocks[start : start + count])
+        value = over(l_ref[...], blocks[start : start + count])
+        total = value if total is None else total + value
         start += count
     out_ref[...] = total
     blocks_ref[...] = blocks[start:]
 
 
 def over(rows, blocks):
-    value = dot(jnp.concatenate(halves(rows), axis=0), blocks.reshape(-1, blocks.shape[2]))
+    high = rows.astype(BF16).astype(F32)
+    value = dot(jnp.concatenate([high, rows - high], axis=0).astype(BF16), blocks.reshape(-1, blocks.shape[2]))
     half = rows.shape[0]
     return value[:half] + value[half:]
 
 
-def last_kernel(reach, p_ref, r_ref, blocks_ref, *rest):
+def last_kernel(reach, p_ref, r_ref, o_ref, blocks_ref, *rest):
     *refs, out_ref, total, l_ref, by, bz, mixed = rest
     rows_kernel(reach, True, p_ref, r_ref, *refs, total, l_ref, by, bz, mixed)
-    deliver(total[...] + over(l_ref[...], blocks_ref[...]), r_ref.shape[1], out_ref)
+    ends = o_ref[...] + over(l_ref[...], blocks_ref[...])
+    deliver(total[...] + dot(refs[7][...], stacked(ends)), r_ref.shape[1], out_ref)
 
 
 def deliver(total, channels, out_ref):
@@ -314,14 +323,15 @@
     each = LANES // (2 * PITCH)
     inner = width_x - 2 * reach
     small = [kernel_north.reshape(1, -1), kernel_east.reshape(1, -1), field_mixing, time_mixing]
-    t, s1, s2, *small = call(
-        functools.partial(turn_kernel, reach),
-        [raw, *small],
-        [full, slab, slab] + [(array.shape, F32) for array in small],
-        [pltpu.VMEM(raw.shape, F32), pltpu.SemaphoreType.DMA((1 + len(small),))],
+    s1, low, high, *small = call(
+        functools.partial(first_kernel, reach),
+        [raw, spatial_modes, *small],
+        [slab] + [((width_x, PITCH, modes), BF16)] * 2 + [(array.shape, F32) for array in small],
+        [pltpu.VMEM((channels, -(-reach // 8) * 8, width_y), F32), pltpu.SemaphoreType.DMA((3 + len(small),))],
         outside=True,
-        weight=3e9,
-    )
+        weight=3e8,
+    )
+    t, s2 = call(functools.partial(turn_kernel, reach), [raw, s1], [full, slab], weight=3e9)
     held = vmem(spatial_modes)
     r1 = lax.ppermute(s1, "gx", pairs(count_x, 0))
     r2 = lax.ppermute(s2, "gx", pairs(count_x, 1))
@@ -329,10 +339,10 @@
         functools.partial(band_kernel, reach),
         [small[0], t],
         [full, narrow, band, band, cross, cross],
-        weight=1e7,
+        weight=1e9,
     )
     block = ((reach, width_x, modes), F32)
-    core, chip = call(functools.partial(block_kernel, reach), [held], [block, block], weight=3e8)
+    core, chip = call(functools.partial(block_kernel, reach), [low, high], [block, block], weight=3e8)
     core = lax.ppermute(core, "gy", pairs(count_y, 0))
     chip = lax.ppermute(chip, "gy", pairs(count_y, 1))
     s, sz, mix, taps = call(
@@ -349,20 +359,20 @@
     p, l0 = call(
         functools.partial(tile_kernel, reach),
         [s, sz, mix, held],
-        [share, ((wide_rows, inner // each * LANES), F32)],
+        [share, ((channels, inner // each * LANES), F32)],
         weight=1e7,
     )
     both = [bh, bl, ch, cl, s, sz, taps, mix, held]
-    layer = (wide_rows, -(-reach // each) * LANES)
+    layer = (channels, -(-reach // each) * LANES)
     room = [pltpu.VMEM(slab[0], F32), pltpu.VMEM((reach, channels, LANES), F32), pltpu.VMEM((reach, wide_rows, width_y), BF16)]
     p, l1 = call(
         functools.partial(rows_kernel, reach, False), [p, r1, *both], [share, (layer, F32)], room, weight=1e9
     )
     slots = inner + 2 * (layer[1] // (2 * PITCH))
-    p, blocks = call(
+    ends, blocks = call(
         functools.partial(over_kernel, reach),
-        [p, l0, l1, core, chip],
-        [share, ((layer[1] // (2 * PITCH), 2 * PITCH, modes), BF16)],
+        [l0, l1, core, chip],
+        [((channels, modes), F32), ((layer[1] // (2 * PITCH), 2 * PITCH, modes), BF16)],
         [pltpu.VMEM((width_x, 2 * PITCH, modes), F32), pltpu.VMEM((slots, 2 * PITCH, modes), BF16)],
         weight=1e7,
     )
@@ -370,7 +380,7 @@
     high = 4 if rows % 4 == 0 else rows
     (out,) = call(
         functools.partial(last_kernel, reach),
-        [p, r2, blocks, *both],
+        [p, r2, ends, blocks, *both],
         [((count_x, count_y, rows // high, high, 128), F32)],
         [pltpu.VMEM(share[0], F32), pltpu.VMEM(layer, F32), *room],
     )

time: 32.7 us -> 32.7 us (level)
  Pallas kernels: 7.81 us -> 7.28 us
  blocking collectives: 16.8 us -> 17.2 us
    pallas_call x9 -> x10, Pallas kernels: 7.81 us -> 7.28 us  [call(): pl.pallas_call(body, out_shape=[make(shape, dtype) for shape, dtype in ou...]
    all_to_all x1, blocking collectives: 16.8 us -> 17.2 us  [local(): parts = lax.all_to_all(out, ('gx', 'gy'), 0, 0, tiled=True)]
where the time goes in v6:
time: 32.7 us; the launch traced here: 32.5 us
  blocking collectives  17.2 us (53%)
  Pallas kernels  7.28 us (22%)
  starting transfers between devices  6.98 us (21%)
  waiting for transfers between devices  0.88 us (3%)
    all_to_all x1, blocking collectives, local(): parts = lax.all_to_all(out, ('gx', 'gy'), 0, 0, tiled=True)  17.2 us
    pallas_call x10, Pallas kernels, call(): pl.pallas_call(body, out_shape=[make(shape, dtype) for shape, dtype in ou...  7.28 us
    ppermute x1, starting transfers between devices, local(): chip = lax.ppermute(chip, 'gy', pairs(count_y, 1))  3.05 us
    ppermute x1, starting transfers between devices, local(): r1 = lax.ppermute(s1, 'gx', pairs(count_x, 0))  2.11 us
    ppermute x1, starting transfers between devices, local(): core = lax.ppermute(core, 'gy', pairs(count_y, 0))  1.02 us
    ppermute x1, waiting for transfers between devices, local(): chip = lax.ppermute(chip, 'gy', pairs(count_y, 1))  0.85 us
    ppermute x1, starting transfers between devices, local(): r2 = lax.ppermute(s2, 'gx', pairs(count_x, 1))  0.81 us
  transfers between devices with their start and end apart: 4, of which 1 were waited for; matrix products, arithmetic and copies ran while one was open for 0% of the time, Pallas kernels for 13%

profile of v6, /device:TPU:1, one launch (start us, length us, event | category | flops | bytes accessed | tf_op | source)
XLA Modules:
  0.0 32.5 jit_solution(13345040872659915132)
XLA Ops:
  0.0 0.0 copy-start.1
  0.0 1.4 %shard_map.73 = (f32[10,24,256]{2,1,0:T(8,128)S(1)}, bf16[32,16,256]{2,1,0:T(8,128)(2,1)S(1)}, bf16[32,16,256]{2,1,0:T(8,128)(2,1)S(1)}, f32[1,21]{1,0:T(1,128)S...) custom-call(f32[24,32,256]{2,1,0:T(8,128)} %bitcast.7, bf16[32,256,256]{2,1,0:T(8,128)(2,1)} %rest_8_.1, ...), custom_call_target="tpu_custom_call" | custom-call | flops 300000000 | bytes 1048576 | tf_op jit(solution)/shard_map/pallas_call | solution.py:292
  1.4 2.1 %collective-permute-start = (f32[10,24,256]{2,1,0:T(8,128)S(1)}, f32[10,24,256]{2,1,0:T(8,128)S(1)}, u32[]{:S(2)}, u32[]{:S(2)}) collective-permute-start(f32[10,24,256]{2,1,0:T(8,128)S(1)} %get-tuple-element.36.before_ref), channel_id=1, source_target_pairs={{0,4},{4,0},{8,12},{12,8},{16,20},{20,16},{24,28},{28,24},{1,5},{5... | collective-permute-start | bytes 737288 | tf_op jit(solution)/shard_map/ppermute | solution.py:336
  3.5 0.2 shard_map.79
  3.7 1.0 %collective-permute-start.2 = (f32[10,32,256]{2,1,0:T(8,128)S(1)}, f32[10,32,256]{2,1,0:T(8,128)S(1)}, u32[]{:S(2)}, u32[]{:S(2)}) collective-permute-start(f32[10,32,256]{2,1,0:T(8,128)S(1)} %get-tuple-element.55), channel_id=1, source_target_pairs={{0,1},{1,0},{2,3},{3,2},{4,5},{5,4},{6,7},{7,6},{8,9},{9,8},{10,11... | collective-permute-start | bytes 983048 | tf_op jit(solution)/shard_map/ppermute | solution.py:346
  4.7 3.0 %collective-permute-start.3 = (f32[10,32,256]{2,1,0:T(8,128)S(1)}, f32[10,32,256]{2,1,0:T(8,128)S(1)}, u32[]{:S(2)}, u32[]{:S(2)}) collective-permute-start(f32[10,32,256]{2,1,0:T(8,128)S(1)} %get-tuple-element.56), channel_id=1, source_target_pairs={{1,2},{2,1},{5,6},{6,5},{9,10},{10,9},{13,14},{14,13},{17,18},{18,... | collective-permute-start | bytes 983048 | tf_op jit(solution)/shard_map/ppermute | solution.py:347
  7.8 0.0 copy-done.1
  7.8 0.2 shard_map.74
  7.9 0.0 copy-start
  7.9 0.8 %collective-permute-start.1 = (f32[10,24,256]{2,1,0:T(8,128)S(1)}, f32[10,24,256]{2,1,0:T(8,128)S(1)}, u32[]{:S(2)}, u32[]{:S(2)}) collective-permute-start(f32[10,24,256]{2,1,0:T(8,128)S(1)} %get-tuple-element.50), channel_id=1, source_target_pairs={{4,8},{8,4},{12,16},{16,12},{20,24},{24,20},{5,9},{9,5},{13,17},{1... | collective-permute-start | bytes 737288 | tf_op jit(solution)/shard_map/ppermute | solution.py:337
  8.8 1.1 %shard_map.75 = (f32[32,24,256]{2,1,0:T(8,128)S(1)}, f32[32,24,128]{2,1,0:T(8,128)S(1)}, bf16[256,256]{1,0:T(8,128)(2,1)S(1)}, bf16[256,256]{1,0:T(8,128)(2,1)S(...) custom-call(f32[1,21]{1,0:T(1,128)S(1)} %get-tuple-element.35.north_ref, ...), custom_call_target="tpu_custom_call" | custom-call | flops 1000000000 | bytes 1048576 | tf_op jit(solution)/shard_map/pallas_call | solution.py:292
  9.9 0.8 %shard_map.76 = (f32[32,24,256]{2,1,0:T(8,128)S(1)}, f32[32,24,128]{2,1,0:T(8,128)S(1)}, bf16[32,96]{1,0:T(8,128)(2,1)S(1)}, f32[21,8,256]{2,1,0:T(8,128)S(1)}) custom-call(f32[1,21]{1,0:T(1,128)S(1)} %get-tuple-element.32.east_ref, f32[4,4]{1,0:T(4,128)S(1)} %get-tuple-element.33.field_ref, f32[6,6]{1,0:T(8,128)S(1)} %get-tuple-element.34.time_ref, ...), custom_call_target="tpu_custom_call" | custom-call | flops 10000000 | bytes 1048576 | tf_op jit(solution)/shard_map/pallas_call | solution.py:292
  10.7 0.0 copy-done
  10.7 0.5 %shard_map.77 = (f32[32,256]{1,0:T(8,128)S(1)}, f32[24,384]{1,0:T(8,128)S(1)}) custom-call(f32[32,24,256]{2,1,0:T(8,128)S(1)} %get-tuple-element.40.s_ref.rest_4_, f32[32,24,128]{2,1,0:T(8,128)S(1)} %get-tuple-element.41.z_ref.rest_5_, bf16[32,96]{1,0:T(8,128)(2,1)S(1)} %get-tuple-element.42.mix_ref.rest_7_, bf16[32,256,256]{2,1,0:T(8,128)(2,1)S(1)} %copy-done), custom_call_target="tpu_custom_call" | custom-call | flops 10000000 | bytes 1048576 | tf_op jit(solution)/shard_map/pallas_call | solution.py:292
  11.2 0.0 collective-permute-done.r_ref
  11.2 1.0 %shard_map.78 = (f32[32,256]{1,0:T(8,128)S(1)}, f32[24,384]{1,0:T(8,128)S(1)}) custom-call(f32[32,256]{1,0:T(8,128)S(1)} %get-tuple-element.43.p_ref, f32[10,24,256]{2,1,0:T(8,128)S(1)} %collective-permute-done.r_ref, bf16[256,256]{1,0:T(8,128)(2,1)S(1)} %get-tuple-element.44.bh_ref.rest_0_, bf16[256,256]{1,0:T(8,128)(2,1)S(1)} %get-tuple-element.45.bl_ref.rest_1_, ...), custom_call_target="tpu_custom_call" | custom-call | flops 1000000000 | bytes 1048576 | tf_op jit(solution)/shard_map/pallas_call | solution.py:292
  12.2 0.0 copy-start.2
  12.2 0.0 collective-permute-done.2.core_ref
  12.2 0.8 %collective-permute-done.3.chip_ref = f32[10,32,256]{2,1,0:T(8,128)S(1)} collective-permute-done((f32[10,32,256]{2,1,0:T(8,128)S(1)}, f32[10,32,256]{2,1,0:T(8,128)S(1)}, u32[]{:S(2)}, u32[]{:S(2)}) %collective-permute-start.3) | collective-permute-done | bytes 327712 | tf_op jit(solution)/shard_map/ppermute | solution.py:347
  13.1 0.3 %shard_map.80 = (f32[24,256]{1,0:T(8,128)S(1)}, bf16[12,32,256]{2,1,0:T(8,128)(2,1)S(1)}) custom-call(f32[24,384]{1,0:T(8,128)S(1)} %get-tuple-element.51.l0_ref, f32[24,384]{1,0:T(8,128)S(1)} %get-tuple-element.52.l1_ref, f32[10,32,256]{2,1,0:T(8,128)S(1)} %collective-permute-done.2.core_ref, f32[10,32,256]{2,1,0:T(8,128)S(1)} %collective-permute-done.3.chip_ref), custom_call_target="tpu_custom_call" | custom-call | flops 10000000 | bytes 1048576 | tf_op jit(solution)/shard_map/pallas_call | solution.py:292
  13.4 0.0 collective-permute-done.1.r_ref
  13.4 1.1 %shard_map.81 = f32[8,4,3,4,128]{4,3,2,1,0:T(4,128)S(1)} custom-call(f32[32,256]{1,0:T(8,128)S(1)} %get-tuple-element.49.p_ref, f32[10,24,256]{2,1,0:T(8,128)S(1)} %collective-permute-done.1.r_ref, f32[24,256]{1,0:T(8,128)S(1)} %get-tuple-element.57.o_ref, bf16[12,32,256]{2,1,0:T(8,128)(2,1)S(1)} %get-tuple-element.58.blocks_ref, ...), custom_call_target="tpu_custom_call" | custom-call | flops 1000000000 | bytes 1048576 | tf_op jit(solution)/shard_map/pallas_call | solution.py:292
  14.6 17.2 %all_to_all.5.parts_ref = f32[32,3,4,128]{3,2,1,0:T(4,128)S(1)} all-to-all(f32[32,3,4,128]{3,2,1,0:T(4,128)S(1)} %bitcast.6), channel_id=1, replica_groups=mesh['gx'=8,'gy'=4] {'gx','gy'}, dimensions={0} | all-to-all | bytes 393216 | tf_op jit(solution)/shard_map/all_to_all | solution.py:388
  31.8 0.0 copy-done.2
  31.8 0.7 %shard_map.82 = f32[24,64]{1,0:T(8,128)} custom-call(f32[32,3,4,128]{3,2,1,0:T(4,128)S(1)} %all_to_all.5.parts_ref, f32[24,64]{1,0:T(8,128)S(1)} %bitcast.9), custom_call_target="tpu_custom_call" | custom-call | flops 1000000000 | bytes 1048576 | tf_op jit(solution)/shard_map/pallas_call | solution.py:292
Async XLA Ops:
  0.0 7.8 %copy-start.1 = (f32[4,6,32,256]{3,2,1,0:T(8,128)S(1)}, f32[4,6,32,256]{3,2,1,0:T(8,128)}, u32[]{:S(2)}) copy-start(f32[4,6,32,256]{3,2,1,0:T(8,128)} %param.7) | copy-start | bytes 2359300
  1.4 9.8 %collective-permute-start = (f32[10,24,256]{2,1,0:T(8,128)S(1)}, f32[10,24,256]{2,1,0:T(8,128)S(1)}, u32[]{:S(2)}, u32[]{:S(2)}) collective-permute-start(f32[10,24,256]{2,1,0:T(8,128)S(1)} %get-tuple-element.36.before_ref), channel_id=1, source_target_pairs={{0,4},{4,0},{8,12},{12,8},{16,20},{20,16},{24,28},{28,24},{1,5},{5... | collective-permute-start | bytes 737288 | tf_op jit(solution)/shard_map/ppermute | solution.py:336
  3.7 8.5 %collective-permute-start.2 = (f32[10,32,256]{2,1,0:T(8,128)S(1)}, f32[10,32,256]{2,1,0:T(8,128)S(1)}, u32[]{:S(2)}, u32[]{:S(2)}) collective-permute-start(f32[10,32,256]{2,1,0:T(8,128)S(1)} %get-tuple-element.55), channel_id=1, source_target_pairs={{0,1},{1,0},{2,3},{3,2},{4,5},{5,4},{6,7},{7,6},{8,9},{9,8},{10,11... | collective-permute-start | bytes 983048 | tf_op jit(solution)/shard_map/ppermute | solution.py:346
  4.7 8.4 %collective-permute-start.3 = (f32[10,32,256]{2,1,0:T(8,128)S(1)}, f32[10,32,256]{2,1,0:T(8,128)S(1)}, u32[]{:S(2)}, u32[]{:S(2)}) collective-permute-start(f32[10,32,256]{2,1,0:T(8,128)S(1)} %get-tuple-element.56), channel_id=1, source_target_pairs={{1,2},{2,1},{5,6},{6,5},{9,10},{10,9},{13,14},{14,13},{17,18},{18,... | collective-permute-start | bytes 983048 | tf_op jit(solution)/shard_map/ppermute | solution.py:347
  7.9 2.7 %copy-start = (bf16[32,256,256]{2,1,0:T(8,128)(2,1)S(1)}, bf16[32,256,256]{2,1,0:T(8,128)(2,1)}, u32[]{:S(2)}) copy-start(bf16[32,256,256]{2,1,0:T(8,128)(2,1)} %rest_8_.1) | copy-start | bytes 12582916
  7.9 5.5 %collective-permute-start.1 = (f32[10,24,256]{2,1,0:T(8,128)S(1)}, f32[10,24,256]{2,1,0:T(8,128)S(1)}, u32[]{:S(2)}, u32[]{:S(2)}) collective-permute-start(f32[10,24,256]{2,1,0:T(8,128)S(1)} %get-tuple-element.50), channel_id=1, source_target_pairs={{4,8},{8,4},{12,16},{16,12},{20,24},{24,20},{5,9},{9,5},{13,17},{1... | collective-permute-start | bytes 737288 | tf_op jit(solution)/shard_map/ppermute | solution.py:337
  12.2 19.6 %copy-start.2 = (f32[64,24]{0,1:T(8,128)S(1)}, f32[64,24]{0,1:T(8,128)}, u32[]{:S(2)}) copy-start(f32[64,24]{0,1:T(8,128)} %param.13) | copy-start | bytes 18436

commit v7 on v6

--- a/solution.py
+++ b/solution.py
@@ -47,17 +47,14 @@
     return jnp.concatenate(parts, axis=1).astype(BF16)
 
 
-def first_kernel(reach, a_hbm, modes_hbm, *refs):
-    count = (len(refs) - 5) // 2
-    small, s1_ref, ends, held = refs[:count], refs[count], refs[count + 1 : count + 3], refs[count + 3 : -2]
-    rows_ref, sem = refs[-2:]
-    window, width_x, width_y = rows_ref.shape[1], a_hbm.shape[1], a_hbm.shape[2]
+def first_kernel(reach, a_hbm, *refs):
+    count = (len(refs) - 3) // 2
+    small, s1_ref, held, (rows_ref, sem) = refs[:count], refs[count], refs[count + 1 : -2], refs[-2:]
+    window, width_x = rows_ref.shape[1], a_hbm.shape[1]
     odd = lax.axis_index("gx") % 2
     start = pl.multiple_of((1 - odd) * (width_x - window), 8)
-    pairs_of = [(a_hbm.at[:, pl.ds(start, window)], rows_ref)]
-    pairs_of += [(modes_hbm.at[:, pl.ds(i * (width_y - PITCH), PITCH)], ends[i]) for i in range(2)]
-    pairs_of += list(zip(small, held))
-    copies = [pltpu.make_async_copy(x, y, sem.at[i]) for i, (x, y) in enumerate(pairs_of)]
+    copies = [pltpu.make_async_copy(a_hbm.at[:, pl.ds(start, window)], rows_ref, sem.at[0])]
+    copies += [pltpu.make_async_copy(x, y, sem.at[i + 1]) for i, (x, y) in enumerate(zip(small, held))]
     for copy in copies:
         copy.start()
     for copy in copies:
@@ -72,10 +69,11 @@
     s2_ref[...] = t_ref[pl.ds(lax.axis_index("gx") % 2 * (t_ref.shape[0] - reach), reach)]
 
 
-def block_kernel(reach, low_ref, high_ref, core_ref, chip_ref):
+def block_kernel(reach, modes_ref, core_ref, chip_ref):
+    width_y = modes_ref.shape[1]
     odd = lax.axis_index("gy") % 2
-    low = jnp.swapaxes(low_ref[...].astype(F32), 0, 1)
-    high = jnp.swapaxes(high_ref[...].astype(F32), 0, 1)
+    low = jnp.swapaxes(modes_ref[:, :PITCH].astype(F32), 0, 1)
+    high = jnp.swapaxes(modes_ref[:, width_y - PITCH :].astype(F32), 0, 1)
     for i in range(reach):
         a, b = low[i], high[PITCH - reach + i]
         core_ref[i] = jnp.where(odd == 1, a, b)
@@ -323,15 +321,15 @@
     each = LANES // (2 * PITCH)
     inner = width_x - 2 * reach
     small = [kernel_north.reshape(1, -1), kernel_east.reshape(1, -1), field_mixing, time_mixing]
-    s1, low, high, *small = call(
+    s1, *small = call(
         functools.partial(first_kernel, reach),
-        [raw, spatial_modes, *small],
-        [slab] + [((width_x, PITCH, modes), BF16)] * 2 + [(array.shape, F32) for array in small],
-        [pltpu.VMEM((channels, -(-reach // 8) * 8, width_y), F32), pltpu.SemaphoreType.DMA((3 + len(small),))],
+        [raw, *small],
+        [slab] + [(array.shape, F32) for array in small],
+        [pltpu.VMEM((channels, -(-reach // 8) * 8, width_y), F32), pltpu.SemaphoreType.DMA((1 + len(small),))],
         outside=True,
-        weight=3e8,
-    )
-    t, s2 = call(functools.partial(turn_kernel, reach), [raw, s1], [full, slab], weight=3e9)
+        weight=3e9,
+    )
+    t, s2 = call(functools.partial(turn_kernel, reach), [raw, s1], [full, slab], weight=1e7)
     held = vmem(spatial_modes)
     r1 = lax.ppermute(s1, "gx", pairs(count_x, 0))
     r2 = lax.ppermute(s2, "gx", pairs(count_x, 1))
@@ -339,10 +337,10 @@
         functools.partial(band_kernel, reach),
         [small[0], t],
         [full, narrow, band, band, cross, cross],
-        weight=1e9,
+        weight=1e7,
     )
     block = ((reach, width_x, modes), F32)
-    core, chip = call(functools.partial(block_kernel, reach), [low, high], [block, block], weight=3e8)
+    core, chip = call(functools.partial(block_kernel, reach), [held], [block, block], weight=3e8)
     core = lax.ppermute(core, "gy", pairs(count_y, 0))
     chip = lax.ppermute(chip, "gy", pairs(count_y, 1))
     s, sz, mix, taps = call(

time: 32.7 us -> 32.4 us (level)
  no operation moved by 1% of the time
where the time goes in v7:
time: 32.4 us; the launch traced here: 32.2 us
  blocking collectives  17 us (52%)
  Pallas kernels  7.2 us (22%)
  starting transfers between devices  6.85 us (21%)
  waiting for transfers between devices  1.03 us (3%)
    all_to_all x1, blocking collectives, local(): parts = lax.all_to_all(out, ('gx', 'gy'), 0, 0, tiled=True)  17 us
    pallas_call x10, Pallas kernels, call(): pl.pallas_call(body, out_shape=[make(shape, dtype) for shape, dtype in ou...  7.2 us
    ppermute x1, starting transfers between devices, local(): chip = lax.ppermute(chip, 'gy', pairs(count_y, 1))  3.05 us
    ppermute x1, starting transfers between devices, local(): r1 = lax.ppermute(s1, 'gx', pairs(count_x, 0))  2.11 us
    ppermute x1, starting transfers between devices, local(): core = lax.ppermute(core, 'gy', pairs(count_y, 0))  1.02 us
    ppermute x1, waiting for transfers between devices, local(): chip = lax.ppermute(chip, 'gy', pairs(count_y, 1))  0.99 us
    ppermute x1, starting transfers between devices, local(): r2 = lax.ppermute(s2, 'gx', pairs(count_x, 1))  0.68 us
  transfers between devices with their start and end apart: 4, of which 1 were waited for; matrix products, arithmetic and copies ran while one was open for 0% of the time, Pallas kernels for 13%

profile of v7, /device:TPU:1, one launch (start us, length us, event | category | flops | bytes accessed | tf_op | source)
XLA Modules:
  0.0 32.2 jit_solution(18026883248365512341)
XLA Ops:
  0.0 0.0 copy-start
  0.0 1.3 %shard_map.73 = (f32[10,24,256]{2,1,0:T(8,128)S(1)}, f32[1,21]{1,0:T(1,128)S(1)}, f32[1,21]{1,0:T(1,128)S(1)}, f32[4,4]{1,0:T(4,128)S(1)}, f32[6,6]{1,0:T(8,128)S(1)}) custom-call(f32[24,32,256]{2,1,0:T(8,128)} %bitcast.7, f32[1,21]{1,0:T(1,128)} %bitcast.10, f32[1,21]{1,0:T(1,128)} %bitcast.11, f32[4,4]{1,0:T(4,128)} %refs_2_.1, f32[6,6]{1,0:T(8,128)} %refs_3_.1), custom_call_target="tpu_custom_call" | custom-call | flops 3000000000 | bytes 1048576 | tf_op jit(solution)/shard_map/pallas_call | solution.py:290
  1.3 0.0 copy-start.1
  1.3 2.1 %collective-permute-start = (f32[10,24,256]{2,1,0:T(8,128)S(1)}, f32[10,24,256]{2,1,0:T(8,128)S(1)}, u32[]{:S(2)}, u32[]{:S(2)}) collective-permute-start(f32[10,24,256]{2,1,0:T(8,128)S(1)} %get-tuple-element.34.before_ref), channel_id=1, source_target_pairs={{0,4},{4,0},{8,12},{12,8},{16,20},{20,16},{24,28},{28,24},{1,5},{5... | collective-permute-start | bytes 737288 | tf_op jit(solution)/shard_map/ppermute | solution.py:334
  3.4 0.0 copy-done
  3.4 0.2 shard_map.79
  3.6 1.0 %collective-permute-start.2 = (f32[10,32,256]{2,1,0:T(8,128)S(1)}, f32[10,32,256]{2,1,0:T(8,128)S(1)}, u32[]{:S(2)}, u32[]{:S(2)}) collective-permute-start(f32[10,32,256]{2,1,0:T(8,128)S(1)} %get-tuple-element.51), channel_id=1, source_target_pairs={{0,1},{1,0},{2,3},{3,2},{4,5},{5,4},{6,7},{7,6},{8,9},{9,8},{10,11... | collective-permute-start | bytes 983048 | tf_op jit(solution)/shard_map/ppermute | solution.py:344
  4.6 3.0 %collective-permute-start.3 = (f32[10,32,256]{2,1,0:T(8,128)S(1)}, f32[10,32,256]{2,1,0:T(8,128)S(1)}, u32[]{:S(2)}, u32[]{:S(2)}) collective-permute-start(f32[10,32,256]{2,1,0:T(8,128)S(1)} %get-tuple-element.52), channel_id=1, source_target_pairs={{1,2},{2,1},{5,6},{6,5},{9,10},{10,9},{13,14},{14,13},{17,18},{18,... | collective-permute-start | bytes 983048 | tf_op jit(solution)/shard_map/ppermute | solution.py:345
  7.7 0.0 copy-done.1
  7.7 0.2 shard_map.74
  7.9 0.7 %collective-permute-start.1 = (f32[10,24,256]{2,1,0:T(8,128)S(1)}, f32[10,24,256]{2,1,0:T(8,128)S(1)}, u32[]{:S(2)}, u32[]{:S(2)}) collective-permute-start(f32[10,24,256]{2,1,0:T(8,128)S(1)} %get-tuple-element.48), channel_id=1, source_target_pairs={{4,8},{8,4},{12,16},{16,12},{20,24},{24,20},{5,9},{9,5},{13,17},{1... | collective-permute-start | bytes 737288 | tf_op jit(solution)/shard_map/ppermute | solution.py:335
  8.5 1.1 %shard_map.75 = (f32[32,24,256]{2,1,0:T(8,128)S(1)}, f32[32,24,128]{2,1,0:T(8,128)S(1)}, bf16[256,256]{1,0:T(8,128)(2,1)S(1)}, bf16[256,256]{1,0:T(8,128)(2,1)S(...) custom-call(f32[1,21]{1,0:T(1,128)S(1)} %get-tuple-element.33.north_ref, ...), custom_call_target="tpu_custom_call" | custom-call | flops 10000000 | bytes 1048576 | tf_op jit(solution)/shard_map/pallas_call | solution.py:290
  9.6 0.8 %shard_map.76 = (f32[32,24,256]{2,1,0:T(8,128)S(1)}, f32[32,24,128]{2,1,0:T(8,128)S(1)}, bf16[32,96]{1,0:T(8,128)(2,1)S(1)}, f32[21,8,256]{2,1,0:T(8,128)S(1)}) custom-call(f32[1,21]{1,0:T(1,128)S(1)} %get-tuple-element.30.east_ref, f32[4,4]{1,0:T(4,128)S(1)} %get-tuple-element.31.field_ref, f32[6,6]{1,0:T(8,128)S(1)} %get-tuple-element.32.time_ref, ...), custom_call_target="tpu_custom_call" | custom-call | flops 10000000 | bytes 1048576 | tf_op jit(solution)/shard_map/pallas_call | solution.py:290
  10.4 0.5 %shard_map.77 = (f32[32,256]{1,0:T(8,128)S(1)}, f32[24,384]{1,0:T(8,128)S(1)}) custom-call(f32[32,24,256]{2,1,0:T(8,128)S(1)} %get-tuple-element.38.s_ref.rest_4_, f32[32,24,128]{2,1,0:T(8,128)S(1)} %get-tuple-element.39.z_ref.rest_5_, bf16[32,96]{1,0:T(8,128)(2,1)S(1)} %get-tuple-element.40.mix_ref.rest_7_, bf16[32,256,256]{2,1,0:T(8,128)(2,1)S(1)} %copy-done), custom_call_target="tpu_custom_call" | custom-call | flops 10000000 | bytes 1048576 | tf_op jit(solution)/shard_map/pallas_call | solution.py:290
  10.9 0.0 collective-permute-done.r_ref
  11.0 1.0 %shard_map.78 = (f32[32,256]{1,0:T(8,128)S(1)}, f32[24,384]{1,0:T(8,128)S(1)}) custom-call(f32[32,256]{1,0:T(8,128)S(1)} %get-tuple-element.41.p_ref, f32[10,24,256]{2,1,0:T(8,128)S(1)} %collective-permute-done.r_ref, bf16[256,256]{1,0:T(8,128)(2,1)S(1)} %get-tuple-element.42.bh_ref.rest_0_, bf16[256,256]{1,0:T(8,128)(2,1)S(1)} %get-tuple-element.43.bl_ref.rest_1_, ...), custom_call_target="tpu_custom_call" | custom-call | flops 1000000000 | bytes 1048576 | tf_op jit(solution)/shard_map/pallas_call | solution.py:290
  12.0 0.0 copy-start.2
  12.0 0.0 collective-permute-done.2.core_ref
  12.0 1.0 %collective-permute-done.3.chip_ref = f32[10,32,256]{2,1,0:T(8,128)S(1)} collective-permute-done((f32[10,32,256]{2,1,0:T(8,128)S(1)}, f32[10,32,256]{2,1,0:T(8,128)S(1)}, u32[]{:S(2)}, u32[]{:S(2)}) %collective-permute-start.3) | collective-permute-done | bytes 327712 | tf_op jit(solution)/shard_map/ppermute | solution.py:345
  13.0 0.3 %shard_map.80 = (f32[24,256]{1,0:T(8,128)S(1)}, bf16[12,32,256]{2,1,0:T(8,128)(2,1)S(1)}) custom-call(f32[24,384]{1,0:T(8,128)S(1)} %get-tuple-element.49.l0_ref, f32[24,384]{1,0:T(8,128)S(1)} %get-tuple-element.50.l1_ref, f32[10,32,256]{2,1,0:T(8,128)S(1)} %collective-permute-done.2.core_ref, f32[10,32,256]{2,1,0:T(8,128)S(1)} %collective-permute-done.3.chip_ref), custom_call_target="tpu_custom_call" | custom-call | flops 10000000 | bytes 1048576 | tf_op jit(solution)/shard_map/pallas_call | solution.py:290
  13.4 0.0 collective-permute-done.1.r_ref
  13.4 1.1 %shard_map.81 = f32[8,4,3,4,128]{4,3,2,1,0:T(4,128)S(1)} custom-call(f32[32,256]{1,0:T(8,128)S(1)} %get-tuple-element.47.p_ref, f32[10,24,256]{2,1,0:T(8,128)S(1)} %collective-permute-done.1.r_ref, f32[24,256]{1,0:T(8,128)S(1)} %get-tuple-element.53.o_ref, bf16[12,32,256]{2,1,0:T(8,128)(2,1)S(1)} %get-tuple-element.54.blocks_ref, ...), custom_call_target="tpu_custom_call" | custom-call | flops 1000000000 | bytes 1048576 | tf_op jit(solution)/shard_map/pallas_call | solution.py:290
  14.5 17.0 %all_to_all.5.parts_ref = f32[32,3,4,128]{3,2,1,0:T(4,128)S(1)} all-to-all(f32[32,3,4,128]{3,2,1,0:T(4,128)S(1)} %bitcast.6), channel_id=1, replica_groups=mesh['gx'=8,'gy'=4] {'gx','gy'}, dimensions={0} | all-to-all | bytes 393216 | tf_op jit(solution)/shard_map/all_to_all | solution.py:386
  31.4 0.0 copy-done.2
  31.5 0.7 %shard_map.82 = f32[24,64]{1,0:T(8,128)} custom-call(f32[32,3,4,128]{3,2,1,0:T(4,128)S(1)} %all_to_all.5.parts_ref, f32[24,64]{1,0:T(8,128)S(1)} %bitcast.9), custom_call_target="tpu_custom_call" | custom-call | flops 1000000000 | bytes 1048576 | tf_op jit(solution)/shard_map/pallas_call | solution.py:290
Async XLA Ops:
  0.0 3.4 %copy-start = (bf16[32,256,256]{2,1,0:T(8,128)(2,1)S(1)}, bf16[32,256,256]{2,1,0:T(8,128)(2,1)}, u32[]{:S(2)}) copy-start(bf16[32,256,256]{2,1,0:T(8,128)(2,1)} %rest_8_.1) | copy-start | bytes 12582916
  1.3 6.4 %copy-start.1 = (f32[4,6,32,256]{3,2,1,0:T(8,128)S(1)}, f32[4,6,32,256]{3,2,1,0:T(8,128)}, u32[]{:S(2)}) copy-start(f32[4,6,32,256]{3,2,1,0:T(8,128)} %param.7) | copy-start | bytes 2359300
  1.3 9.7 %collective-permute-start = (f32[10,24,256]{2,1,0:T(8,128)S(1)}, f32[10,24,256]{2,1,0:T(8,128)S(1)}, u32[]{:S(2)}, u32[]{:S(2)}) collective-permute-start(f32[10,24,256]{2,1,0:T(8,128)S(1)} %get-tuple-element.34.before_ref), channel_id=1, source_target_pairs={{0,4},{4,0},{8,12},{12,8},{16,20},{20,16},{24,28},{28,24},{1,5},{5... | collective-permute-start | bytes 737288 | tf_op jit(solution)/shard_map/ppermute | solution.py:334
  3.6 8.4 %collective-permute-start.2 = (f32[10,32,256]{2,1,0:T(8,128)S(1)}, f32[10,32,256]{2,1,0:T(8,128)S(1)}, u32[]{:S(2)}, u32[]{:S(2)}) collective-permute-start(f32[10,32,256]{2,1,0:T(8,128)S(1)} %get-tuple-element.51), channel_id=1, source_target_pairs={{0,1},{1,0},{2,3},{3,2},{4,5},{5,4},{6,7},{7,6},{8,9},{9,8},{10,11... | collective-permute-start | bytes 983048 | tf_op jit(solution)/shard_map/ppermute | solution.py:344
  4.6 8.4 %collective-permute-start.3 = (f32[10,32,256]{2,1,0:T(8,128)S(1)}, f32[10,32,256]{2,1,0:T(8,128)S(1)}, u32[]{:S(2)}, u32[]{:S(2)}) collective-permute-start(f32[10,32,256]{2,1,0:T(8,128)S(1)} %get-tuple-element.52), channel_id=1, source_target_pairs={{1,2},{2,1},{5,6},{6,5},{9,10},{10,9},{13,14},{14,13},{17,18},{18,... | collective-permute-start | bytes 983048 | tf_op jit(solution)/shard_map/ppermute | solution.py:345
  7.9 5.5 %collective-permute-start.1 = (f32[10,24,256]{2,1,0:T(8,128)S(1)}, f32[10,24,256]{2,1,0:T(8,128)S(1)}, u32[]{:S(2)}, u32[]{:S(2)}) collective-permute-start(f32[10,24,256]{2,1,0:T(8,128)S(1)} %get-tuple-element.48), channel_id=1, source_target_pairs={{4,8},{8,4},{12,16},{16,12},{20,24},{24,20},{5,9},{9,5},{13,17},{1... | collective-permute-start | bytes 737288 | tf_op jit(solution)/shard_map/ppermute | solution.py:335
  12.0 19.5 %copy-start.2 = (f32[64,24]{0,1:T(8,128)S(1)}, f32[64,24]{0,1:T(8,128)}, u32[]{:S(2)}) copy-start(f32[64,24]{0,1:T(8,128)} %param.13) | copy-start | bytes 18436

commit v8 on v7

--- a/solution.py
+++ b/solution.py
@@ -48,19 +48,33 @@
 
 
 def first_kernel(reach, a_hbm, *refs):
-    count = (len(refs) - 3) // 2
-    small, s1_ref, held, (rows_ref, sem) = refs[:count], refs[count], refs[count + 1 : -2], refs[-2:]
-    window, width_x = rows_ref.shape[1], a_hbm.shape[1]
+    count = (len(refs) - 2) // 2
+    small, s1_ref, held, sem = refs[:count], refs[count], refs[count + 1 : -1], refs[-1]
     odd = lax.axis_index("gx") % 2
-    start = pl.multiple_of((1 - odd) * (width_x - window), 8)
-    copies = [pltpu.make_async_copy(a_hbm.at[:, pl.ds(start, window)], rows_ref, sem.at[0])]
-    copies += [pltpu.make_async_copy(x, y, sem.at[i + 1]) for i, (x, y) in enumerate(zip(small, held))]
+    far = a_hbm.shape[1] - reach
+    copies = [pltpu.make_async_copy(x, y, sem.at[i]) for i, (x, y) in enumerate(zip(small, held))]
+
+    def rows(start):
+        return [pltpu.make_async_copy(a_hbm.at[:, start + n], s1_ref.at[n], sem.at[count + n]) for n in range(reach)]
+
+    for left in range(2):
+
+        @pl.when(odd == left)
+        def _():
+            for copy in rows((1 - left) * far):
+                copy.start()
+
     for copy in copies:
         copy.start()
+    for left in range(2):
+
+        @pl.when(odd == left)
+        def _():
+            for copy in rows((1 - left) * far):
+                copy.wait()
+
     for copy in copies:
         copy.wait()
-    rows = jnp.swapaxes(rows_ref[...], 0, 1)
-    s1_ref[...] = jnp.where(odd == 1, rows[:reach], rows[window - reach :])
 
 
 def turn_kernel(reach, a_ref, before_ref, t_ref, s2_ref):
@@ -325,7 +339,7 @@
         functools.partial(first_kernel, reach),
         [raw, *small],
         [slab] + [(array.shape, F32) for array in small],
-        [pltpu.VMEM((channels, -(-reach // 8) * 8, width_y), F32), pltpu.SemaphoreType.DMA((1 + len(small),))],
+        [pltpu.SemaphoreType.DMA((reach + len(small),))],
         outside=True,
         weight=3e9,
     )

time: 32.4 us -> 32.3 us (level)
  no operation moved by 1% of the time
where the time goes in v8:
time: 32.3 us; the launch traced here: 32.1 us
  blocking collectives  17 us (53%)
  Pallas kernels  7.08 us (22%)
  starting transfers between devices  6.85 us (21%)
  waiting for transfers between devices  1.03 us (3%)
    all_to_all x1, blocking collectives, local(): parts = lax.all_to_all(out, ('gx', 'gy'), 0, 0, tiled=True)  17 us
    pallas_call x10, Pallas kernels, call(): pl.pallas_call(body, out_shape=[make(shape, dtype) for shape, dtype in ou...  7.08 us
    ppermute x1, starting transfers between devices, local(): chip = lax.ppermute(chip, 'gy', pairs(count_y, 1))  3.05 us
    ppermute x1, starting transfers between devices, local(): r1 = lax.ppermute(s1, 'gx', pairs(count_x, 0))  2.11 us
    ppermute x1, starting transfers between devices, local(): core = lax.ppermute(core, 'gy', pairs(count_y, 0))  1.02 us
    ppermute x1, waiting for transfers between devices, local(): chip = lax.ppermute(chip, 'gy', pairs(count_y, 1))  0.99 us
    ppermute x1, starting transfers between devices, local(): r2 = lax.ppermute(s2, 'gx', pairs(count_x, 1))  0.68 us
  transfers between devices with their start and end apart: 4, of which 1 were waited for; matrix products, arithmetic and copies ran while one was open for 0% of the time, Pallas kernels for 13%

profile of v8, /device:TPU:1, one launch (start us, length us, event | category | flops | bytes accessed | tf_op | source)
XLA Modules:
  0.0 32.1 jit_solution(1543859206195809420)
XLA Ops:
  0.0 0.0 copy-start
  0.0 1.2 %shard_map.73 = (f32[10,24,256]{2,1,0:T(8,128)S(1)}, f32[1,21]{1,0:T(1,128)S(1)}, f32[1,21]{1,0:T(1,128)S(1)}, f32[4,4]{1,0:T(4,128)S(1)}, f32[6,6]{1,0:T(8,128)S(1)}) custom-call(f32[24,32,256]{2,1,0:T(8,128)} %bitcast.7, f32[1,21]{1,0:T(1,128)} %bitcast.10, f32[1,21]{1,0:T(1,128)} %bitcast.11, f32[4,4]{1,0:T(4,128)} %refs_2_.1, f32[6,6]{1,0:T(8,128)} %refs_3_.1), custom_call_target="tpu_custom_call" | custom-call | flops 3000000000 | bytes 1048576 | tf_op jit(solution)/shard_map/pallas_call | solution.py:304
  1.2 0.0 copy-start.1
  1.2 2.1 %collective-permute-start = (f32[10,24,256]{2,1,0:T(8,128)S(1)}, f32[10,24,256]{2,1,0:T(8,128)S(1)}, u32[]{:S(2)}, u32[]{:S(2)}) collective-permute-start(f32[10,24,256]{2,1,0:T(8,128)S(1)} %get-tuple-element.34.before_ref), channel_id=1, source_target_pairs={{0,4},{4,0},{8,12},{12,8},{16,20},{20,16},{24,28},{28,24},{1,5},{5... | collective-permute-start | bytes 737288 | tf_op jit(solution)/shard_map/ppermute | solution.py:348
  3.3 0.0 copy-done
  3.3 0.2 shard_map.79
  3.5 1.0 %collective-permute-start.2 = (f32[10,32,256]{2,1,0:T(8,128)S(1)}, f32[10,32,256]{2,1,0:T(8,128)S(1)}, u32[]{:S(2)}, u32[]{:S(2)}) collective-permute-start(f32[10,32,256]{2,1,0:T(8,128)S(1)} %get-tuple-element.51), channel_id=1, source_target_pairs={{0,1},{1,0},{2,3},{3,2},{4,5},{5,4},{6,7},{7,6},{8,9},{9,8},{10,11... | collective-permute-start | bytes 983048 | tf_op jit(solution)/shard_map/ppermute | solution.py:358
  4.5 3.0 %collective-permute-start.3 = (f32[10,32,256]{2,1,0:T(8,128)S(1)}, f32[10,32,256]{2,1,0:T(8,128)S(1)}, u32[]{:S(2)}, u32[]{:S(2)}) collective-permute-start(f32[10,32,256]{2,1,0:T(8,128)S(1)} %get-tuple-element.52), channel_id=1, source_target_pairs={{1,2},{2,1},{5,6},{6,5},{9,10},{10,9},{13,14},{14,13},{17,18},{18,... | collective-permute-start | bytes 983048 | tf_op jit(solution)/shard_map/ppermute | solution.py:359
  7.6 0.0 copy-done.1
  7.6 0.2 shard_map.74
  7.7 0.7 %collective-permute-start.1 = (f32[10,24,256]{2,1,0:T(8,128)S(1)}, f32[10,24,256]{2,1,0:T(8,128)S(1)}, u32[]{:S(2)}, u32[]{:S(2)}) collective-permute-start(f32[10,24,256]{2,1,0:T(8,128)S(1)} %get-tuple-element.48), channel_id=1, source_target_pairs={{4,8},{8,4},{12,16},{16,12},{20,24},{24,20},{5,9},{9,5},{13,17},{1... | collective-permute-start | bytes 737288 | tf_op jit(solution)/shard_map/ppermute | solution.py:349
  8.4 1.1 %shard_map.75 = (f32[32,24,256]{2,1,0:T(8,128)S(1)}, f32[32,24,128]{2,1,0:T(8,128)S(1)}, bf16[256,256]{1,0:T(8,128)(2,1)S(1)}, bf16[256,256]{1,0:T(8,128)(2,1)S(...) custom-call(f32[1,21]{1,0:T(1,128)S(1)} %get-tuple-element.33.north_ref, ...), custom_call_target="tpu_custom_call" | custom-call | flops 10000000 | bytes 1048576 | tf_op jit(solution)/shard_map/pallas_call | solution.py:304
  9.5 0.8 %shard_map.76 = (f32[32,24,256]{2,1,0:T(8,128)S(1)}, f32[32,24,128]{2,1,0:T(8,128)S(1)}, bf16[32,96]{1,0:T(8,128)(2,1)S(1)}, f32[21,8,256]{2,1,0:T(8,128)S(1)}) custom-call(f32[1,21]{1,0:T(1,128)S(1)} %get-tuple-element.30.east_ref, f32[4,4]{1,0:T(4,128)S(1)} %get-tuple-element.31.field_ref, f32[6,6]{1,0:T(8,128)S(1)} %get-tuple-element.32.time_ref, ...), custom_call_target="tpu_custom_call" | custom-call | flops 10000000 | bytes 1048576 | tf_op jit(solution)/shard_map/pallas_call | solution.py:304
  10.3 0.5 %shard_map.77 = (f32[32,256]{1,0:T(8,128)S(1)}, f32[24,384]{1,0:T(8,128)S(1)}) custom-call(f32[32,24,256]{2,1,0:T(8,128)S(1)} %get-tuple-element.38.s_ref.rest_4_, f32[32,24,128]{2,1,0:T(8,128)S(1)} %get-tuple-element.39.z_ref.rest_5_, bf16[32,96]{1,0:T(8,128)(2,1)S(1)} %get-tuple-element.40.mix_ref.rest_7_, bf16[32,256,256]{2,1,0:T(8,128)(2,1)S(1)} %copy-done), custom_call_target="tpu_custom_call" | custom-call | flops 10000000 | bytes 1048576 | tf_op jit(solution)/shard_map/pallas_call | solution.py:304
  10.8 0.0 collective-permute-done.r_ref
  10.9 1.0 %shard_map.78 = (f32[32,256]{1,0:T(8,128)S(1)}, f32[24,384]{1,0:T(8,128)S(1)}) custom-call(f32[32,256]{1,0:T(8,128)S(1)} %get-tuple-element.41.p_ref, f32[10,24,256]{2,1,0:T(8,128)S(1)} %collective-permute-done.r_ref, bf16[256,256]{1,0:T(8,128)(2,1)S(1)} %get-tuple-element.42.bh_ref.rest_0_, bf16[256,256]{1,0:T(8,128)(2,1)S(1)} %get-tuple-element.43.bl_ref.rest_1_, ...), custom_call_target="tpu_custom_call" | custom-call | flops 1000000000 | bytes 1048576 | tf_op jit(solution)/shard_map/pallas_call | solution.py:304
  11.9 0.0 copy-start.2
  11.9 0.0 collective-permute-done.2.core_ref
  11.9 1.0 %collective-permute-done.3.chip_ref = f32[10,32,256]{2,1,0:T(8,128)S(1)} collective-permute-done((f32[10,32,256]{2,1,0:T(8,128)S(1)}, f32[10,32,256]{2,1,0:T(8,128)S(1)}, u32[]{:S(2)}, u32[]{:S(2)}) %collective-permute-start.3) | collective-permute-done | bytes 327712 | tf_op jit(solution)/shard_map/ppermute | solution.py:359
  12.9 0.3 %shard_map.80 = (f32[24,256]{1,0:T(8,128)S(1)}, bf16[12,32,256]{2,1,0:T(8,128)(2,1)S(1)}) custom-call(f32[24,384]{1,0:T(8,128)S(1)} %get-tuple-element.49.l0_ref, f32[24,384]{1,0:T(8,128)S(1)} %get-tuple-element.50.l1_ref, f32[10,32,256]{2,1,0:T(8,128)S(1)} %collective-permute-done.2.core_ref, f32[10,32,256]{2,1,0:T(8,128)S(1)} %collective-permute-done.3.chip_ref), custom_call_target="tpu_custom_call" | custom-call | flops 10000000 | bytes 1048576 | tf_op jit(solution)/shard_map/pallas_call | solution.py:304
  13.2 0.0 collective-permute-done.1.r_ref
  13.3 1.1 %shard_map.81 = f32[8,4,3,4,128]{4,3,2,1,0:T(4,128)S(1)} custom-call(f32[32,256]{1,0:T(8,128)S(1)} %get-tuple-element.47.p_ref, f32[10,24,256]{2,1,0:T(8,128)S(1)} %collective-permute-done.1.r_ref, f32[24,256]{1,0:T(8,128)S(1)} %get-tuple-element.53.o_ref, bf16[12,32,256]{2,1,0:T(8,128)(2,1)S(1)} %get-tuple-element.54.blocks_ref, ...), custom_call_target="tpu_custom_call" | custom-call | flops 1000000000 | bytes 1048576 | tf_op jit(solution)/shard_map/pallas_call | solution.py:304
  14.4 17.0 %all_to_all.5.parts_ref = f32[32,3,4,128]{3,2,1,0:T(4,128)S(1)} all-to-all(f32[32,3,4,128]{3,2,1,0:T(4,128)S(1)} %bitcast.6), channel_id=1, replica_groups=mesh['gx'=8,'gy'=4] {'gx','gy'}, dimensions={0} | all-to-all | bytes 393216 | tf_op jit(solution)/shard_map/all_to_all | solution.py:400
  31.3 0.0 copy-done.2
  31.3 0.7 %shard_map.82 = f32[24,64]{1,0:T(8,128)} custom-call(f32[32,3,4,128]{3,2,1,0:T(4,128)S(1)} %all_to_all.5.parts_ref, f32[24,64]{1,0:T(8,128)S(1)} %bitcast.9), custom_call_target="tpu_custom_call" | custom-call | flops 1000000000 | bytes 1048576 | tf_op jit(solution)/shard_map/pallas_call | solution.py:304
Async XLA Ops:
  0.0 3.3 %copy-start = (bf16[32,256,256]{2,1,0:T(8,128)(2,1)S(1)}, bf16[32,256,256]{2,1,0:T(8,128)(2,1)}, u32[]{:S(2)}) copy-start(bf16[32,256,256]{2,1,0:T(8,128)(2,1)} %rest_8_.1) | copy-start | bytes 12582916
  1.2 6.4 %copy-start.1 = (f32[4,6,32,256]{3,2,1,0:T(8,128)S(1)}, f32[4,6,32,256]{3,2,1,0:T(8,128)}, u32[]{:S(2)}) copy-start(f32[4,6,32,256]{3,2,1,0:T(8,128)} %param.7) | copy-start | bytes 2359300
  1.2 9.7 %collective-permute-start = (f32[10,24,256]{2,1,0:T(8,128)S(1)}, f32[10,24,256]{2,1,0:T(8,128)S(1)}, u32[]{:S(2)}, u32[]{:S(2)}) collective-permute-start(f32[10,24,256]{2,1,0:T(8,128)S(1)} %get-tuple-element.34.before_ref), channel_id=1, source_target_pairs={{0,4},{4,0},{8,12},{12,8},{16,20},{20,16},{24,28},{28,24},{1,5},{5... | collective-permute-start | bytes 737288 | tf_op jit(solution)/shard_map/ppermute | solution.py:348
  3.5 8.4 %collective-permute-start.2 = (f32[10,32,256]{2,1,0:T(8,128)S(1)}, f32[10,32,256]{2,1,0:T(8,128)S(1)}, u32[]{:S(2)}, u32[]{:S(2)}) collective-permute-start(f32[10,32,256]{2,1,0:T(8,128)S(1)} %get-tuple-element.51), channel_id=1, source_target_pairs={{0,1},{1,0},{2,3},{3,2},{4,5},{5,4},{6,7},{7,6},{8,9},{9,8},{10,11... | collective-permute-start | bytes 983048 | tf_op jit(solution)/shard_map/ppermute | solution.py:358
  4.5 8.4 %collective-permute-start.3 = (f32[10,32,256]{2,1,0:T(8,128)S(1)}, f32[10,32,256]{2,1,0:T(8,128)S(1)}, u32[]{:S(2)}, u32[]{:S(2)}) collective-permute-start(f32[10,32,256]{2,1,0:T(8,128)S(1)} %get-tuple-element.52), channel_id=1, source_target_pairs={{1,2},{2,1},{5,6},{6,5},{9,10},{10,9},{13,14},{14,13},{17,18},{18,... | collective-permute-start | bytes 983048 | tf_op jit(solution)/shard_map/ppermute | solution.py:359
  7.7 5.5 %collective-permute-start.1 = (f32[10,24,256]{2,1,0:T(8,128)S(1)}, f32[10,24,256]{2,1,0:T(8,128)S(1)}, u32[]{:S(2)}, u32[]{:S(2)}) collective-permute-start(f32[10,24,256]{2,1,0:T(8,128)S(1)} %get-tuple-element.48), channel_id=1, source_target_pairs={{4,8},{8,4},{12,16},{16,12},{20,24},{24,20},{5,9},{9,5},{13,17},{1... | collective-permute-start | bytes 737288 | tf_op jit(solution)/shard_map/ppermute | solution.py:349
  11.9 19.5 %copy-start.2 = (f32[64,24]{0,1:T(8,128)S(1)}, f32[64,24]{0,1:T(8,128)}, u32[]{:S(2)}) copy-start(f32[64,24]{0,1:T(8,128)} %param.13) | copy-start | bytes 18436

commit v9 on v8

--- a/solution.py
+++ b/solution.py
@@ -188,38 +188,28 @@
     return value.reshape(count, lanes)
 
 
-def side(reach, left, rows, s_ref, taps_ref, mix_ref, modes_ref, mixed):
+def rows_kernel(
+    reach, second, p_ref, r_ref, bh_ref, bl_ref, ch_ref, cl_ref, s_ref, z_ref, taps_ref, mix_ref, modes_ref, out_ref, l_ref, by, mixed
+):
     width_x, channels, width_y = s_ref.shape
+    odd = lax.axis_index("gx") % 2
+    left = 1 - odd if second else odd
+    for m in range(reach):
+        by[m] = added(reach, left, r_ref, taps_ref, m, channels, width_y)
+    rows = halves(by[...].reshape(reach * channels, width_y))
+    here = dot2(rows, (bh_ref[...], bl_ref[...])).reshape(by.shape)
     mix = mix_ref[...]
     for m in range(reach):
-        value = s_ref[place(reach, left, width_x, m)] + added(reach, left, rows, taps_ref, m, channels, width_y)
-        mixed[m] = dot(mix, stacked(value)).astype(BF16)
+        mixed[m] = dot(mix, stacked(s_ref[place(reach, left, width_x, m)] + here[m])).astype(BF16)
+    over = dot2(rows, (ch_ref[...], cl_ref[...])).reshape(reach, channels, LANES)
+    over = [z_ref[place(reach, left, width_x, m)] + over[m] for m in range(reach)]
+    over += [jnp.zeros(over[0].shape, F32)] * (-reach % (LANES // (2 * PITCH)))
+    packed(l_ref, over)
     total = None
     for m in range(reach):
         term = dot(mixed[m], modes_ref[place(reach, left, width_x, m)])
         total = term if total is None else total + term
-    return total
-
-
-def smoothed(r_ref, wide_ref, high_ref, low_ref):
-    rows = halves(r_ref[...].reshape(-1, r_ref.shape[2]))
-    return dot2(rows, (high_ref[...], low_ref[...])).reshape(wide_ref.shape)
-
-
-def rows_kernel(
-    reach, second, p_ref, r_ref, bh_ref, bl_ref, ch_ref, cl_ref, s_ref, z_ref, taps_ref, mix_ref, modes_ref, out_ref, l_ref, by, bz, mixed
-):
-    width_x, channels, _ = s_ref.shape
-    odd = lax.axis_index("gx") % 2
-    left = 1 - odd if second else odd
-    by[...] = smoothed(r_ref, by, bh_ref, bl_ref)
-    bz[...] = smoothed(r_ref, bz, ch_ref, cl_ref)
-    over = []
-    for m in range(reach):
-        over.append(z_ref[place(reach, left, width_x, m)] + added(reach, left, bz, taps_ref, m, channels, LANES))
-    over += [jnp.zeros(over[0].shape, F32)] * (-reach % (LANES // (2 * PITCH)))
-    packed(l_ref, over)
-    out_ref[...] = p_ref[...] + side(reach, left, by, s_ref, taps_ref, mix_ref, modes_ref, mixed)
+    out_ref[...] = p_ref[...] + total
 
 
 def gather_kernel(reach, core_ref, chip_ref, out_ref, both):
@@ -262,8 +252,8 @@
 
 
 def last_kernel(reach, p_ref, r_ref, o_ref, blocks_ref, *rest):
-    *refs, out_ref, total, l_ref, by, bz, mixed = rest
-    rows_kernel(reach, True, p_ref, r_ref, *refs, total, l_ref, by, bz, mixed)
+    *refs, out_ref, total, l_ref, by, mixed = rest
+    rows_kernel(reach, True, p_ref, r_ref, *refs, total, l_ref, by, mixed)
     ends = o_ref[...] + over(l_ref[...], blocks_ref[...])
     deliver(total[...] + dot(refs[7][...], stacked(ends)), r_ref.shape[1], out_ref)
 
@@ -376,7 +366,7 @@
     )
     both = [bh, bl, ch, cl, s, sz, taps, mix, held]
     layer = (channels, -(-reach // each) * LANES)
-    room = [pltpu.VMEM(slab[0], F32), pltpu.VMEM((reach, channels, LANES), F32), pltpu.VMEM((reach, wide_rows, width_y), BF16)]
+    room = [pltpu.VMEM(slab[0], F32), pltpu.VMEM((reach, wide_rows, width_y), BF16)]
     p, l1 = call(
         functools.partial(rows_kernel, reach, False), [p, r1, *both], [share, (layer, F32)], room, weight=1e9
     )

time: 32.3 us -> 32.1 us (level)
  transfers between devices with their start and end apart: 4 -> 4, of which waited for: 1 -> 1; matrix products, arithmetic and copies ran while one was open for 0% -> 0% of each run, Pallas kernels for 13% -> 12%
where the time goes in v9:
time: 32.1 us; the launch traced here: 31.9 us
  blocking collectives  17 us (53%)
  starting transfers between devices  6.85 us (21%)
  Pallas kernels  6.8 us (21%)
  waiting for transfers between devices  1.19 us (4%)
    all_to_all x1, blocking collectives, local(): parts = lax.all_to_all(out, ('gx', 'gy'), 0, 0, tiled=True)  17 us
    pallas_call x10, Pallas kernels, call(): pl.pallas_call(body, out_shape=[make(shape, dtype) for shape, dtype in ou...  6.8 us
    ppermute x1, starting transfers between devices, local(): chip = lax.ppermute(chip, 'gy', pairs(count_y, 1))  3.05 us
    ppermute x1, starting transfers between devices, local(): r1 = lax.ppermute(s1, 'gx', pairs(count_x, 0))  2.11 us
    ppermute x1, waiting for transfers between devices, local(): chip = lax.ppermute(chip, 'gy', pairs(count_y, 1))  1.15 us
    ppermute x1, starting transfers between devices, local(): core = lax.ppermute(core, 'gy', pairs(count_y, 0))  1.02 us
    ppermute x1, starting transfers between devices, local(): r2 = lax.ppermute(s2, 'gx', pairs(count_x, 1))  0.68 us
  transfers between devices with their start and end apart: 4, of which 1 were waited for; matrix products, arithmetic and copies ran while one was open for 0% of the time, Pallas kernels for 12%

profile of v9, /device:TPU:1, one launch (start us, length us, event | category | flops | bytes accessed | tf_op | source)
XLA Modules:
  0.0 31.9 jit_solution(17559322077858214948)
XLA Ops:
  0.0 0.0 copy-start
  0.0 1.2 %shard_map.73 = (f32[10,24,256]{2,1,0:T(8,128)S(1)}, f32[1,21]{1,0:T(1,128)S(1)}, f32[1,21]{1,0:T(1,128)S(1)}, f32[4,4]{1,0:T(4,128)S(1)}, f32[6,6]{1,0:T(8,128)S(1)}) custom-call(f32[24,32,256]{2,1,0:T(8,128)} %bitcast.7, f32[1,21]{1,0:T(1,128)} %bitcast.10, f32[1,21]{1,0:T(1,128)} %bitcast.11, f32[4,4]{1,0:T(4,128)} %refs_2_.1, f32[6,6]{1,0:T(8,128)} %refs_3_.1), custom_call_target="tpu_custom_call" | custom-call | flops 3000000000 | bytes 1048576 | tf_op jit(solution)/shard_map/pallas_call | solution.py:294
  1.2 0.0 copy-start.1
  1.2 2.1 %collective-permute-start = (f32[10,24,256]{2,1,0:T(8,128)S(1)}, f32[10,24,256]{2,1,0:T(8,128)S(1)}, u32[]{:S(2)}, u32[]{:S(2)}) collective-permute-start(f32[10,24,256]{2,1,0:T(8,128)S(1)} %get-tuple-element.34.before_ref), channel_id=1, source_target_pairs={{0,4},{4,0},{8,12},{12,8},{16,20},{20,16},{24,28},{28,24},{1,5},{5... | collective-permute-start | bytes 737288 | tf_op jit(solution)/shard_map/ppermute | solution.py:338
  3.3 0.0 copy-done
  3.3 0.2 shard_map.79
  3.5 1.0 %collective-permute-start.2 = (f32[10,32,256]{2,1,0:T(8,128)S(1)}, f32[10,32,256]{2,1,0:T(8,128)S(1)}, u32[]{:S(2)}, u32[]{:S(2)}) collective-permute-start(f32[10,32,256]{2,1,0:T(8,128)S(1)} %get-tuple-element.51), channel_id=1, source_target_pairs={{0,1},{1,0},{2,3},{3,2},{4,5},{5,4},{6,7},{7,6},{8,9},{9,8},{10,11... | collective-permute-start | bytes 983048 | tf_op jit(solution)/shard_map/ppermute | solution.py:348
  4.5 3.0 %collective-permute-start.3 = (f32[10,32,256]{2,1,0:T(8,128)S(1)}, f32[10,32,256]{2,1,0:T(8,128)S(1)}, u32[]{:S(2)}, u32[]{:S(2)}) collective-permute-start(f32[10,32,256]{2,1,0:T(8,128)S(1)} %get-tuple-element.52), channel_id=1, source_target_pairs={{1,2},{2,1},{5,6},{6,5},{9,10},{10,9},{13,14},{14,13},{17,18},{18,... | collective-permute-start | bytes 983048 | tf_op jit(solution)/shard_map/ppermute | solution.py:349
  7.6 0.0 copy-done.1
  7.6 0.2 shard_map.74
  7.7 0.7 %collective-permute-start.1 = (f32[10,24,256]{2,1,0:T(8,128)S(1)}, f32[10,24,256]{2,1,0:T(8,128)S(1)}, u32[]{:S(2)}, u32[]{:S(2)}) collective-permute-start(f32[10,24,256]{2,1,0:T(8,128)S(1)} %get-tuple-element.48), channel_id=1, source_target_pairs={{4,8},{8,4},{12,16},{16,12},{20,24},{24,20},{5,9},{9,5},{13,17},{1... | collective-permute-start | bytes 737288 | tf_op jit(solution)/shard_map/ppermute | solution.py:339
  8.4 1.1 %shard_map.75 = (f32[32,24,256]{2,1,0:T(8,128)S(1)}, f32[32,24,128]{2,1,0:T(8,128)S(1)}, bf16[256,256]{1,0:T(8,128)(2,1)S(1)}, bf16[256,256]{1,0:T(8,128)(2,1)S(...) custom-call(f32[1,21]{1,0:T(1,128)S(1)} %get-tuple-element.33.north_ref, ...), custom_call_target="tpu_custom_call" | custom-call | flops 10000000 | bytes 1048576 | tf_op jit(solution)/shard_map/pallas_call | solution.py:294
  9.5 0.8 %shard_map.76 = (f32[32,24,256]{2,1,0:T(8,128)S(1)}, f32[32,24,128]{2,1,0:T(8,128)S(1)}, bf16[32,96]{1,0:T(8,128)(2,1)S(1)}, f32[21,8,256]{2,1,0:T(8,128)S(1)}) custom-call(f32[1,21]{1,0:T(1,128)S(1)} %get-tuple-element.30.east_ref, f32[4,4]{1,0:T(4,128)S(1)} %get-tuple-element.31.field_ref, f32[6,6]{1,0:T(8,128)S(1)} %get-tuple-element.32.time_ref, ...), custom_call_target="tpu_custom_call" | custom-call | flops 10000000 | bytes 1048576 | tf_op jit(solution)/shard_map/pallas_call | solution.py:294
  10.3 0.5 %shard_map.77 = (f32[32,256]{1,0:T(8,128)S(1)}, f32[24,384]{1,0:T(8,128)S(1)}) custom-call(f32[32,24,256]{2,1,0:T(8,128)S(1)} %get-tuple-element.38.s_ref.rest_4_, f32[32,24,128]{2,1,0:T(8,128)S(1)} %get-tuple-element.39.z_ref.rest_5_, bf16[32,96]{1,0:T(8,128)(2,1)S(1)} %get-tuple-element.40.mix_ref.rest_7_, bf16[32,256,256]{2,1,0:T(8,128)(2,1)S(1)} %copy-done), custom_call_target="tpu_custom_call" | custom-call | flops 10000000 | bytes 1048576 | tf_op jit(solution)/shard_map/pallas_call | solution.py:294
  10.8 0.0 collective-permute-done.r_ref
  10.9 0.8 %shard_map.78 = (f32[32,256]{1,0:T(8,128)S(1)}, f32[24,384]{1,0:T(8,128)S(1)}) custom-call(f32[32,256]{1,0:T(8,128)S(1)} %get-tuple-element.41.p_ref, f32[10,24,256]{2,1,0:T(8,128)S(1)} %collective-permute-done.r_ref, bf16[256,256]{1,0:T(8,128)(2,1)S(1)} %get-tuple-element.42.bh_ref.rest_0_, bf16[256,256]{1,0:T(8,128)(2,1)S(1)} %get-tuple-element.43.bl_ref.rest_1_, ...), custom_call_target="tpu_custom_call" | custom-call | flops 1000000000 | bytes 1048576 | tf_op jit(solution)/shard_map/pallas_call | solution.py:294
  11.7 0.0 copy-start.2
  11.7 0.0 collective-permute-done.2.core_ref
  11.7 1.2 %collective-permute-done.3.chip_ref = f32[10,32,256]{2,1,0:T(8,128)S(1)} collective-permute-done((f32[10,32,256]{2,1,0:T(8,128)S(1)}, f32[10,32,256]{2,1,0:T(8,128)S(1)}, u32[]{:S(2)}, u32[]{:S(2)}) %collective-permute-start.3) | collective-permute-done | bytes 327712 | tf_op jit(solution)/shard_map/ppermute | solution.py:349
  12.9 0.3 %shard_map.80 = (f32[24,256]{1,0:T(8,128)S(1)}, bf16[12,32,256]{2,1,0:T(8,128)(2,1)S(1)}) custom-call(f32[24,384]{1,0:T(8,128)S(1)} %get-tuple-element.49.l0_ref, f32[24,384]{1,0:T(8,128)S(1)} %get-tuple-element.50.l1_ref, f32[10,32,256]{2,1,0:T(8,128)S(1)} %collective-permute-done.2.core_ref, f32[10,32,256]{2,1,0:T(8,128)S(1)} %collective-permute-done.3.chip_ref), custom_call_target="tpu_custom_call" | custom-call | flops 10000000 | bytes 1048576 | tf_op jit(solution)/shard_map/pallas_call | solution.py:294
  13.2 0.0 collective-permute-done.1.r_ref
  13.3 1.0 %shard_map.81 = f32[8,4,3,4,128]{4,3,2,1,0:T(4,128)S(1)} custom-call(f32[32,256]{1,0:T(8,128)S(1)} %get-tuple-element.47.p_ref, f32[10,24,256]{2,1,0:T(8,128)S(1)} %collective-permute-done.1.r_ref, f32[24,256]{1,0:T(8,128)S(1)} %get-tuple-element.53.o_ref, bf16[12,32,256]{2,1,0:T(8,128)(2,1)S(1)} %get-tuple-element.54.blocks_ref, ...), custom_call_target="tpu_custom_call" | custom-call | flops 1000000000 | bytes 1048576 | tf_op jit(solution)/shard_map/pallas_call | solution.py:294
  14.3 17.0 %all_to_all.5.parts_ref = f32[32,3,4,128]{3,2,1,0:T(4,128)S(1)} all-to-all(f32[32,3,4,128]{3,2,1,0:T(4,128)S(1)} %bitcast.6), channel_id=1, replica_groups=mesh['gx'=8,'gy'=4] {'gx','gy'}, dimensions={0} | all-to-all | bytes 393216 | tf_op jit(solution)/shard_map/all_to_all | solution.py:390
  31.2 0.0 copy-done.2
  31.2 0.7 %shard_map.82 = f32[24,64]{1,0:T(8,128)} custom-call(f32[32,3,4,128]{3,2,1,0:T(4,128)S(1)} %all_to_all.5.parts_ref, f32[24,64]{1,0:T(8,128)S(1)} %bitcast.9), custom_call_target="tpu_custom_call" | custom-call | flops 1000000000 | bytes 1048576 | tf_op jit(solution)/shard_map/pallas_call | solution.py:294
Async XLA Ops:
  0.0 3.3 %copy-start = (bf16[32,256,256]{2,1,0:T(8,128)(2,1)S(1)}, bf16[32,256,256]{2,1,0:T(8,128)(2,1)}, u32[]{:S(2)}) copy-start(bf16[32,256,256]{2,1,0:T(8,128)(2,1)} %rest_8_.1) | copy-start | bytes 12582916
  1.2 6.4 %copy-start.1 = (f32[4,6,32,256]{3,2,1,0:T(8,128)S(1)}, f32[4,6,32,256]{3,2,1,0:T(8,128)}, u32[]{:S(2)}) copy-start(f32[4,6,32,256]{3,2,1,0:T(8,128)} %param.7) | copy-start | bytes 2359300
  1.2 9.7 %collective-permute-start = (f32[10,24,256]{2,1,0:T(8,128)S(1)}, f32[10,24,256]{2,1,0:T(8,128)S(1)}, u32[]{:S(2)}, u32[]{:S(2)}) collective-permute-start(f32[10,24,256]{2,1,0:T(8,128)S(1)} %get-tuple-element.34.before_ref), channel_id=1, source_target_pairs={{0,4},{4,0},{8,12},{12,8},{16,20},{20,16},{24,28},{28,24},{1,5},{5... | collective-permute-start | bytes 737288 | tf_op jit(solution)/shard_map/ppermute | solution.py:338
  3.5 8.2 %collective-permute-start.2 = (f32[10,32,256]{2,1,0:T(8,128)S(1)}, f32[10,32,256]{2,1,0:T(8,128)S(1)}, u32[]{:S(2)}, u32[]{:S(2)}) collective-permute-start(f32[10,32,256]{2,1,0:T(8,128)S(1)} %get-tuple-element.51), channel_id=1, source_target_pairs={{0,1},{1,0},{2,3},{3,2},{4,5},{5,4},{6,7},{7,6},{8,9},{9,8},{10,11... | collective-permute-start | bytes 983048 | tf_op jit(solution)/shard_map/ppermute | solution.py:348
  4.5 8.4 %collective-permute-start.3 = (f32[10,32,256]{2,1,0:T(8,128)S(1)}, f32[10,32,256]{2,1,0:T(8,128)S(1)}, u32[]{:S(2)}, u32[]{:S(2)}) collective-permute-start(f32[10,32,256]{2,1,0:T(8,128)S(1)} %get-tuple-element.52), channel_id=1, source_target_pairs={{1,2},{2,1},{5,6},{6,5},{9,10},{10,9},{13,14},{14,13},{17,18},{18,... | collective-permute-start | bytes 983048 | tf_op jit(solution)/shard_map/ppermute | solution.py:349
  7.7 5.5 %collective-permute-start.1 = (f32[10,24,256]{2,1,0:T(8,128)S(1)}, f32[10,24,256]{2,1,0:T(8,128)S(1)}, u32[]{:S(2)}, u32[]{:S(2)}) collective-permute-start(f32[10,24,256]{2,1,0:T(8,128)S(1)} %get-tuple-element.48), channel_id=1, source_target_pairs={{4,8},{8,4},{12,16},{16,12},{20,24},{24,20},{5,9},{9,5},{13,17},{1... | collective-permute-start | bytes 737288 | tf_op jit(solution)/shard_map/ppermute | solution.py:339
  11.7 19.5 %copy-start.2 = (f32[64,24]{0,1:T(8,128)S(1)}, f32[64,24]{0,1:T(8,128)}, u32[]{:S(2)}) copy-start(f32[64,24]{0,1:T(8,128)} %param.13) | copy-start | bytes 18436

commit v10 on v9

--- a/solution.py
+++ b/solution.py
@@ -77,10 +77,19 @@
         copy.wait()
 
 
-def turn_kernel(reach, a_ref, before_ref, t_ref, s2_ref):
+def second_kernel(reach, a_ref, before_ref, s2_ref):
+    del before_ref
+    width_x = a_ref.shape[1]
+    window = -(-reach // 8) * 8
+    odd = lax.axis_index("gx") % 2
+    rows = a_ref[:, pl.ds(pl.multiple_of(odd * (width_x - window), 8), window)]
+    rows = jnp.swapaxes(rows, 0, 1)
+    s2_ref[...] = jnp.where(odd == 1, rows[window - reach :], rows[:reach])
+
+
+def turn_kernel(a_ref, before_ref, t_ref):
     del before_ref
     t_ref[...] = jnp.swapaxes(a_ref[...], 0, 1)
-    s2_ref[...] = t_ref[pl.ds(lax.axis_index("gx") % 2 * (t_ref.shape[0] - reach), reach)]
 
 
 def block_kernel(reach, modes_ref, core_ref, chip_ref):
@@ -333,7 +342,9 @@
         outside=True,
         weight=3e9,
     )
-    t, s2 = call(functools.partial(turn_kernel, reach), [raw, s1], [full, slab], weight=1e7)
+    raw = vmem(raw)
+    (s2,) = call(functools.partial(second_kernel, reach), [raw, s1], [slab], weight=1e7)
+    (t,) = call(turn_kernel, [raw, s2], [full], weight=1e7)
     held = vmem(spatial_modes)
     r1 = lax.ppermute(s1, "gx", pairs(count_x, 0))
     r2 = lax.ppermute(s2, "gx", pairs(count_x, 1))

time: 32.1 us -> 32.1 us (level)
    pallas_call x10 -> x11, Pallas kernels: 6.8 us -> 6.88 us  [call(): pl.pallas_call(body, out_shape=[make(shape, dtype) for shape, dtype in ou...]
  transfers between devices with their start and end apart: 4 -> 4, of which waited for: 1 -> 1; matrix products, arithmetic and copies ran while one was open for 0% -> 0% of each run, Pallas kernels for 12% -> 13%
where the time goes in v10:
time: 32.1 us; the launch traced here: 31.9 us
  blocking collectives  16.9 us (53%)
  Pallas kernels  6.88 us (21%)
  starting transfers between devices  6.85 us (21%)
  waiting for transfers between devices  1.1 us (3%)
    all_to_all x1, blocking collectives, local(): parts = lax.all_to_all(out, ('gx', 'gy'), 0, 0, tiled=True)  16.9 us
    pallas_call x11, Pallas kernels, call(): pl.pallas_call(body, out_shape=[make(shape, dtype) for shape, dtype in ou...  6.88 us
    ppermute x1, starting transfers between devices, local(): chip = lax.ppermute(chip, 'gy', pairs(count_y, 1))  3.05 us
    ppermute x1, starting transfers between devices, local(): r1 = lax.ppermute(s1, 'gx', pairs(count_x, 0))  2.11 us
    ppermute x1, waiting for transfers between devices, local(): chip = lax.ppermute(chip, 'gy', pairs(count_y, 1))  1.07 us
    ppermute x1, starting transfers between devices, local(): core = lax.ppermute(core, 'gy', pairs(count_y, 0))  1.02 us
    ppermute x1, starting transfers between devices, local(): r2 = lax.ppermute(s2, 'gx', pairs(count_x, 1))  0.68 us
  transfers between devices with their start and end apart: 4, of which 1 were waited for; matrix products, arithmetic and copies ran while one was open for 0% of the time, Pallas kernels for 13%

profile of v10, /device:TPU:1, one launch (start us, length us, event | category | flops | bytes accessed | tf_op | source)
XLA Modules:
  0.0 31.9 jit_solution(13609529780119796169)
XLA Ops:
  0.0 0.0 copy-start
  0.0 1.2 %shard_map.73 = (f32[10,24,256]{2,1,0:T(8,128)S(1)}, f32[1,21]{1,0:T(1,128)S(1)}, f32[1,21]{1,0:T(1,128)S(1)}, f32[4,4]{1,0:T(4,128)S(1)}, f32[6,6]{1,0:T(8,128)S(1)}) custom-call(f32[24,32,256]{2,1,0:T(8,128)} %bitcast.6, f32[1,21]{1,0:T(1,128)} %bitcast.11, f32[1,21]{1,0:T(1,128)} %bitcast.12, f32[4,4]{1,0:T(4,128)} %refs_2_.1, f32[6,6]{1,0:T(8,128)} %refs_3_.1), custom_call_target="tpu_custom_call" | custom-call | flops 3000000000 | bytes 1048576 | tf_op jit(solution)/shard_map/pallas_call | solution.py:303
  1.2 0.0 copy-start.1
  1.2 2.1 %collective-permute-start = (f32[10,24,256]{2,1,0:T(8,128)S(1)}, f32[10,24,256]{2,1,0:T(8,128)S(1)}, u32[]{:S(2)}, u32[]{:S(2)}) collective-permute-start(f32[10,24,256]{2,1,0:T(8,128)S(1)} %get-tuple-element.32.before_ref), channel_id=1, source_target_pairs={{0,4},{4,0},{8,12},{12,8},{16,20},{20,16},{24,28},{28,24},{1,5},{5... | collective-permute-start | bytes 737288 | tf_op jit(solution)/shard_map/ppermute | solution.py:349
  3.3 0.0 copy-done
  3.3 0.2 shard_map.80
  3.5 1.0 %collective-permute-start.2 = (f32[10,32,256]{2,1,0:T(8,128)S(1)}, f32[10,32,256]{2,1,0:T(8,128)S(1)}, u32[]{:S(2)}, u32[]{:S(2)}) collective-permute-start(f32[10,32,256]{2,1,0:T(8,128)S(1)} %get-tuple-element.47), channel_id=1, source_target_pairs={{0,1},{1,0},{2,3},{3,2},{4,5},{5,4},{6,7},{7,6},{8,9},{9,8},{10,11... | collective-permute-start | bytes 983048 | tf_op jit(solution)/shard_map/ppermute | solution.py:359
  4.5 3.0 %collective-permute-start.3 = (f32[10,32,256]{2,1,0:T(8,128)S(1)}, f32[10,32,256]{2,1,0:T(8,128)S(1)}, u32[]{:S(2)}, u32[]{:S(2)}) collective-permute-start(f32[10,32,256]{2,1,0:T(8,128)S(1)} %get-tuple-element.48), channel_id=1, source_target_pairs={{1,2},{2,1},{5,6},{6,5},{9,10},{10,9},{13,14},{14,13},{17,18},{18,... | collective-permute-start | bytes 983048 | tf_op jit(solution)/shard_map/ppermute | solution.py:360
  7.6 0.0 copy-done.1
  7.6 0.1 shard_map.74.before_ref
  7.7 0.7 %collective-permute-start.1 = (f32[10,24,256]{2,1,0:T(8,128)S(1)}, f32[10,24,256]{2,1,0:T(8,128)S(1)}, u32[]{:S(2)}, u32[]{:S(2)}) collective-permute-start(f32[10,24,256]{2,1,0:T(8,128)S(1)} %shard_map.74.before_ref), channel_id=1, source_target_pairs={{4,8},{8,4},{12,16},{16,12},{20,24},{24,20},{5,9},{9,5},{13,17},{1... | collective-permute-start | bytes 737288 | tf_op jit(solution)/shard_map/ppermute | solution.py:350
  8.4 0.1 shard_map.75.t_ref
  8.5 1.1 %shard_map.76 = (f32[32,24,256]{2,1,0:T(8,128)S(1)}, f32[32,24,128]{2,1,0:T(8,128)S(1)}, bf16[256,256]{1,0:T(8,128)(2,1)S(1)}, bf16[256,256]{1,0:T(8,128)(2,1)S(...) custom-call(f32[1,21]{1,0:T(1,128)S(1)} %get-tuple-element.31.north_ref, f32[32,24,256]{2,1,0:T(8,128)S(1)} %shard_map.75.t_ref), custom_call_target="tpu_custom_call" | custom-call | flops 10000000 | bytes 1048576 | tf_op jit(solution)/shard_map/pallas_call | solution.py:303
  9.6 0.8 %shard_map.77 = (f32[32,24,256]{2,1,0:T(8,128)S(1)}, f32[32,24,128]{2,1,0:T(8,128)S(1)}, bf16[32,96]{1,0:T(8,128)(2,1)S(1)}, f32[21,8,256]{2,1,0:T(8,128)S(1)}) custom-call(f32[1,21]{1,0:T(1,128)S(1)} %get-tuple-element.28.east_ref, f32[4,4]{1,0:T(4,128)S(1)} %get-tuple-element.29.field_ref, f32[6,6]{1,0:T(8,128)S(1)} %get-tuple-element.30.time_ref, ...), custom_call_target="tpu_custom_call" | custom-call | flops 10000000 | bytes 1048576 | tf_op jit(solution)/shard_map/pallas_call | solution.py:303
  10.4 0.5 %shard_map.78 = (f32[32,256]{1,0:T(8,128)S(1)}, f32[24,384]{1,0:T(8,128)S(1)}) custom-call(f32[32,24,256]{2,1,0:T(8,128)S(1)} %get-tuple-element.35.s_ref.rest_4_, f32[32,24,128]{2,1,0:T(8,128)S(1)} %get-tuple-element.36.z_ref.rest_5_, bf16[32,96]{1,0:T(8,128)(2,1)S(1)} %get-tuple-element.37.mix_ref.rest_7_, bf16[32,256,256]{2,1,0:T(8,128)(2,1)S(1)} %copy-done), custom_call_target="tpu_custom_call" | custom-call | flops 10000000 | bytes 1048576 | tf_op jit(solution)/shard_map/pallas_call | solution.py:303
  10.9 0.0 collective-permute-done.r_ref
  10.9 0.9 %shard_map.79 = (f32[32,256]{1,0:T(8,128)S(1)}, f32[24,384]{1,0:T(8,128)S(1)}) custom-call(f32[32,256]{1,0:T(8,128)S(1)} %get-tuple-element.38.p_ref, f32[10,24,256]{2,1,0:T(8,128)S(1)} %collective-permute-done.r_ref, bf16[256,256]{1,0:T(8,128)(2,1)S(1)} %get-tuple-element.39.bh_ref.rest_0_, bf16[256,256]{1,0:T(8,128)(2,1)S(1)} %get-tuple-element.40.bl_ref.rest_1_, ...), custom_call_target="tpu_custom_call" | custom-call | flops 1000000000 | bytes 1048576 | tf_op jit(solution)/shard_map/pallas_call | solution.py:303
  11.8 0.0 copy-start.2
  11.8 0.0 collective-permute-done.2.core_ref
  11.8 1.1 %collective-permute-done.3.chip_ref = f32[10,32,256]{2,1,0:T(8,128)S(1)} collective-permute-done((f32[10,32,256]{2,1,0:T(8,128)S(1)}, f32[10,32,256]{2,1,0:T(8,128)S(1)}, u32[]{:S(2)}, u32[]{:S(2)}) %collective-permute-start.3) | collective-permute-done | bytes 327712 | tf_op jit(solution)/shard_map/ppermute | solution.py:360
  12.9 0.3 %shard_map.81 = (f32[24,256]{1,0:T(8,128)S(1)}, bf16[12,32,256]{2,1,0:T(8,128)(2,1)S(1)}) custom-call(f32[24,384]{1,0:T(8,128)S(1)} %get-tuple-element.45.l0_ref, f32[24,384]{1,0:T(8,128)S(1)} %get-tuple-element.46.l1_ref, f32[10,32,256]{2,1,0:T(8,128)S(1)} %collective-permute-done.2.core_ref, f32[10,32,256]{2,1,0:T(8,128)S(1)} %collective-permute-done.3.chip_ref), custom_call_target="tpu_custom_call" | custom-call | flops 10000000 | bytes 1048576 | tf_op jit(solution)/shard_map/pallas_call | solution.py:303
  13.2 0.0 collective-permute-done.1.r_ref
  13.3 1.0 %shard_map.82 = f32[8,4,3,4,128]{4,3,2,1,0:T(4,128)S(1)} custom-call(f32[32,256]{1,0:T(8,128)S(1)} %get-tuple-element.44.p_ref, f32[10,24,256]{2,1,0:T(8,128)S(1)} %collective-permute-done.1.r_ref, f32[24,256]{1,0:T(8,128)S(1)} %get-tuple-element.49.o_ref, bf16[12,32,256]{2,1,0:T(8,128)(2,1)S(1)} %get-tuple-element.50.blocks_ref, ...), custom_call_target="tpu_custom_call" | custom-call | flops 1000000000 | bytes 1048576 | tf_op jit(solution)/shard_map/pallas_call | solution.py:303
  14.3 16.9 %all_to_all.5.parts_ref = f32[32,3,4,128]{3,2,1,0:T(4,128)S(1)} all-to-all(f32[32,3,4,128]{3,2,1,0:T(4,128)S(1)} %bitcast.9), channel_id=1, replica_groups=mesh['gx'=8,'gy'=4] {'gx','gy'}, dimensions={0} | all-to-all | bytes 393216 | tf_op jit(solution)/shard_map/all_to_all | solution.py:401
  31.2 0.0 copy-done.2
  31.2 0.7 %shard_map.83 = f32[24,64]{1,0:T(8,128)} custom-call(f32[32,3,4,128]{3,2,1,0:T(4,128)S(1)} %all_to_all.5.parts_ref, f32[24,64]{1,0:T(8,128)S(1)} %bitcast.10), custom_call_target="tpu_custom_call" | custom-call | flops 1000000000 | bytes 1048576 | tf_op jit(solution)/shard_map/pallas_call | solution.py:303
Async XLA Ops:
  0.0 3.3 %copy-start = (bf16[32,256,256]{2,1,0:T(8,128)(2,1)S(1)}, bf16[32,256,256]{2,1,0:T(8,128)(2,1)}, u32[]{:S(2)}) copy-start(bf16[32,256,256]{2,1,0:T(8,128)(2,1)} %rest_8_.1) | copy-start | bytes 12582916
  1.2 6.4 %copy-start.1 = (f32[4,6,32,256]{3,2,1,0:T(8,128)S(1)}, f32[4,6,32,256]{3,2,1,0:T(8,128)}, u32[]{:S(2)}) copy-start(f32[4,6,32,256]{3,2,1,0:T(8,128)} %param.7) | copy-start | bytes 2359300
  1.2 9.8 %collective-permute-start = (f32[10,24,256]{2,1,0:T(8,128)S(1)}, f32[10,24,256]{2,1,0:T(8,128)S(1)}, u32[]{:S(2)}, u32[]{:S(2)}) collective-permute-start(f32[10,24,256]{2,1,0:T(8,128)S(1)} %get-tuple-element.32.before_ref), channel_id=1, source_target_pairs={{0,4},{4,0},{8,12},{12,8},{16,20},{20,16},{24,28},{28,24},{1,5},{5... | collective-permute-start | bytes 737288 | tf_op jit(solution)/shard_map/ppermute | solution.py:349
  3.5 8.3 %collective-permute-start.2 = (f32[10,32,256]{2,1,0:T(8,128)S(1)}, f32[10,32,256]{2,1,0:T(8,128)S(1)}, u32[]{:S(2)}, u32[]{:S(2)}) collective-permute-start(f32[10,32,256]{2,1,0:T(8,128)S(1)} %get-tuple-element.47), channel_id=1, source_target_pairs={{0,1},{1,0},{2,3},{3,2},{4,5},{5,4},{6,7},{7,6},{8,9},{9,8},{10,11... | collective-permute-start | bytes 983048 | tf_op jit(solution)/shard_map/ppermute | solution.py:359
  4.5 8.4 %collective-permute-start.3 = (f32[10,32,256]{2,1,0:T(8,128)S(1)}, f32[10,32,256]{2,1,0:T(8,128)S(1)}, u32[]{:S(2)}, u32[]{:S(2)}) collective-permute-start(f32[10,32,256]{2,1,0:T(8,128)S(1)} %get-tuple-element.48), channel_id=1, source_target_pairs={{1,2},{2,1},{5,6},{6,5},{9,10},{10,9},{13,14},{14,13},{17,18},{18,... | collective-permute-start | bytes 983048 | tf_op jit(solution)/shard_map/ppermute | solution.py:360
  7.7 5.6 %collective-permute-start.1 = (f32[10,24,256]{2,1,0:T(8,128)S(1)}, f32[10,24,256]{2,1,0:T(8,128)S(1)}, u32[]{:S(2)}, u32[]{:S(2)}) collective-permute-start(f32[10,24,256]{2,1,0:T(8,128)S(1)} %shard_map.74.before_ref), channel_id=1, source_target_pairs={{4,8},{8,4},{12,16},{16,12},{20,24},{24,20},{5,9},{9,5},{13,17},{1... | collective-permute-start | bytes 737288 | tf_op jit(solution)/shard_map/ppermute | solution.py:350
  11.8 19.4 %copy-start.2 = (f32[64,24]{0,1:T(8,128)S(1)}, f32[64,24]{0,1:T(8,128)}, u32[]{:S(2)}) copy-start(f32[64,24]{0,1:T(8,128)} %param.13) | copy-start | bytes 18436

commit v11 on v9

--- a/solution.py
+++ b/solution.py
@@ -35,7 +35,7 @@
     high = v.astype(BF16).astype(F32)
     parts = [high, v - high, high]
     if (3 * v.shape[0]) % 16:
-        parts.append(jnp.zeros((-3 * v.shape[0] % 96, v.shape[1]), F32))
+        parts.append(jnp.zeros((-3 * v.shape[0] % 16, v.shape[1]), F32))
     return jnp.concatenate(parts, axis=0).astype(BF16)
 
 
@@ -43,7 +43,7 @@
     high = m.astype(BF16).astype(F32)
     parts = [high, high, m - high]
     if (3 * m.shape[1]) % 16:
-        parts.append(jnp.zeros((m.shape[0], -3 * m.shape[1] % 96), F32))
+        parts.append(jnp.zeros((m.shape[0], -3 * m.shape[1] % 16), F32))
     return jnp.concatenate(parts, axis=1).astype(BF16)
 
 
@@ -353,7 +353,7 @@
         [
             full,
             narrow,
-            ((wide_rows, 3 * channels + -3 * channels % 96), BF16),
+            ((wide_rows, 3 * channels + -3 * channels % 16), BF16),
             ((2 * reach + 1, 8, width_y), F32),
         ],
         weight=1e7,

time: 32.1 us -> 32.1 us (level)
  no operation moved by 1% of the time
where the time goes in v11:
time: 32.1 us; the launch traced here: 31.9 us
  blocking collectives  17 us (53%)
  starting transfers between devices  6.85 us (21%)
  Pallas kernels  6.8 us (21%)
  waiting for transfers between devices  1.19 us (4%)
    all_to_all x1, blocking collectives, local(): parts = lax.all_to_all(out, ('gx', 'gy'), 0, 0, tiled=True)  17 us
    pallas_call x10, Pallas kernels, call(): pl.pallas_call(body, out_shape=[make(shape, dtype) for shape, dtype in ou...  6.8 us
    ppermute x1, starting transfers between devices, local(): chip = lax.ppermute(chip, 'gy', pairs(count_y, 1))  3.05 us
    ppermute x1, starting transfers between devices, local(): r1 = lax.ppermute(s1, 'gx', pairs(count_x, 0))  2.11 us
    ppermute x1, waiting for transfers between devices, local(): chip = lax.ppermute(chip, 'gy', pairs(count_y, 1))  1.15 us
    ppermute x1, starting transfers between devices, local(): core = lax.ppermute(core, 'gy', pairs(count_y, 0))  1.02 us
    ppermute x1, starting transfers between devices, local(): r2 = lax.ppermute(s2, 'gx', pairs(count_x, 1))  0.68 us
  transfers between devices with their start and end apart: 4, of which 1 were waited for; matrix products, arithmetic and copies ran while one was open for 0% of the time, Pallas kernels for 12%

profile of v11, /device:TPU:1, one launch (start us, length us, event | category | flops | bytes accessed | tf_op | source)
XLA Modules:
  0.0 31.9 jit_solution(5591617816851854490)
XLA Ops:
  0.0 0.0 copy-start
  0.0 1.2 %shard_map.73 = (f32[10,24,256]{2,1,0:T(8,128)S(1)}, f32[1,21]{1,0:T(1,128)S(1)}, f32[1,21]{1,0:T(1,128)S(1)}, f32[4,4]{1,0:T(4,128)S(1)}, f32[6,6]{1,0:T(8,128)S(1)}) custom-call(f32[24,32,256]{2,1,0:T(8,128)} %bitcast.7, f32[1,21]{1,0:T(1,128)} %bitcast.10, f32[1,21]{1,0:T(1,128)} %bitcast.11, f32[4,4]{1,0:T(4,128)} %refs_2_.1, f32[6,6]{1,0:T(8,128)} %refs_3_.1), custom_call_target="tpu_custom_call" | custom-call | flops 3000000000 | bytes 1048576 | tf_op jit(solution)/shard_map/pallas_call | solution.py:294
  1.2 0.0 copy-start.1
  1.2 2.1 %collective-permute-start = (f32[10,24,256]{2,1,0:T(8,128)S(1)}, f32[10,24,256]{2,1,0:T(8,128)S(1)}, u32[]{:S(2)}, u32[]{:S(2)}) collective-permute-start(f32[10,24,256]{2,1,0:T(8,128)S(1)} %get-tuple-element.34.before_ref), channel_id=1, source_target_pairs={{0,4},{4,0},{8,12},{12,8},{16,20},{20,16},{24,28},{28,24},{1,5},{5... | collective-permute-start | bytes 737288 | tf_op jit(solution)/shard_map/ppermute | solution.py:338
  3.3 0.0 copy-done
  3.3 0.2 shard_map.79
  3.5 1.0 %collective-permute-start.2 = (f32[10,32,256]{2,1,0:T(8,128)S(1)}, f32[10,32,256]{2,1,0:T(8,128)S(1)}, u32[]{:S(2)}, u32[]{:S(2)}) collective-permute-start(f32[10,32,256]{2,1,0:T(8,128)S(1)} %get-tuple-element.51), channel_id=1, source_target_pairs={{0,1},{1,0},{2,3},{3,2},{4,5},{5,4},{6,7},{7,6},{8,9},{9,8},{10,11... | collective-permute-start | bytes 983048 | tf_op jit(solution)/shard_map/ppermute | solution.py:348
  4.5 3.0 %collective-permute-start.3 = (f32[10,32,256]{2,1,0:T(8,128)S(1)}, f32[10,32,256]{2,1,0:T(8,128)S(1)}, u32[]{:S(2)}, u32[]{:S(2)}) collective-permute-start(f32[10,32,256]{2,1,0:T(8,128)S(1)} %get-tuple-element.52), channel_id=1, source_target_pairs={{1,2},{2,1},{5,6},{6,5},{9,10},{10,9},{13,14},{14,13},{17,18},{18,... | collective-permute-start | bytes 983048 | tf_op jit(solution)/shard_map/ppermute | solution.py:349
  7.6 0.0 copy-done.1
  7.6 0.2 shard_map.74
  7.7 0.7 %collective-permute-start.1 = (f32[10,24,256]{2,1,0:T(8,128)S(1)}, f32[10,24,256]{2,1,0:T(8,128)S(1)}, u32[]{:S(2)}, u32[]{:S(2)}) collective-permute-start(f32[10,24,256]{2,1,0:T(8,128)S(1)} %get-tuple-element.48), channel_id=1, source_target_pairs={{4,8},{8,4},{12,16},{16,12},{20,24},{24,20},{5,9},{9,5},{13,17},{1... | collective-permute-start | bytes 737288 | tf_op jit(solution)/shard_map/ppermute | solution.py:339
  8.4 1.1 %shard_map.75 = (f32[32,24,256]{2,1,0:T(8,128)S(1)}, f32[32,24,128]{2,1,0:T(8,128)S(1)}, bf16[256,256]{1,0:T(8,128)(2,1)S(1)}, bf16[256,256]{1,0:T(8,128)(2,1)S(...) custom-call(f32[1,21]{1,0:T(1,128)S(1)} %get-tuple-element.33.north_ref, ...), custom_call_target="tpu_custom_call" | custom-call | flops 10000000 | bytes 1048576 | tf_op jit(solution)/shard_map/pallas_call | solution.py:294
  9.5 0.8 %shard_map.76 = (f32[32,24,256]{2,1,0:T(8,128)S(1)}, f32[32,24,128]{2,1,0:T(8,128)S(1)}, bf16[32,80]{1,0:T(8,128)(2,1)S(1)}, f32[21,8,256]{2,1,0:T(8,128)S(1)}) custom-call(f32[1,21]{1,0:T(1,128)S(1)} %get-tuple-element.30.east_ref, f32[4,4]{1,0:T(4,128)S(1)} %get-tuple-element.31.field_ref, f32[6,6]{1,0:T(8,128)S(1)} %get-tuple-element.32.time_ref, ...), custom_call_target="tpu_custom_call" | custom-call | flops 10000000 | bytes 1048576 | tf_op jit(solution)/shard_map/pallas_call | solution.py:294
  10.3 0.5 %shard_map.77 = (f32[32,256]{1,0:T(8,128)S(1)}, f32[24,384]{1,0:T(8,128)S(1)}) custom-call(f32[32,24,256]{2,1,0:T(8,128)S(1)} %get-tuple-element.38.s_ref.rest_4_, f32[32,24,128]{2,1,0:T(8,128)S(1)} %get-tuple-element.39.z_ref.rest_5_, bf16[32,80]{1,0:T(8,128)(2,1)S(1)} %get-tuple-element.40.mix_ref.rest_7_, bf16[32,256,256]{2,1,0:T(8,128)(2,1)S(1)} %copy-done), custom_call_target="tpu_custom_call" | custom-call | flops 10000000 | bytes 1048576 | tf_op jit(solution)/shard_map/pallas_call | solution.py:294
  10.8 0.0 collective-permute-done.r_ref
  10.9 0.8 %shard_map.78 = (f32[32,256]{1,0:T(8,128)S(1)}, f32[24,384]{1,0:T(8,128)S(1)}) custom-call(f32[32,256]{1,0:T(8,128)S(1)} %get-tuple-element.41.p_ref, f32[10,24,256]{2,1,0:T(8,128)S(1)} %collective-permute-done.r_ref, bf16[256,256]{1,0:T(8,128)(2,1)S(1)} %get-tuple-element.42.bh_ref.rest_0_, bf16[256,256]{1,0:T(8,128)(2,1)S(1)} %get-tuple-element.43.bl_ref.rest_1_, ...), custom_call_target="tpu_custom_call" | custom-call | flops 1000000000 | bytes 1048576 | tf_op jit(solution)/shard_map/pallas_call | solution.py:294
  11.7 0.0 copy-start.2
  11.7 0.0 collective-permute-done.2.core_ref
  11.7 1.2 %collective-permute-done.3.chip_ref = f32[10,32,256]{2,1,0:T(8,128)S(1)} collective-permute-done((f32[10,32,256]{2,1,0:T(8,128)S(1)}, f32[10,32,256]{2,1,0:T(8,128)S(1)}, u32[]{:S(2)}, u32[]{:S(2)}) %collective-permute-start.3) | collective-permute-done | bytes 327712 | tf_op jit(solution)/shard_map/ppermute | solution.py:349
  12.9 0.3 %shard_map.80 = (f32[24,256]{1,0:T(8,128)S(1)}, bf16[12,32,256]{2,1,0:T(8,128)(2,1)S(1)}) custom-call(f32[24,384]{1,0:T(8,128)S(1)} %get-tuple-element.49.l0_ref, f32[24,384]{1,0:T(8,128)S(1)} %get-tuple-element.50.l1_ref, f32[10,32,256]{2,1,0:T(8,128)S(1)} %collective-permute-done.2.core_ref, f32[10,32,256]{2,1,0:T(8,128)S(1)} %collective-permute-done.3.chip_ref), custom_call_target="tpu_custom_call" | custom-call | flops 10000000 | bytes 1048576 | tf_op jit(solution)/shard_map/pallas_call | solution.py:294
  13.2 0.0 collective-permute-done.1.r_ref
  13.3 1.0 %shard_map.81 = f32[8,4,3,4,128]{4,3,2,1,0:T(4,128)S(1)} custom-call(f32[32,256]{1,0:T(8,128)S(1)} %get-tuple-element.47.p_ref, f32[10,24,256]{2,1,0:T(8,128)S(1)} %collective-permute-done.1.r_ref, f32[24,256]{1,0:T(8,128)S(1)} %get-tuple-element.53.o_ref, bf16[12,32,256]{2,1,0:T(8,128)(2,1)S(1)} %get-tuple-element.54.blocks_ref, ...), custom_call_target="tpu_custom_call" | custom-call | flops 1000000000 | bytes 1048576 | tf_op jit(solution)/shard_map/pallas_call | solution.py:294
  14.3 17.0 %all_to_all.5.parts_ref = f32[32,3,4,128]{3,2,1,0:T(4,128)S(1)} all-to-all(f32[32,3,4,128]{3,2,1,0:T(4,128)S(1)} %bitcast.6), channel_id=1, replica_groups=mesh['gx'=8,'gy'=4] {'gx','gy'}, dimensions={0} | all-to-all | bytes 393216 | tf_op jit(solution)/shard_map/all_to_all | solution.py:390
  31.2 0.0 copy-done.2
  31.2 0.7 %shard_map.82 = f32[24,64]{1,0:T(8,128)} custom-call(f32[32,3,4,128]{3,2,1,0:T(4,128)S(1)} %all_to_all.5.parts_ref, f32[24,64]{1,0:T(8,128)S(1)} %bitcast.9), custom_call_target="tpu_custom_call" | custom-call | flops 1000000000 | bytes 1048576 | tf_op jit(solution)/shard_map/pallas_call | solution.py:294
Async XLA Ops:
  0.0 3.3 %copy-start = (bf16[32,256,256]{2,1,0:T(8,128)(2,1)S(1)}, bf16[32,256,256]{2,1,0:T(8,128)(2,1)}, u32[]{:S(2)}) copy-start(bf16[32,256,256]{2,1,0:T(8,128)(2,1)} %rest_8_.1) | copy-start | bytes 12582916
  1.2 6.4 %copy-start.1 = (f32[4,6,32,256]{3,2,1,0:T(8,128)S(1)}, f32[4,6,32,256]{3,2,1,0:T(8,128)}, u32[]{:S(2)}) copy-start(f32[4,6,32,256]{3,2,1,0:T(8,128)} %param.7) | copy-start | bytes 2359300
  1.2 9.7 %collective-permute-start = (f32[10,24,256]{2,1,0:T(8,128)S(1)}, f32[10,24,256]{2,1,0:T(8,128)S(1)}, u32[]{:S(2)}, u32[]{:S(2)}) collective-permute-start(f32[10,24,256]{2,1,0:T(8,128)S(1)} %get-tuple-element.34.before_ref), channel_id=1, source_target_pairs={{0,4},{4,0},{8,12},{12,8},{16,20},{20,16},{24,28},{28,24},{1,5},{5... | collective-permute-start | bytes 737288 | tf_op jit(solution)/shard_map/ppermute | solution.py:338
  3.5 8.2 %collective-permute-start.2 = (f32[10,32,256]{2,1,0:T(8,128)S(1)}, f32[10,32,256]{2,1,0:T(8,128)S(1)}, u32[]{:S(2)}, u32[]{:S(2)}) collective-permute-start(f32[10,32,256]{2,1,0:T(8,128)S(1)} %get-tuple-element.51), channel_id=1, source_target_pairs={{0,1},{1,0},{2,3},{3,2},{4,5},{5,4},{6,7},{7,6},{8,9},{9,8},{10,11... | collective-permute-start | bytes 983048 | tf_op jit(solution)/shard_map/ppermute | solution.py:348
  4.5 8.4 %collective-permute-start.3 = (f32[10,32,256]{2,1,0:T(8,128)S(1)}, f32[10,32,256]{2,1,0:T(8,128)S(1)}, u32[]{:S(2)}, u32[]{:S(2)}) collective-permute-start(f32[10,32,256]{2,1,0:T(8,128)S(1)} %get-tuple-element.52), channel_id=1, source_target_pairs={{1,2},{2,1},{5,6},{6,5},{9,10},{10,9},{13,14},{14,13},{17,18},{18,... | collective-permute-start | bytes 983048 | tf_op jit(solution)/shard_map/ppermute | solution.py:349
  7.7 5.5 %collective-permute-start.1 = (f32[10,24,256]{2,1,0:T(8,128)S(1)}, f32[10,24,256]{2,1,0:T(8,128)S(1)}, u32[]{:S(2)}, u32[]{:S(2)}) collective-permute-start(f32[10,24,256]{2,1,0:T(8,128)S(1)} %get-tuple-element.48), channel_id=1, source_target_pairs={{4,8},{8,4},{12,16},{16,12},{20,24},{24,20},{5,9},{9,5},{13,17},{1... | collective-permute-start | bytes 737288 | tf_op jit(solution)/shard_map/ppermute | solution.py:339
  11.7 19.5 %copy-start.2 = (f32[64,24]{0,1:T(8,128)S(1)}, f32[64,24]{0,1:T(8,128)}, u32[]{:S(2)}) copy-start(f32[64,24]{0,1:T(8,128)} %param.13) | copy-start | bytes 18436
